TPU v7x, 32 devices: a whole 2x2x4 slice. The times are simulated.
32 devices in a mesh: dp: 8 (over z, x), dir: 4 (over y, core).
Axes of the slice: x: 2, y: 2, z: 4, core: 2. Of those that a mesh axis runs over, the one named last changes fastest.
Arguments:
- tokens: bfloat16 [16, 256, 1536], P('dp', 'dir'), may hold values from -6 to 6
- cond: bfloat16 [16, 1536], P('dp'), may hold values from -6 to 6
- counts: int32 [8], P('dp'), may hold values from 1 to 2, as said below
- valid: int32 [16, 256], P('dp'), may hold values from 0 to 1, as said below
- ada_weight: bfloat16 [1536, 4608], replicated, may hold values from -0.15625 to 0.15625
- ada_bias: bfloat16 [4608], replicated, may hold values from -3 to 3
- in_weight: bfloat16 [1536, 6144], P(None, 'dir'), may hold values from -0.15625 to 0.15625
- conv_weight: bfloat16 [6144, 4], P('dir'), may hold values from -3 to 3
- conv_bias: bfloat16 [6144], P('dir'), may hold values from -3 to 3
- xproj_weight: bfloat16 [6144, 128], P('dir'), may hold values from -0.109375 to 0.109375
- dtproj_weight: bfloat16 [96, 6144], P(None, 'dir'), may hold values from -0.625 to 0.625
- dt_bias: float32 [6144], P('dir'), may hold values from -6 to -2.5
- a_log: float32 [6144, 16], P('dir'), may hold values from 0 to 2.77
- skip_gain: float32 [6144], P('dir'), may hold values from 0.5 to 1.5
- out_weight: bfloat16 [3072, 1536], P('dir'), may hold values from -0.3125 to 0.3125
- cotangent: bfloat16 [16, 256, 1536], P('dp', 'dir'), may hold values from -6 to 6
Outputs:
- mixed: float32 [16, 256, 1536], P('dp', 'dir')
- tokens_grad: float32 [16, 256, 1536], P('dp', 'dir')
- cond_grad: float32 [16, 1536], P('dp')
- ada_weight_grad: float32 [1536, 4608], P('dp', 'dir')
- ada_bias_grad: float32 [4608], P('dp')
- in_weight_grad: float32 [1536, 6144], P('dp', 'dir')
- conv_weight_grad: float32 [6144, 4], P('dir')
- conv_bias_grad: float32 [6144], P('dir')
- xproj_weight_grad: float32 [6144, 128], P('dir')
- dtproj_weight_grad: float32 [96, 6144], P(None, 'dir')
- dt_bias_grad: float32 [6144], P('dir')
- a_log_grad: float32 [6144, 16], P('dir')
- skip_gain_grad: float32 [6144], P('dir')
- out_weight_grad: float32 [3072, 1536], P('dir', 'dp')
Inputs may be any that keep to these rules, and one draw needn't show every extreme that they name: `counts`: the live slots of an index of dp are its first ones, the rest are empty; some index has all 2 live. The valid rows of an item are its first ones, 128 or more of them; some item is valid in all 256 rows.
All inputs are finite; a program needn't handle non-finite values.
Results may differ from a plain program's by a relative error of at most 0.014.
The roundings to bfloat16 on the way count: a program that leaves them out, or rounds other values in their place, can miss the bound.
Values may be sent and summed in bfloat16 or wider, within the bound.
No kernel may reach another device: no remote copies, remote signals or barrier semaphores. Data moves between devices by JAX's collectives and lax.ppermute only.
A program may use at most 256 MiB of HBM per device.

v0:
```python
import functools

import jax
import jax.numpy as jnp
from jax import lax
from jax.experimental import pallas as pl
from jax.experimental.pallas import tpu as pltpu
from jax.sharding import PartitionSpec as P

EPSILON = 1e-06
LOG2E = 1.4426950408889634
CHUNK = 16
MARGIN = 8

bf16 = jnp.bfloat16
f32 = jnp.float32


def swap(block, axis, bit):
    count = lax.axis_size(axis)
    return lax.ppermute(block, axis, [(at, at ^ (1 << bit)) for at in range(count)])


def contract_rows(left, right):
    return lax.dot_general(
        left, right, (((0,), (0,)), ((), ())), preferred_element_type=f32
    )


def contract_cols(left, right):
    return lax.dot_general(
        left, right, (((1,), (1,)), ((), ())), preferred_element_type=f32
    )


def matmul(left, right):
    return jnp.dot(left, right, preferred_element_type=f32)


def ordered(bit, own, other, axis):
    return jnp.where(
        bit == 0,
        jnp.concatenate([own, other], axis),
        jnp.concatenate([other, own], axis),
    )


def halves(values, bit, axis):
    size = values.shape[axis] // 2
    keep = lax.dynamic_slice_in_dim(values, bit * size, size, axis)
    send = lax.dynamic_slice_in_dim(values, (1 - bit) * size, size, axis)
    return keep, send


class Scatter:
    def __init__(self, values, axis, order):
        self.axis, self.order = axis, list(order)
        bits = len(order)
        self.values = values.reshape((2,) * bits + (values.shape[0] >> bits,) + values.shape[1:])
        self.left = sorted(order, reverse=True)
        self.split()

    def split(self):
        if not self.order:
            return
        at = self.left.index(self.order[0])
        mine = (lax.axis_index(self.axis) >> self.order[0]) & 1
        self.keep = lax.dynamic_index_in_dim(self.values, mine, at, keepdims=False)
        send = lax.dynamic_index_in_dim(self.values, 1 - mine, at, keepdims=False)
        self.send = send.astype(bf16)

    def step(self, *earlier):
        bit = self.order.pop(0)
        self.left.remove(bit)
        arrived = after(swap(self.send, self.axis, bit), *earlier)
        self.values = self.keep.astype(f32) + arrived.astype(f32)
        self.split()


class SharedSum:
    def __init__(self, values, axis, order):
        self.axis = axis
        few = list(order[:2])
        self.plan = [("halve", bit) for bit in few] + [("add", bit) for bit in order[2:]]
        self.plan += [("join", bit) for bit in few[::-1]]
        self.start(*values)

    def start(self, keep, send):
        self.keep, self.send = keep, send

    def begin(self):
        kind, bit = self.plan[0] if self.plan else ("", 0)
        self.mine = (lax.axis_index(self.axis) >> bit) & 1
        if kind == "halve":
            self.keep, self.send = halves(self.values, self.mine, 0)
            self.send = self.send.astype(bf16)
        else:
            self.keep = self.send = self.values.astype(bf16)

    def step(self, *earlier):
        kind, bit = self.plan.pop(0)
        arrived = after(swap(self.send, self.axis, bit), *earlier)
        if kind == "join":
            self.values = ordered(self.mine, self.keep, arrived, 0)
        else:
            self.values = self.keep.astype(f32) + arrived.astype(f32)
        self.begin()

    def last(self, *earlier):
        _, bit = self.plan.pop(0)
        return self.keep, after(swap(self.send, self.axis, bit), *earlier)


def after(values, *earlier):
    return lax.optimization_barrier((values, earlier))[0] if earlier else values


def gather_bit(values, axis, bit, have, *earlier):
    at = len([other for other in have if other > bit])
    mine = (lax.axis_index(axis) >> bit) & 1
    arrived = after(swap(values, axis, bit), *earlier)
    have.append(bit)
    return jnp.where(
        mine == 0, jnp.stack([values, arrived], at), jnp.stack([arrived, values], at)
    )


def bit_orders(axis):
    bits = lax.axis_size(axis).bit_length() - 1
    first = list(range(bits))
    second = list(range(bits))
    if bits > 1:
        second[0], second[1] = 1, 0
    return first, second


def shifted(padded, length, by, flip):
    return jnp.where(
        flip == 1,
        padded[MARGIN + by : MARGIN + by + length, :],
        padded[MARGIN - by : MARGIN - by + length, :],
    )


def kernel_params(megabytes):
    return pltpu.CompilerParams(vmem_limit_bytes=megabytes * 1024 * 1024)


LIGHT = pl.CostEstimate(flops=1000, bytes_accessed=1000, transcendentals=0)


def whole(*shape):
    return pl.BlockSpec(shape, lambda *at: (0,) * len(shape))


def scalars():
    return pl.BlockSpec(memory_space=pltpu.SMEM)


def shaped(shape, kind):
    return jax.ShapeDtypeStruct(shape, kind)


def outer(shape, kind):
    return pltpu.HBM(shape, kind)


def held(values):
    return pltpu.with_memory_space_constraint(values, pltpu.HBM)


def split_columns(values_ref, side_ref, chunk, keep_ref, give_ref):
    for side in range(2):

        @pl.when(side_ref[0] == side)
        def _():
            for at, start in enumerate(range(0, values_ref.shape[1], 2 * chunk)):
                to = slice(at * chunk, (at + 1) * chunk)
                first = values_ref[:, start : start + chunk]
                second = values_ref[:, start + chunk : start + 2 * chunk]
                keep_ref[:, to] = second if side else first
                give_ref[:, to] = first if side else second


def norm_kernel(
    chunk, me_ref, side_ref, own_ref, over_ref, beside_ref, far_ref, mask_ref, mod_ref, weight_ref,
    keep_ref, give_ref, proj_ref, normed_s
):
    slots, rows, _ = own_ref.shape
    length = mask_ref.shape[1]

    @pl.when(pl.program_id(0) == 0)
    def _():
        for slot in range(slots):
            shift = mod_ref[slot, 0:1, :]
            scale = mod_ref[slot, 1:2, :]
            for code, block in ((0, own_ref), (2, over_ref), (1, beside_ref), (3, far_ref)):
                start = pl.multiple_of((me_ref[0] ^ code) * rows, rows)
                raw = block[slot].astype(f32)
                centred = raw - jnp.mean(raw, axis=1, keepdims=True)
                spread = jnp.mean(centred * centred, axis=1, keepdims=True)
                hat = centred * lax.rsqrt(spread + EPSILON)
                mask = mask_ref[slot, pl.ds(start, rows), :]
                normed_s[pl.ds(slot * length + start, rows), :] = (
                    mask * (hat * (1.0 + scale) + shift)
                ).astype(bf16)
        split_columns(normed_s, side_ref, chunk, keep_ref, give_ref)

    proj_ref[...] = matmul(normed_s[...], weight_ref[...]).astype(bf16)


def norm_call(me, side, blocks, mask, mods, weight, width, chunk):
    slots, rows, model = blocks[0].shape
    count = slots * mask.shape[1]
    channels = weight.shape[1]
    return pl.pallas_call(
        functools.partial(norm_kernel, chunk),
        grid=(channels // width,),
        in_specs=[scalars(), scalars()]
        + [whole(slots, rows, model)] * 4
        + [whole(*mask.shape), whole(slots, 3, model), pl.BlockSpec((model, width), lambda j: (0, j))],
        out_specs=[
            whole(count, model // 2),
            whole(count, model // 2),
            pl.BlockSpec((count, width), lambda j: (0, j)),
        ],
        out_shape=[
            shaped((count, model // 2), bf16),
            shaped((count, model // 2), bf16),
            shaped((count, channels), bf16),
        ],
        scratch_shapes=[pltpu.VMEM((count, model), bf16)],
        compiler_params=kernel_params(20),
        cost_estimate=LIGHT,
        name="norm_project",
    )(me, side, *blocks, mask, mods, held(weight))


def gate_kernel(
    chunk, me_ref, side_ref, own_ref, over_ref, beside_ref, far_ref, mask_ref, mod_ref, mine_ref,
    theirs_ref, keep_ref, give_ref, out_ref, grad_s
):
    slots, rows, _ = own_ref.shape
    length = mask_ref.shape[1]
    step = pl.program_id(0)

    @pl.when(step == 0)
    def _():
        for slot in range(slots):
            gate = mod_ref[slot, 2:3, :]
            for code, block in ((0, own_ref), (2, over_ref), (1, beside_ref), (3, far_ref)):
                start = pl.multiple_of((me_ref[0] ^ code) * rows, rows)
                mask = mask_ref[slot, pl.ds(start, rows), :]
                grad_s[pl.ds(slot * length + start, rows), :] = (
                    mask * block[slot].astype(f32) * gate
                ).astype(bf16)
        split_columns(grad_s, side_ref, chunk, keep_ref, give_ref)

    @pl.when(step < pl.num_programs(0) // 2)
    def _():
        out_ref[...] = contract_cols(grad_s[...], mine_ref[...]).astype(bf16)

    @pl.when(step >= pl.num_programs(0) // 2)
    def _():
        out_ref[...] = contract_cols(grad_s[...], theirs_ref[...]).astype(bf16)


def gate_call(me, side, blocks, mask, mods, mine, theirs, chunk):
    slots, rows, model = blocks[0].shape
    count = slots * mask.shape[1]
    quarter = mine.shape[0]
    parts = 2
    width = quarter // parts

    def out_at(j, me_ref, side_ref):
        return (0, ((me_ref[0] & 1) ^ (j // parts)) * parts + j % parts)

    fixed = lambda *shape: pl.BlockSpec(shape, lambda j, *refs: (0,) * len(shape))
    return pl.pallas_call(
        functools.partial(gate_kernel, chunk),
        grid_spec=pltpu.PrefetchScalarGridSpec(
            num_scalar_prefetch=2,
            grid=(2 * parts,),
            in_specs=[fixed(slots, rows, model)] * 4
            + [
                fixed(*mask.shape),
                fixed(slots, 3, model),
                pl.BlockSpec((width, model), lambda j, *refs: (jnp.minimum(j, parts - 1), 0)),
                pl.BlockSpec((width, model), lambda j, *refs: (jnp.maximum(j - parts, 0), 0)),
            ],
            out_specs=[
                fixed(count, model // 2),
                fixed(count, model // 2),
                pl.BlockSpec((count, width), out_at),
            ],
            scratch_shapes=[pltpu.VMEM((count, model), bf16)],
        ),
        out_shape=[
            shaped((count, model // 2), bf16),
            shaped((count, model // 2), bf16),
            outer((count, 2 * quarter), bf16),
        ],
        compiler_params=kernel_params(20),
        cost_estimate=LIGHT,
        name="gate_project",
    )(me, side, *blocks, mask, mods, held(mine), held(theirs))


def pair_kernel(first_ref, second_ref, third_ref, fourth_ref, left_ref, right_ref):
    left_ref[...] = (first_ref[...].astype(f32) + second_ref[...].astype(f32)).astype(bf16)
    right_ref[...] = (third_ref[...].astype(f32) + fourth_ref[...].astype(f32)).astype(bf16)


def pair_call(first, second, third, fourth, blocks):
    rows, cols = first.shape
    block = pl.BlockSpec((rows // blocks, cols), lambda i: (i, 0))
    return pl.pallas_call(
        pair_kernel,
        grid=(blocks,),
        in_specs=[block] * 4,
        out_specs=[block] * 2,
        out_shape=[shaped((rows, cols), bf16)] * 2,
        compiler_params=kernel_params(10),
        cost_estimate=LIGHT,
        name="pair_sums",
    )(held(first), held(second), held(third), held(fourth))


def join_kernel(*refs):
    out_ref = refs[-1]
    rows = refs[0].shape[0]
    for at in range(len(refs) // 2):
        total = refs[2 * at][...].astype(f32) + refs[2 * at + 1][...].astype(f32)
        out_ref[at * rows : (at + 1) * rows, :] = total.astype(bf16)


def join_call(pairs):
    rows, cols = pairs[0][0].shape
    return pl.pallas_call(
        join_kernel,
        out_shape=shaped((len(pairs) * rows, cols), bf16),
        compiler_params=kernel_params(10),
        cost_estimate=LIGHT,
        name="join_sums",
    )(*[part for pair in pairs for part in pair])


def pack_kernel(side_ref, conv_ref, scan_ref, keep_ref, send_ref, total):
    count = conv_ref.shape[0]
    rows = keep_ref.shape[0]
    total[0:count, :] = conv_ref[...]
    total[count:, :] = scan_ref[...]
    side = side_ref[0]
    keep_ref[...] = total[pl.ds(pl.multiple_of(side * rows, rows), rows), :]
    send_ref[...] = total[pl.ds(pl.multiple_of((1 - side) * rows, rows), rows), :].astype(bf16)


def pack_call(side, conv, scan):
    cols = conv.shape[1]
    rows = (conv.shape[0] + scan.shape[0]) // 2
    return pl.pallas_call(
        pack_kernel,
        in_specs=[scalars(), whole(*conv.shape), whole(*scan.shape)],
        out_specs=[whole(rows, cols)] * 2,
        grid=(1,),
        out_shape=[shaped((rows, cols), f32), shaped((rows, cols), bf16)],
        scratch_shapes=[pltpu.VMEM((2 * rows, cols), f32)],
        compiler_params=kernel_params(14),
        cost_estimate=LIGHT,
        name="pack_sums",
    )(side, conv, scan)


def unpack_kernel(spots, side_ref, keep_ref, there_ref, xproj_ref, taps_ref, dtproj_ref, rates_ref, vec_ref, total):
    rows = keep_ref.shape[0]
    cols, tap_count, base, rank, states = spots
    side = side_ref[0]
    total[pl.ds(pl.multiple_of(side * rows, rows), rows), :] = keep_ref[...].astype(f32)
    total[pl.ds(pl.multiple_of((1 - side) * rows, rows), rows), :] = there_ref[...].astype(f32)
    dtproj_ref[...] = total[base : base + rank, :]
    vec_ref[...] = jnp.zeros_like(vec_ref)
    vec_ref[0:1, :] = total[cols + tap_count : cols + tap_count + 1, :]
    vec_ref[1:3, :] = total[base + rank + states : base + rank + states + 2, :]
    for at in range(0, total.shape[1], 128):
        here = slice(at, at + 128)
        xproj_ref[here, :] = jnp.transpose(total[0:cols, here])
        turned = jnp.transpose(total[cols : cols + 128, here])
        taps_ref[here, :] = turned[:, 0:tap_count]
        first = base + rank - cols
        rates_ref[here, :] = turned[:, first : first + states]


def unpack_call(side, keep, there, cols, tap_count, base, rank, states):
    rows, channels = keep.shape
    shapes = [(channels, cols), (channels, tap_count), (rank, channels), (channels, states), (8, channels)]
    return pl.pallas_call(
        functools.partial(unpack_kernel, (cols, tap_count, base, rank, states)),
        grid=(1,),
        in_specs=[scalars(), whole(rows, channels), whole(rows, channels)],
        out_specs=[whole(*shape) for shape in shapes],
        out_shape=[shaped(shape, f32) for shape in shapes],
        scratch_shapes=[pltpu.VMEM((2 * rows, channels), f32)],
        compiler_params=kernel_params(16),
        cost_estimate=LIGHT,
        name="unpack_sums",
    )(side, keep, there)


def fold_kernel(slots, rows, me_ref, keep_ref, there_ref, mine_ref, sent_ref):
    chip = me_ref[0] >> 1
    for slot in range(slots):
        for which, out_ref in ((chip, mine_ref), (1 - chip, sent_ref)):
            here = pl.ds(pl.multiple_of((2 * slot + which) * rows, rows), rows)
            out_ref[slot] = (keep_ref[here, :] + there_ref[here, :].astype(f32)).astype(out_ref.dtype)


def fold_call(me, keep, there, slots):
    count, model = keep.shape
    rows = count // slots // 2
    return pl.pallas_call(
        functools.partial(fold_kernel, slots, rows),
        grid=(1,),
        in_specs=[scalars(), whole(count, model), whole(count, model)],
        out_specs=[whole(slots, rows, model)] * 2,
        out_shape=[shaped((slots, rows, model), f32), shaped((slots, rows, model), bf16)],
        compiler_params=kernel_params(14),
        cost_estimate=LIGHT,
        name="fold_rows",
    )(me, keep, there)


def rows_kernel(
    tokens_ref, cot_ref, mask_ref, mod_ref, branch_ref, branch_far_ref, norm_ref, norm_far_ref,
    mixed_ref, grad_ref, mod_grad_ref
):
    raw = tokens_ref[...].astype(f32)
    mask = mask_ref[...]
    gate = mod_ref[2:3, :]
    branch = branch_ref[...] + branch_far_ref[...].astype(f32)
    mixed_ref[...] = mask * (raw + gate * branch)
    res_grad = mask * cot_ref[...].astype(f32)
    centred = raw - jnp.mean(raw, axis=1, keepdims=True)
    spread = jnp.mean(centred * centred, axis=1, keepdims=True)
    inverse = lax.rsqrt(spread + EPSILON)
    hat = centred * inverse
    normed_grad = mask * (norm_ref[...] + norm_far_ref[...].astype(f32))
    q = normed_grad * (1.0 + mod_ref[1:2, :])
    grad_ref[...] = res_grad + inverse * (
        q - jnp.mean(q, axis=1, keepdims=True) - hat * jnp.mean(q * hat, axis=1, keepdims=True)
    )
    mod_grad_ref[0:1, :] = jnp.sum(normed_grad, axis=0, keepdims=True)
    mod_grad_ref[1:2, :] = jnp.sum(normed_grad * hat, axis=0, keepdims=True)
    mod_grad_ref[2:3, :] = jnp.sum(res_grad * branch, axis=0, keepdims=True)


def rows_call(tokens, cot, mask, mods, branch, branch_far, norm, norm_far):
    slots, rows, model = tokens.shape
    row = pl.BlockSpec((None, rows, model), lambda i: (i, 0, 0))
    mod = pl.BlockSpec((None, 3, model), lambda i: (i, 0, 0))
    return pl.pallas_call(
        rows_kernel,
        grid=(slots,),
        in_specs=[row, row, pl.BlockSpec((None, rows, 1), lambda i: (i, 0, 0)), mod, row, row, row, row],
        out_specs=[row, row, mod],
        out_shape=[
            shaped((slots, rows, model), f32),
            shaped((slots, rows, model), f32),
            shaped((slots, 3, model), f32),
        ],
        compiler_params=kernel_params(14),
        cost_estimate=LIGHT,
        name="owned_rows",
    )(tokens, cot, mask, mods, branch, branch_far, norm, norm_far)


def pick_rows(values_ref, parity, chips, rows):
    blocks = []
    for at in range(values_ref.shape[0] // rows // 2):
        start = pl.multiple_of((2 * at + parity) * rows, rows)
        blocks.append(values_ref[pl.ds(start, rows), :])
    return jnp.concatenate(blocks, 0)


def branch_kernel(rows, flip_ref, values_ref, weight_ref, keep_ref, send_ref):
    core = flip_ref[0]
    keep_ref[...] = matmul(pick_rows(values_ref, core, 2, rows), weight_ref[...])
    send_ref[...] = matmul(pick_rows(values_ref, 1 - core, 2, rows), weight_ref[...]).astype(bf16)


def branch_call(flip, values, weight, rows, width):
    count, depth = values.shape
    model = weight.shape[1]
    out = [shaped((count // 2, model), f32), shaped((count // 2, model), bf16)]
    return pl.pallas_call(
        functools.partial(branch_kernel, rows),
        grid=(model // width,),
        in_specs=[
            pl.BlockSpec(memory_space=pltpu.SMEM),
            pl.BlockSpec((count, depth), lambda j: (0, 0)),
            pl.BlockSpec((depth, width), lambda j: (0, j)),
        ],
        out_specs=[pl.BlockSpec((count // 2, width), lambda j: (0, j))] * 2,
        out_shape=out,
        compiler_params=kernel_params(10),
        cost_estimate=pl.CostEstimate(flops=1000, bytes_accessed=1000, transcendentals=0),
        name="branch_rows",
    )(flip, values, weight)


def proj_back_kernel(rows, flip_ref, x_ref, z_ref, weight_ref, there_ref, keep_ref, send_ref, x_s, z_s, mine_s):
    core = flip_ref[0]
    half = there_ref.shape[1]

    @pl.when(core == 0)
    def _():
        x_s[...] = x_ref[...]
        z_s[...] = z_ref[...]
        mine_s[...] = weight_ref[:, :half]

    @pl.when(core == 1)
    def _():
        x_s[...] = z_ref[...]
        z_s[...] = x_ref[...]
        mine_s[...] = weight_ref[:, half:]

    for parity, out_ref in ((core, keep_ref), (1 - core, send_ref)):
        total = contract_cols(pick_rows(x_s, parity, 2, rows), mine_s[...]) + contract_cols(
            pick_rows(z_s, parity, 2, rows), there_ref[...]
        )
        out_ref[...] = total.astype(out_ref.dtype)


def proj_back_call(flip, x, z, weight, there, rows, width):
    count, depth = x.shape
    model = there.shape[0]
    out = [shaped((count // 2, model), f32), shaped((count // 2, model), bf16)]
    return pl.pallas_call(
        functools.partial(proj_back_kernel, rows),
        grid=(model // width,),
        in_specs=[
            scalars(),
            whole(count, depth),
            whole(count, depth),
            pl.BlockSpec((width, 2 * depth), lambda j: (j, 0)),
            pl.BlockSpec((width, depth), lambda j: (j, 0)),
        ],
        out_specs=[pl.BlockSpec((count // 2, width), lambda j: (0, j))] * 2,
        out_shape=out,
        scratch_shapes=[pltpu.VMEM((count, depth), bf16)] * 2 + [pltpu.VMEM((width, depth), bf16)],
        compiler_params=kernel_params(18),
        cost_estimate=LIGHT,
        name="proj_back",
    )(flip, x, z, held(weight), held(there))


def cond_kernel(mod_ref, weight_ref, cond_ref, out_ref):
    value = cond_ref[...].astype(f32)
    sig = jax.nn.sigmoid(value)
    out_ref[...] = contract_cols(mod_ref[...], weight_ref[...]) * sig * (1.0 + value * (1.0 - sig))


def cond_call(mods, weight, cond):
    slots, columns = mods.shape
    model = weight.shape[0]
    width = 256 if model % 256 == 0 else 128
    return pl.pallas_call(
        cond_kernel,
        grid=(model // width,),
        in_specs=[
            whole(slots, columns),
            pl.BlockSpec((width, columns), lambda j: (j, 0)),
            pl.BlockSpec((slots, width), lambda j: (0, j)),
        ],
        out_specs=pl.BlockSpec((slots, width), lambda j: (0, j)),
        out_shape=shaped((slots, model), f32),
        compiler_params=kernel_params(14),
        cost_estimate=LIGHT,
        name="cond_rows",
    )(mods, held(weight), cond)


def conv_kernel(
    flip_ref, own_ref, other_ref, mask_ref, taps_ref, xproj_ref, x_ref, z_ref, u_ref, dbl_ref, pad
):
    step = pl.program_id(1)
    length, width = own_ref.shape
    flip = flip_ref[0]

    @pl.when(flip == 0)
    def _():
        x_ref[...] = own_ref[...]
        z_ref[...] = other_ref[...]

    @pl.when(flip == 1)
    def _():
        x_ref[...] = other_ref[...]
        z_ref[...] = own_ref[...]

    pad[0:MARGIN, :] = jnp.zeros((MARGIN, width), f32)
    pad[MARGIN + length :, :] = jnp.zeros((MARGIN, width), f32)
    pad[MARGIN : MARGIN + length, :] = x_ref[...].astype(f32)
    taps = taps_ref.shape[0] - 1
    conv = taps_ref[taps : taps + 1, :] + pad[MARGIN : MARGIN + length, :] * taps_ref[taps - 1 : taps, :]
    for by in range(1, taps):
        conv = conv + shifted(pad, length, by, flip) * taps_ref[taps - 1 - by : taps - by, :]
    u = (mask_ref[...] * (conv * jax.nn.sigmoid(conv))).astype(bf16)
    u_ref[...] = u
    part = matmul(u, xproj_ref[...])

    @pl.when(step == 0)
    def _():
        dbl_ref[...] = part

    @pl.when(step > 0)
    def _():
        dbl_ref[...] += part


def conv_back_kernel(
    flip_ref, x_ref, u_ref, mask_ref, taps_ref, xproj_ref, us_ref, dg_ref, prev_ref, keep_ref, send_ref,
    packed_ref, pad
):
    length, width = x_ref.shape
    flip = flip_ref[0]
    pad[0:MARGIN, :] = jnp.zeros((MARGIN, width), f32)
    pad[MARGIN + length :, :] = jnp.zeros((MARGIN, width), f32)
    pad[MARGIN : MARGIN + length, :] = x_ref[...].astype(f32)
    taps = taps_ref.shape[0] - 1
    conv = taps_ref[taps : taps + 1, :] + pad[MARGIN : MARGIN + length, :] * taps_ref[taps - 1 : taps, :]
    for by in range(1, taps):
        conv = conv + shifted(pad, length, by, flip) * taps_ref[taps - 1 - by : taps - by, :]
    sig = jax.nn.sigmoid(conv)
    dg = dg_ref[...]
    u_grad = us_ref[...] + contract_cols(dg, xproj_ref[...])
    conv_grad = u_grad * mask_ref[...] * (sig * (1.0 + conv * (1.0 - sig)))
    cols = dg.shape[1]
    packed_ref[0:cols, :] = prev_ref[0:cols, :] + matmul(jnp.transpose(dg.astype(f32)).astype(bf16), u_ref[...])
    for by in range(taps):
        moved = pad[MARGIN : MARGIN + length, :] if by == 0 else shifted(pad, length, by, flip)
        row = cols + taps - 1 - by
        packed_ref[row : row + 1, :] = prev_ref[row : row + 1, :] + jnp.sum(conv_grad * moved, axis=0, keepdims=True)
    row = cols + taps
    packed_ref[row : row + 1, :] = prev_ref[row : row + 1, :] + jnp.sum(conv_grad, axis=0, keepdims=True)
    rest = packed_ref.shape[0] - cols - taps - 1
    packed_ref[cols + taps + 1 :, :] = jnp.zeros((rest, width), f32)
    pad[MARGIN : MARGIN + length, :] = conv_grad
    grad = conv_grad * taps_ref[taps - 1 : taps, :]
    for by in range(1, taps):
        grad = grad + shifted(pad, length, by, 1 - flip) * taps_ref[taps - 1 - by : taps - by, :]
    grad = grad.astype(bf16)

    @pl.when(pl.program_id(0) == flip)
    def _():
        keep_ref[...] = grad

    @pl.when(pl.program_id(0) != flip)
    def _():
        send_ref[...] = grad


def conv_call(flip, own, other, mask, taps, xproj, width):
    slots, length = mask.shape[:2]
    channels = own.shape[1]
    cols = xproj.shape[1]
    block = pl.BlockSpec((length, width), lambda i, j: (i, j))
    return pl.pallas_call(
        conv_kernel,
        grid=(slots, channels // width),
        in_specs=[
            scalars(),
            block,
            block,
            pl.BlockSpec((None, length, 1), lambda i, j: (i, 0, 0)),
            pl.BlockSpec((taps.shape[0], width), lambda i, j: (0, j)),
            pl.BlockSpec((width, cols), lambda i, j: (j, 0)),
        ],
        out_specs=[block, block, block, pl.BlockSpec((length, cols), lambda i, j: (i, 0))],
        out_shape=[outer((slots * length, channels), bf16)] * 3
        + [shaped((slots * length, cols), f32)],
        scratch_shapes=[pltpu.VMEM((length + 2 * MARGIN, width), f32)],
        compiler_params=kernel_params(12),
        cost_estimate=LIGHT,
        name="conv_forward",
    )(flip, own, other, mask, taps, xproj)


def conv_back_call(flip, slot, x, u, mask, taps, xproj, us, dg, prev):
    length = mask.shape[1]
    channels = x.shape[1]
    cols = xproj.shape[1]
    width = channels // 2
    rows = prev.shape[0]
    item = pl.BlockSpec((length, width), lambda j: (slot, j))
    return pl.pallas_call(
        conv_back_kernel,
        grid=(2,),
        in_specs=[
            scalars(),
            item,
            item,
            pl.BlockSpec((None, length, 1), lambda j: (slot, 0, 0)),
            pl.BlockSpec((taps.shape[0], width), lambda j: (0, j)),
            pl.BlockSpec((width, cols), lambda j: (j, 0)),
            pl.BlockSpec((length, width), lambda j: (0, j)),
            whole(length, cols),
            pl.BlockSpec((rows, width), lambda j: (0, j)),
        ],
        out_specs=[
            whole(length, width),
            whole(length, width),
            pl.BlockSpec((rows, width), lambda j: (0, j)),
        ],
        out_shape=[
            shaped((length, width), bf16),
            shaped((length, width), bf16),
            shaped((rows, channels), f32),
        ],
        scratch_shapes=[pltpu.VMEM((length + 2 * MARGIN, width), f32)],
        compiler_params=kernel_params(16),
        cost_estimate=LIGHT,
        name="conv_backward",
    )(flip, held(x), held(u), mask, taps, xproj, held(us), dg, prev)


def spread(dbl_ref, first, b_wide, c_wide, rows_s, states):
    length, cols = dbl_ref.shape
    rest = dbl_ref[...]
    row = lax.broadcasted_iota(jnp.int32, (cols, cols), 0)
    col = lax.broadcasted_iota(jnp.int32, (cols, cols), 1)
    rows = jnp.zeros((length, cols), f32)
    for part in range(3):
        piece = rest.astype(bf16)
        rest = rest - piece.astype(f32)
        pick = ((row == first + col % (2*states)) & (col // (2*states) == part))
        rows = rows + matmul(piece, jnp.where(pick, 1.0, 0.0).astype(bf16))
    rows_s[...] = rows
    which = lax.broadcasted_iota(jnp.int32, (states, cols), 0)
    lane = lax.broadcasted_iota(jnp.int32, (states, cols), 1)
    mine = jnp.where(lane % states == which, 1.0, 0.0)
    row = lax.broadcasted_iota(jnp.int32, (cols, 2*cols), 0)
    col = lax.broadcasted_iota(jnp.int32, (cols, 2*cols), 1)
    wide = jnp.where((row % (2*states)) // states == col // cols, 1.0, 0.0).astype(bf16)
    def some(at, _):
        left = [(mine*jnp.broadcast_to(rows_s[pl.ds(at*CHUNK+t, 1), :], (states, cols))).astype(bf16) for t in range(CHUNK)]
        got = matmul(jnp.concatenate(left, 0), wide)
        here = pl.ds(pl.multiple_of(at*CHUNK*states, CHUNK*states), CHUNK*states)
        b_wide[here, :] = got[:, :cols]
        c_wide[here, :] = got[:, cols:]
        return 0
    lax.fori_loop(0, length//CHUNK, some, 0, unroll=4)

def tiles_of(values):
    return [values[:, at:at+128] for at in range(0, values.shape[1], 128)]

def fold(values, tmp, tt, states):
    for at, tile in enumerate(tiles_of(values)):
        total = tile[:8]
        for part in range(1, states//8):
            total = total + tile[part*8:(part+1)*8]
        tmp[at, pl.ds(tt//8*64 + tt%8, 8, stride=8), :] = total

def add_tiles(values):
    parts = tiles_of(values)
    total = parts[0]
    for part in parts[1:]:
        total = total + part
    return total

def unfold(tmp, out, base):
    for at in range(out.shape[1]//128):
        for part in range(CHUNK//8):
            acc = tmp[at, part*64:part*64+8, :]
            for row in range(1, 8):
                acc = acc + tmp[at, part*64+row*8:part*64+row*8+8, :]
            out[pl.ds(pl.multiple_of(base+part*8, 8), 8), at*128:(at+1)*128] = acc

def collect(acc, tmp, out, length, states):
    which = lax.broadcasted_iota(jnp.int32, (states, 128), 0)
    lane = lax.broadcasted_iota(jnp.int32, (states, 128), 1)
    mine = which == lane
    def some(at, _):
        base = pl.multiple_of(at*CHUNK, CHUNK)
        for tt in range(CHUNK):
            sums = jnp.sum(acc[pl.ds((base+tt)*states, states), :], axis=1, keepdims=True)
            fold(jnp.where(mine, sums, 0.0), tmp, tt, states)
        unfold(tmp, out, base)
        return 0
    lax.fori_loop(0, length//CHUNK, some, 0, unroll=4)

def fwd_kernel(states, flip_ref, dbl_ref, dtp_ref, vec_ref, rate2_ref, u_ref, z_ref, gg_ref,
               gate_keep, gate_send, z_keep, z_send, delta_ref, yg_ref, prior_ref, cout_ref,
               b_wide, c_wide, drive_s, y_s, y_tmp, c_acc, rows_s):
    step = pl.program_id(1)
    length, width = u_ref.shape
    rank = dtp_ref.shape[0]
    group = CHUNK*states
    chunks = length//CHUNK
    flip = flip_ref[0]
    @pl.when(step == 0)
    def _():
        spread(dbl_ref, rank, b_wide, c_wide, rows_s, states)
        c_acc[...] = jnp.zeros_like(c_acc)
    low = dbl_ref[:, :rank].astype(bf16)
    pre = matmul(low, dtp_ref[...]) + vec_ref[0:1, :]
    delta = jnp.maximum(pre, 0.0) + jnp.log1p(jnp.exp(-jnp.abs(pre)))
    delta_ref[...] = delta
    drive_s[...] = delta * u_ref[...].astype(f32)
    z = z_ref[...].astype(f32)
    yg_ref[...] = gg_ref[...].astype(f32) * (z * (0.5 + 0.5*jnp.tanh(0.5*z)))
    def run(flipped):
        def ahead(chunk, state):
            place = chunks-1-chunk if flipped else chunk
            base = pl.multiple_of(place*CHUNK, CHUNK)
            wide = pl.multiple_of(place*group, group)
            for at in range(CHUNK):
                tt = CHUNK-1-at if flipped else at
                t = base + tt
                here = pl.ds(wide + tt*states, states)
                d = jnp.broadcast_to(delta_ref[pl.ds(t,1),:], (states,width))
                x = jnp.broadcast_to(drive_s[pl.ds(t,1),:], (states,width))
                g = jnp.broadcast_to(yg_ref[pl.ds(t,1),:], (states,width))
                b = jnp.concatenate([b_wide[here,:]]*(width//128), axis=1)
                c = jnp.concatenate([c_wide[here,:]]*(width//128), axis=1)
                prior = jnp.exp2(d*rate2_ref[...])*state
                state = prior + x*b
                prior_ref[here,:] = prior.astype(bf16)
                fold(state*c, y_tmp, tt, states)
                c_acc[here,:] += add_tiles(state*g)
            unfold(y_tmp, y_s, base)
            return state
        lax.fori_loop(0, chunks, ahead, jnp.zeros((states,width), f32))
    pl.when(flip == 0)(lambda: run(False))
    pl.when(flip == 1)(lambda: run(True))
    u = u_ref[...].astype(f32)
    z = z_ref[...].astype(f32)
    sig = (0.5 + 0.5*jnp.tanh(0.5*z))
    y = y_s[...] + vec_ref[1:2,:]*u
    gated = (y*(z*sig)).astype(bf16)
    zg = (gg_ref[...].astype(f32)*y*(sig*(1.0+z*(1.0-sig)))).astype(bf16)
    half = gate_keep.shape[1]
    for at in range(2*half//width):
        for core in range(2):
            def put(at=at, core=core):
                for side in range(2):
                    low, high = max(at*width, side*half), min((at+1)*width, (side+1)*half)
                    if low < high:
                        to = slice(low-side*half, high-side*half)
                        of = slice(low-at*width, high-at*width)
                        (gate_keep if side == core else gate_send)[:, to] = gated[:, of]
                        (z_keep if side == core else z_send)[:, to] = zg[:, of]
            pl.when((step == at) & (flip == core))(put)
    @pl.when(step == pl.num_programs(1)-1)
    def _():
        collect(c_acc, y_tmp, rows_s, length, states)
        cout_ref[...] = rows_s[:, :states]

def bwd_kernel(states, flip_ref, dbl_ref, dtp_ref, vec_ref, rate2_ref, u_ref, delta_ref, yg_ref, prior_ref, cout_ref, prev_ref,
               us_ref, part_ref, packed_ref,
               b_wide, c_wide, drive_s, r_s, w_s, low_t, rank_s, r_tmp, w_tmp, b_acc, rows_s):
    step = pl.program_id(0)
    length, width = u_ref.shape
    rank = dtp_ref.shape[0]
    group = CHUNK*states
    chunks = length//CHUNK
    flip = flip_ref[0]
    @pl.when(step == 0)
    def _():
        low_t[...] = jnp.transpose(dbl_ref[...])[:rank,:].astype(bf16)
        spread(dbl_ref, rank, b_wide, c_wide, rows_s, states)
        b_acc[...] = jnp.zeros_like(b_acc)
        rank_s[...] = jnp.zeros_like(rank_s)
    u = u_ref[...].astype(f32)
    drive_s[...] = delta_ref[...]*u
    def run(flipped):
        def back(chunk, carry):
            carried, total = carry
            place = chunk if flipped else chunks-1-chunk
            base = pl.multiple_of(place*CHUNK, CHUNK)
            wide = pl.multiple_of(place*group, group)
            for at in range(CHUNK):
                tt = at if flipped else CHUNK-1-at
                t = base + tt
                here = pl.ds(wide + tt*states, states)
                d = jnp.broadcast_to(delta_ref[pl.ds(t,1),:], (states,width))
                x = jnp.broadcast_to(yg_ref[pl.ds(t,1),:], (states,width))
                e = jnp.broadcast_to(drive_s[pl.ds(t,1),:], (states,width))
                b = jnp.concatenate([b_wide[here,:]]*(width//128), axis=1)
                c = jnp.concatenate([c_wide[here,:]]*(width//128), axis=1)
                power = d*rate2_ref[...]
                adj = carried + x*c
                moved = (adj*prior_ref[here,:].astype(f32))*power
                total = total + moved
                fold(moved, w_tmp, tt, states)
                fold(adj*b, r_tmp, tt, states)
                b_acc[here,:] += add_tiles(adj*e)
                carried = jnp.exp2(power)*adj
            unfold(w_tmp, w_s, base)
            unfold(r_tmp, r_s, base)
            return carried, total
        zero = jnp.zeros((states,width), f32)
        _, total = lax.fori_loop(0, chunks, back, (zero, zero))
        packed_ref[rank:rank+states,:] = prev_ref[rank:rank+states,:] + total*(1.0/LOG2E)
    pl.when(flip == 0)(lambda: run(False))
    pl.when(flip == 1)(lambda: run(True))
    yg = yg_ref[...]
    r = r_s[...]
    delta = delta_ref[...]
    us_ref[...] = delta*r + vec_ref[1:2,:]*yg
    low = dbl_ref[:, :rank].astype(bf16)
    pre = matmul(low, dtp_ref[...]) + vec_ref[0:1,:]
    sig = jnp.exp(pre-delta)
    ratio = jnp.where(delta > 1e-30, sig/jnp.maximum(delta, 1e-30), 1.0)
    pre_grad = w_s[...]*(1.0/LOG2E)*ratio + u*r*sig
    pre_low = pre_grad.astype(bf16)
    rank_s[...] += contract_cols(pre_low, dtp_ref[...])
    packed_ref[0:rank,:] = prev_ref[0:rank,:] + matmul(low_t[...], pre_low)
    packed_ref[rank+states:rank+states+1,:] = prev_ref[rank+states:rank+states+1,:] + jnp.sum(pre_grad, axis=0, keepdims=True)
    packed_ref[rank+states+1:rank+states+2,:] = prev_ref[rank+states+1:rank+states+2,:] + jnp.sum(yg*u, axis=0, keepdims=True)
    rest = packed_ref.shape[0]-rank-states-2
    packed_ref[rank+states+2:,:] = jnp.zeros((rest,width), f32)
    @pl.when(step == pl.num_programs(0)-1)
    def _():
        collect(b_acc, r_tmp, rows_s, length, states)
        part_ref[...] = jnp.concatenate([rank_s[...], rows_s[:, :states], cout_ref[...]], axis=1)


def forward_call(flip, dbl, dtproj, vec, rates2, u, z, gg, slots, width):
    count, channels = u.shape
    length = count // slots
    half = channels // 2
    states, rank, cols = rates2.shape[0], dtproj.shape[0], dbl.shape[1]
    weight = lambda rows: pl.BlockSpec((rows, width), lambda i, j: (0, j))
    block = lambda rows: pl.BlockSpec((rows, width), lambda i, j: (i, j))
    item = lambda wide: pl.BlockSpec((length, wide), lambda i, j: (i, 0))
    return pl.pallas_call(
        functools.partial(fwd_kernel, states),
        grid=(slots, channels // width),
        in_specs=[scalars(), item(cols), weight(rank), weight(2), weight(states)] + [block(length)] * 3,
        out_specs=[item(half)] * 4 + [block(length)] * 2 + [block(length * states), item(states)],
        out_shape=[outer((count, half), bf16)] * 4
        + [outer((count, channels), f32)] * 2
        + [outer((count * states, channels), bf16), shaped((count, states), f32)],
        scratch_shapes=[
            pltpu.VMEM((length * states, 128), f32),
            pltpu.VMEM((length * states, 128), f32),
            pltpu.VMEM((length, width), f32),
            pltpu.VMEM((length, width), f32),
            pltpu.VMEM((width // 128, CHUNK * 8, 128), f32),
            pltpu.VMEM((length * states, 128), f32),
            pltpu.VMEM((length, cols), f32),
        ],
        compiler_params=kernel_params(40),
        cost_estimate=pl.CostEstimate(
            flops=32000000000, bytes_accessed=40000000, transcendentals=14000000
        ),
        name="scan_forward",
    )(flip, dbl, dtproj, vec, rates2, held(u), held(z), held(gg))


def backward_call(flip, slot, slots, dbl, dtproj, vec, rates2, u, delta, yg, prior, cout, prev, width):
    count, channels = u.shape
    length = count // slots
    states, rank, cols = rates2.shape[0], dtproj.shape[0], dbl.shape[1]
    rows = prev.shape[0]
    weight = lambda rows: pl.BlockSpec((rows, width), lambda j: (0, j))
    block = lambda rows: pl.BlockSpec((rows, width), lambda j: (slot, j))
    item = lambda wide: pl.BlockSpec((length, wide), lambda j: (slot, 0))
    return pl.pallas_call(
        functools.partial(bwd_kernel, states),
        grid=(channels // width,),
        in_specs=[scalars(), item(cols), weight(rank), weight(2), weight(states)]
        + [block(length)] * 3
        + [block(length * states), item(states), weight(rows)],
        out_specs=[weight(length), whole(length, cols), weight(rows)],
        out_shape=[
            outer((length, channels), f32),
            shaped((length, cols), f32),
            shaped((rows, channels), f32),
        ],
        scratch_shapes=[
            pltpu.VMEM((length * states, 128), f32),
            pltpu.VMEM((length * states, 128), f32),
            pltpu.VMEM((length, width), f32),
            pltpu.VMEM((length, width), f32),
            pltpu.VMEM((length, width), f32),
            pltpu.VMEM((rank, length), bf16),
            pltpu.VMEM((length, rank), f32),
            pltpu.VMEM((width // 128, CHUNK * 8, 128), f32),
            pltpu.VMEM((width // 128, CHUNK * 8, 128), f32),
            pltpu.VMEM((length * states, 128), f32),
            pltpu.VMEM((length, cols), f32),
        ],
        compiler_params=kernel_params(40),
        cost_estimate=pl.CostEstimate(
            flops=22000000000, bytes_accessed=20000000, transcendentals=7000000
        ),
        name="scan_backward",
    )(flip, dbl, dtproj, vec, rates2, held(u), held(delta), held(yg), held(prior), cout, prev)


def local(
    tokens,
    cond,
    counts,
    valid,
    ada_weight,
    ada_bias,
    in_weight,
    conv_weight,
    conv_bias,
    xproj_weight,
    dtproj_weight,
    dt_bias,
    a_log,
    skip_gain,
    out_weight,
    cotangent,
):
    slot_count, shard_rows, model = tokens.shape
    dirs = lax.axis_size("dir")
    dps = lax.axis_size("dp")
    me = lax.axis_index("dir")
    dp_index = lax.axis_index("dp")
    core = me & 1
    half = in_weight.shape[1] // 2
    rank = dtproj_weight.shape[0]
    states = a_log.shape[1]
    tap_count = conv_weight.shape[1]
    cols = xproj_weight.shape[1]
    slots = range(slot_count)
    width = 512 if dt_bias.shape[0] % 512 == 0 else 128
    first, second = bit_orders("dp")
    z_bit, out_bit = first[0], second[0]
    scalar = lambda value: value.astype(jnp.int32).reshape(1)
    flip, me_ref = scalar(core), scalar(me)
    z_side, out_side = scalar((dp_index >> z_bit) & 1), scalar((dp_index >> out_bit) & 1)

    live_slots = (jnp.arange(slot_count) < counts[0]).astype(f32)
    full_mask = valid.astype(f32) * live_slots[:, None]
    mask_cols = full_mask[:, :, None]
    local_mask = lax.dynamic_slice_in_dim(full_mask, me * shard_rows, shard_rows, 1)[:, :, None]

    def gather_rows(block, *earlier):
        over = after(swap(block, "dir", 1), *earlier)
        return block, over, swap(block, "dir", 0), swap(over, "dir", 0)

    in_send = lax.dynamic_slice_in_dim(in_weight, (1 - core) * half, half, 1)
    in_there = swap(in_send, "dir", 0)
    cond_act = jax.nn.silu(cond.astype(f32)).astype(bf16)
    modulation = matmul(after(cond_act, in_send), ada_weight) + ada_bias.astype(f32)[None, :]
    mods = modulation.reshape(slot_count, 3, model)
    token_blocks = gather_rows(tokens, modulation)
    cot_blocks = gather_rows(cotangent, token_blocks[1])
    out_there = swap(out_weight, "dir", 0)

    taps = jnp.concatenate(
        [jnp.transpose(conv_weight.astype(f32)), conv_bias.astype(f32)[None, :]], 0
    )
    vec = jnp.stack([dt_bias, skip_gain])
    rates2 = -jnp.exp(jnp.transpose(a_log)) * LOG2E

    left_mine, left_give, own = norm_call(
        me_ref,
        z_side,
        token_blocks,
        mask_cols,
        after(mods, cot_blocks[1]),
        in_weight,
        width,
        model // dps << z_bit,
    )
    other = swap(own, "dir", 0)
    x, z, u, part = conv_call(flip, own, other, mask_cols, taps, xproj_weight, half)
    part_there = swap(part, "dir", 1)
    branch_mine, branch_give, gg = gate_call(
        me_ref,
        out_side,
        cot_blocks,
        mask_cols,
        after(mods, part),
        out_weight,
        out_there,
        model // dps << out_bit,
    )
    left_there = swap(left_give, "dp", z_bit)
    branch_there = swap(branch_give, "dp", out_bit)
    dbl = part + after(part_there, gg)
    gate_keep, gate_send, z_keep, z_send, *saved = forward_call(
        flip, dbl, dtproj_weight, vec, rates2, u, z, gg, slot_count, width
    )
    gate_send, z_send = after((gate_send, z_send), left_there, branch_there)
    gate_all, z_all = pair_call(
        gate_keep, swap(gate_send, "dir", 0), z_keep, swap(z_send, "dir", 0), slot_count
    )
    gate_there = swap(gate_all, "dp", out_bit)
    z_there = swap(z_all, "dp", z_bit)

    rest = lambda out: [bit for bit in first if bit != out]
    scan_rows = -(-(rank + states + 2) // 8) * 8
    packed = jnp.zeros((scan_rows, dt_bias.shape[0]), f32)
    backs, dgs = [], []
    u_tied = after(u, z_all, gate_all)
    for slot in slots:
        us, part_back, packed = backward_call(
            flip, slot, slot_count, dbl, dtproj_weight, vec, rates2, u_tied, *saved, packed, width
        )
        there = swap(part_back, "dir", 1)
        backs.append((us, part_back, there))
        if slot == 0:
            z_part = Scatter(
                contract_rows(left_mine, after(z_all, part_back))
                + contract_rows(left_there, after(z_there, part_back)),
                "dp",
                rest(z_bit),
            )
            out_part = Scatter(
                contract_rows(branch_mine, after(gate_all, part_back))
                + contract_rows(branch_there, after(gate_there, part_back)),
                "dp",
                rest(out_bit),
            )
            dgs.append((part_back + after(there, z_part.send, out_part.send)).astype(bf16))
            u_tied, z_part.send, out_part.send = after((u, z_part.send, out_part.send), dgs[0])
    end = backs[-1][1]
    z_part.step(end)
    out_part.step(end)

    conv_rows = -(-(cols + tap_count + 1) // 8) * 8
    conv_packed = jnp.zeros((conv_rows, dt_bias.shape[0]), f32)
    pairs = []
    for slot in slots:
        us, part_back, there = backs[slot]
        if slot == 0:
            dg = after(dgs[0], z_part.send, out_part.send)
        else:
            dg = (part_back + after(there, pairs[-1][0])).astype(bf16)
        keep, send, conv_packed = conv_back_call(
            flip, slot, x, u, mask_cols, taps, xproj_weight, us, dg, conv_packed
        )
        pairs.append((keep, send))
    z_part.step(pairs[-1][1])
    pairs = [(keep, swap(after(send, z_part.values), "dir", 0)) for keep, send in pairs]
    x_all = join_call(pairs)
    x_there = swap(x_all, "dp", z_bit)
    shared = SharedSum(pack_call(out_side, after(conv_packed, x_all), packed), "dp", second)
    norm_keep, norm_give = proj_back_call(
        flip, after(x_all, shared.send), z_all, in_weight, in_there, shard_rows, width
    )
    rows_keep, rows_give = branch_call(
        flip, after(gate_all, norm_give), out_weight, shard_rows, width
    )
    out_part.step(rows_give)
    shared.step(out_part.values)
    x_part = contract_rows(left_mine, after(x_all, shared.send)) + contract_rows(
        left_there, after(x_there, shared.send)
    )
    x_part = Scatter(x_part, "dp", rest(z_bit))
    norm_there = swap(after(norm_give, x_part.send), "dir", 0)
    rows_there = swap(after(rows_give, x_part.send), "dir", 0)
    norm_mine, norm_sent = fold_call(me_ref, norm_keep, norm_there, slot_count)
    norm_far = swap(norm_sent, "dir", 1)
    rows_mine, branch_sent = fold_call(me_ref, rows_keep, after(rows_there, norm_sent), slot_count)
    branch_far = swap(branch_sent, "dir", 1)
    shared.step(branch_sent)

    mixed, token_grads, mod_part = rows_call(
        tokens,
        cotangent,
        local_mask,
        mods,
        rows_mine,
        after(branch_far, shared.send),
        norm_mine,
        after(norm_far, shared.send),
    )
    mod_there = swap(mod_part, "dir", 0)
    shared.step(mod_part)
    x_part.step(shared.send)
    mod_pair = mod_part + after(mod_there, x_part.send)
    mod_far = swap(mod_pair, "dir", 1)
    shared.step(mod_pair)
    mod_total = mod_pair + after(mod_far, shared.send)
    mod_low = mod_total.astype(bf16).reshape(slot_count, 3 * model)
    cond_grad = cond_call(mod_low, ada_weight, cond)
    have = []
    sides = jnp.concatenate([mod_low, after(cond_act, end)], 1)
    sides = gather_bit(sides, "dp", first[0], have, cond_grad)
    while len(shared.plan) > 1:
        shared.step(sides)
    keep, there = shared.last(sides)
    for bit in first[1:-1]:
        sides = gather_bit(sides, "dp", bit, have)
    sides = gather_bit(sides, "dp", first[-1], have)
    sides = sides.reshape(dps * slot_count, -1)
    total_columns = ada_weight.shape[1]
    columns = total_columns // dirs
    rows = ada_weight.shape[0] // dps
    mod_all = lax.dynamic_slice_in_dim(sides, me * columns, columns, 1)
    act_mine = lax.dynamic_slice_in_dim(sides, total_columns + dp_index * rows, rows, 1)
    ada_sum = contract_rows(act_mine, mod_all)
    portion = total_columns // dps
    bias_part = lax.dynamic_slice_in_dim(sides, dp_index * portion, portion, 1)
    bias_sum = jnp.sum(bias_part.astype(f32), axis=0)

    xproj_sum, kernel_sum, dtproj_sum, rate_sum, vec_sum = unpack_call(
        out_side, keep, there, cols, tap_count, conv_rows, rank, states
    )
    while x_part.order:
        x_part.step(xproj_sum)
    while z_part.order:
        z_part.step(xproj_sum)
    while out_part.order:
        out_part.step(xproj_sum)
    x_sum = x_part.values
    z_sum = z_part.values
    out_sum = jnp.transpose(out_part.values)
    keep_sum = jnp.where(core == 0, x_sum, z_sum)
    send_sum = jnp.where(core == 0, z_sum, x_sum)
    in_sum = ordered(core, keep_sum, swap(send_sum, "dir", 0), 1)

    return (
        mixed,
        token_grads,
        cond_grad,
        ada_sum,
        bias_sum,
        in_sum,
        kernel_sum,
        vec_sum[0],
        xproj_sum,
        dtproj_sum,
        vec_sum[1],
        rate_sum,
        vec_sum[2],
        out_sum,
    )


def solution(mesh):
    in_specs = (
        P("dp", "dir", None),
        P("dp", None),
        P("dp"),
        P("dp", None),
        P(),
        P(),
        P(None, "dir"),
        P("dir", None),
        P("dir"),
        P("dir", None),
        P(None, "dir"),
        P("dir"),
        P("dir", None),
        P("dir"),
        P("dir", None),
        P("dp", "dir", None),
    )
    out_specs = (
        P("dp", "dir", None),
        P("dp", "dir", None),
        P("dp", None),
        P("dp", "dir"),
        P("dp"),
        P("dp", "dir"),
        P("dir", None),
        P("dir"),
        P("dir", None),
        P(None, "dir"),
        P("dir"),
        P("dir", None),
        P("dir"),
        P("dir", "dp"),
    )
    return jax.shard_map(local, mesh=mesh, in_specs=in_specs, out_specs=out_specs, check_vma=False)
```

profile of v0, /device:TPU:0, one launch (start us, length us, event | category | flops | bytes accessed | tf_op | source)
XLA Modules:
  0.0 272.6 jit_solution(9901682792901917586)
XLA Ops:
  0.6 3.0 %collective-permute-start = (bf16[2,64,1536]{2,1,0:T(8,128)(2,1)}, bf16[2,64,1536]{2,1,0:T(8,128)(2,1)S(1)}, u32[]{:S(2)}, u32[]{:S(2)}) collective-permute-start(bf16[2,64,1536]{2,1,0:T(8,128)(2,1)} %tokens_ref.1), channel_id=1, source_target_pairs={{0,2},{1,3},{2,0},{3,1},{4,6},{5,7},{6,4},{7,5},{8,10},{9,11},{10,... | collective-permute-start | bytes 1179656 | tf_op jit(solution)/shard_map/ppermute | solution.py:21
  4.6 3.2 %constant_dynamic-slice_fusion = bf16[1536,768]{1,0:T(8,128)(2,1)} fusion(bf16[1536,1536]{1,0:T(8,128)(2,1)} %weight_ref.5, s32[]{:T(128)S(6)} %select_n.135), kind=kLoop, calls=%fused_computation.57 | loop fusion | bytes 4718596 | tf_op jit(solution)/shard_map/dynamic_slice | solution.py:1047
  7.8 7.1 %convolution_add_fusion = f32[2,4608]{1,0:T(2,128)S(1)} fusion(bf16[2,1536]{1,0:T(2,128)(2,1)S(1)} %fusion.13, bf16[1536,4608]{1,0:T(8,128)(2,1)} %weight_ref.7, f32[4608]{0:T(1024)S(1)} %convert_element_type.112), kind=kOutput, calls=%fused_computation | convolution fusion | flops 28320768 | bytes 14217216 | tf_op jit(solution)/shard_map/dot_general | solution.py:37
  17.2 4.4 %collective-permute-done.3.over_ref = bf16[2,64,1536]{2,1,0:T(8,128)(2,1)} collective-permute-done((bf16[2,64,1536]{2,1,0:T(8,128)(2,1)}, bf16[2,64,1536]{2,1,0:T(8,128)(2,1)}, u32[]{:S(2)}, u32[]{:S(2)}) %collective-permute-start.3) | collective-permute-done | bytes 393248 | tf_op jit(solution)/shard_map/ppermute | solution.py:21
  22.6 6.8 %norm_project.1 = (bf16[512,768]{1,0:T(8,128)(2,1)S(1)}, bf16[512,768]{1,0:T(8,128)(2,1)S(1)}, bf16[512,1536]{1,0:T(8,128)(2,1)S(1)}) custom-call(s32[1]{0:T(128)} %bitcast.2.me_ref, s32[1]{0:T(128)} %bitcast.4.side_ref, bf16[2,64,1536]{2,1,0:T(8,128)(2,1)S(1)} %copy-done.9, bf16[2,64,1536]{2,1,0:T(8,128)(2,1)S(1)} %copy-done.21, ...), custom_call_target="tpu_custom_call" | custom-call | flops 1000 | bytes 1000 | tf_op jit(solution)/shard_map/norm_project/pallas_call | solution.py:216
  31.0 3.8 %collective-permute-done.4.other_ref = bf16[512,1536]{1,0:T(8,128)(2,1)S(1)} collective-permute-done((bf16[512,1536]{1,0:T(8,128)(2,1)S(1)}, bf16[512,1536]{1,0:T(8,128)(2,1)S(1)}, u32[]{:S(2)}, u32[]{:S(2)}) %collective-permute-start.4) | collective-permute-done | bytes 1572896 | tf_op jit(solution)/shard_map/ppermute | solution.py:21
  34.9 5.7 %conv_forward.1 = (bf16[512,1536]{1,0:T(8,128)(2,1)}, bf16[512,1536]{1,0:T(8,128)(2,1)}, bf16[512,1536]{1,0:T(8,128)(2,1)}, f32[512,128]{1,0:T(8,128)}) custom-call(s32[1]{0:T(128)} %bitcast.3.flip_ref, bf16[512,1536]{1,0:T(8,128)(2,1)S(1)} %get-tuple-element.114.own_ref, bf16[512,1536]{1,0:T(8,128)(2,1)S(1)} %collective-permute-done.4.other_ref, ...), custom_call_target="tpu_custom_call" | custom-call | flops 1000 | bytes 1000 | tf_op jit(solution)/shard_map/conv_forward/pallas_call | solution.py:666
  40.5 1.7 collective-permute-start.5
  43.0 1.6 collective-permute-start.9
  44.6 8.0 %gate_project.1 = (bf16[512,768]{1,0:T(8,128)(2,1)S(1)}, bf16[512,768]{1,0:T(8,128)(2,1)S(1)}, bf16[512,1536]{1,0:T(8,128)(2,1)}) custom-call(s32[1]{0:T(128)} %bitcast.2.me_ref, s32[1]{0:T(128)} %bitcast.7.side_ref, bf16[2,64,1536]{2,1,0:T(8,128)(2,1)} %cot_ref.1, bf16[2,64,1536]{2,1,0:T(8,128)(2,1)} %collective-permute-done.3.over_ref, ...), custom_call_target="tpu_custom_call" | custom-call | flops 1000 | bytes 1000 | tf_op jit(solution)/shard_map/gate_project/pallas_call | solution.py:279
  53.5 1.6 collective-permute-start.10
  56.2 34.8 %scan_forward.1 = (bf16[512,768]{1,0:T(8,128)(2,1)}, bf16[512,768]{1,0:T(8,128)(2,1)}, bf16[512,768]{1,0:T(8,128)(2,1)}, bf16[512,768]{1,0:T(8,128)(2,1)}, f32[5...) custom-call(s32[1]{0:T(128)} %bitcast.3.flip_ref, ...), custom_call_target="tpu_custom_call" | custom-call | flops 32000000000 | bytes 40000000 | tf_op jit(solution)/shard_map/scan_forward/pallas_call | solution.py:935
  94.0 2.0 collective-permute-done.11.second_ref
  96.0 2.2 collective-permute-done.12.fourth_ref
  99.1 2.0 pair_sums.1
  102.3 22.3 %scan_backward.2 = (f32[256,1536]{1,0:T(8,128)}, f32[256,128]{1,0:T(8,128)S(1)}, f32[120,1536]{1,0:T(8,128)S(1)}) custom-call(s32[1]{0:T(128)} %bitcast.3.flip_ref, f32[512,128]{1,0:T(8,128)S(1)} %add.120.dbl_ref, bf16[96,1536]{1,0:T(8,128)(2,1)S(1)} %copy-done.26, f32[2,1536]{1,0:T(2,128)S(1)} %pad_maximum_fusion.vec_ref, f32[16,1536]{1,0:T(8,128)S(1)} %copy-done.22, ...), custom_call_target="tpu_custom_call" | custom-call | flops 22000001024 | bytes 20000000 | tf_op jit(solution)/shard_map/scan_backward/pallas_call | solution.py:968
  129.6 1.6 collective-permute-start.17
  131.2 1.6 collective-permute-start.16
  132.8 22.2 %scan_backward.3 = (f32[256,1536]{1,0:T(8,128)}, f32[256,128]{1,0:T(8,128)S(1)}, f32[120,1536]{1,0:T(8,128)S(1)}) custom-call(s32[1]{0:T(128)} %bitcast.3.flip_ref, f32[512,128]{1,0:T(8,128)S(1)} %add.120.dbl_ref, bf16[96,1536]{1,0:T(8,128)(2,1)S(1)} %copy-done.27, f32[2,1536]{1,0:T(2,128)S(1)} %pad_maximum_fusion.vec_ref, f32[16,1536]{1,0:T(8,128)S(1)} %copy-done.23, ...), custom_call_target="tpu_custom_call" | custom-call | flops 22000001024 | bytes 20000000 | tf_op jit(solution)/shard_map/scan_backward/pallas_call | solution.py:968
  155.0 1.2 collective-permute-start.19
  156.3 2.7 collective-permute-start.18
  160.0 6.3 %conv_backward.2 = (bf16[256,768]{1,0:T(8,128)(2,1)S(1)}, bf16[256,768]{1,0:T(8,128)(2,1)S(1)}, f32[136,1536]{1,0:T(8,128)S(1)}) custom-call(s32[1]{0:T(128)} %bitcast.3.flip_ref, bf16[512,1536]{1,0:T(8,128)(2,1)} %get-tuple-element.130.x_ref, bf16[512,1536]{1,0:T(8,128)(2,1)} %get-tuple-element.147.u_ref, f32[2,256,1]{2,1,0:T(8,128)S(1)} %copy.36.mask_ref, ...), custom_call_target="tpu_custom_call" | custom-call | flops 1000 | bytes 1000 | tf_op jit(solution)/shard_map/conv_backward/pallas_call | solution.py:694
  166.4 6.3 %conv_backward.3 = (bf16[256,768]{1,0:T(8,128)(2,1)S(1)}, bf16[256,768]{1,0:T(8,128)(2,1)S(1)}, f32[136,1536]{1,0:T(8,128)S(1)}) custom-call(s32[1]{0:T(128)} %bitcast.3.flip_ref, bf16[512,1536]{1,0:T(8,128)(2,1)} %get-tuple-element.130.x_ref, bf16[512,1536]{1,0:T(8,128)(2,1)} %get-tuple-element.147.u_ref, f32[2,256,1]{2,1,0:T(8,128)S(1)} %copy.36.mask_ref, ...), custom_call_target="tpu_custom_call" | custom-call | flops 1000 | bytes 1000 | tf_op jit(solution)/shard_map/conv_backward/pallas_call | solution.py:694
  178.0 6.7 %proj_back.1 = (f32[256,1536]{1,0:T(8,128)S(1)}, bf16[256,1536]{1,0:T(8,128)(2,1)}) custom-call(s32[1]{0:T(128)} %bitcast.3.flip_ref, bf16[512,768]{1,0:T(8,128)(2,1)S(1)} %join_sums.1.x_ref, bf16[512,768]{1,0:T(8,128)(2,1)S(1)} %get-tuple-element.140.z_ref, bf16[1536,1536]{1,0:T(8,128)(2,1)} %weight_ref.5, bf16[1536,768]{1,0:T(8,128)(2,1)} %collective-permute-done.22.there_ref), custom_call_target="tpu_custom_call" | custom-call | flops 1000 | bytes 1000 | tf_op jit(solution)/shard_map/proj_back/pallas_call | solution.py:537
  184.7 2.7 %branch_rows.1 = (f32[256,1536]{1,0:T(8,128)S(1)}, bf16[256,1536]{1,0:T(8,128)(2,1)}) custom-call(s32[1]{0:T(128)} %bitcast.3.flip_ref, bf16[512,768]{1,0:T(8,128)(2,1)S(1)} %copy-done.6, bf16[768,1536]{1,0:T(8,128)(2,1)S(1)} %copy-done.1), custom_call_target="tpu_custom_call" | custom-call | flops 1000 | bytes 1000 | tf_op jit(solution)/shard_map/branch_rows/pallas_call | solution.py:494
  187.5 3.1 %collective-permute-done.24 = bf16[192,768]{1,0:T(8,128)(2,1)} collective-permute-done((bf16[192,768]{1,0:T(8,128)(2,1)}, bf16[192,768]{1,0:T(8,128)(2,1)}, u32[]{:S(2)}, u32[]{:S(2)}) %collective-permute-start.24) | collective-permute-done | bytes 294944 | tf_op jit(solution)/shard_map/ppermute | solution.py:21
  190.6 1.8 bitcast_add_fusion.4
  192.4 2.3 collective-permute-done.23
  201.1 1.6 collective-permute-start.32
  203.8 1.4 copy-done.8
  205.2 2.1 fold_rows.2
  210.8 1.2 collective-permute-start.28
  213.1 7.2 %collective-permute-done.30.norm_far_ref = bf16[2,64,1536]{2,1,0:T(8,128)(2,1)S(1)} collective-permute-done((bf16[2,64,1536]{2,1,0:T(8,128)(2,1)}, bf16[2,64,1536]{2,1,0:T(8,128)(2,1)S(1)}, u32[]{:S(2)}, u32[]{:S(2)}) %collective-permute-start.30) | collective-permute-done | bytes 393248 | tf_op jit(solution)/shard_map/ppermute | solution.py:21
  220.4 7.6 %collective-permute-done.28.branch_far_ref = bf16[2,64,1536]{2,1,0:T(8,128)(2,1)S(1)} collective-permute-done((bf16[2,64,1536]{2,1,0:T(8,128)(2,1)}, bf16[2,64,1536]{2,1,0:T(8,128)(2,1)S(1)}, u32[]{:S(2)}, u32[]{:S(2)}) %collective-permute-start.28) | collective-permute-done | bytes 393248 | tf_op jit(solution)/shard_map/ppermute | solution.py:21
  228.0 1.1 copy-done.15
  229.1 1.1 copy-done.17
  230.3 3.0 %owned_rows.1 = (f32[2,64,1536]{2,1,0:T(8,128)}, f32[2,64,1536]{2,1,0:T(8,128)}, f32[2,3,1536]{2,1,0:T(4,128)S(1)}) custom-call(bf16[2,64,1536]{2,1,0:T(8,128)(2,1)S(1)} %copy-done.9, bf16[2,64,1536]{2,1,0:T(8,128)(2,1)} %cot_ref.1, f32[2,64,1]{2,1,0:T(8,128)S(1)} %copy.44.mask_ref, f32[2,3,1536]{2,1,0:T(4,128)S(1)} %copy-done.11, ...), custom_call_target="tpu_custom_call" | custom-call | flops 1000 | bytes 1000 | tf_op jit(solution)/shard_map/owned_rows/pallas_call | solution.py:460
  234.0 1.2 bitcast_add_fusion
  236.1 4.6 %collective-permute-done.35 = bf16[64,1536]{1,0:T(8,128)(2,1)S(1)} collective-permute-done((bf16[64,1536]{1,0:T(8,128)(2,1)S(1)}, bf16[64,1536]{1,0:T(8,128)(2,1)S(1)}, u32[]{:S(2)}, u32[]{:S(2)}) %collective-permute-start.35) | collective-permute-done | bytes 196640 | tf_op jit(solution)/shard_map/ppermute | solution.py:21
  242.6 1.2 collective-permute-start.40
  243.8 8.8 %cond_rows.1 = f32[2,1536]{1,0:T(2,128)} custom-call(bf16[2,4608]{1,0:T(2,128)(2,1)S(1)} %bitcast.84, bf16[1536,4608]{1,0:T(8,128)(2,1)} %weight_ref.7, bf16[2,1536]{1,0:T(2,128)(2,1)S(1)} %copy-done.24), custom_call_target="tpu_custom_call" | custom-call | flops 1000 | bytes 1000 | tf_op jit(solution)/shard_map/cond_rows/pallas_call | solution.py:566
  253.8 6.4 %collective-permute-done.37 = bf16[2,2,6144]{2,1,0:T(2,128)(2,1)S(1)} collective-permute-done((bf16[2,2,6144]{2,1,0:T(2,128)(2,1)S(1)}, bf16[2,2,6144]{2,1,0:T(2,128)(2,1)S(1)}, u32[]{:S(2)}, u32[]{:S(2)}) %collective-permute-start.37) | collective-permute-done | bytes 49184 | tf_op jit(solution)/shard_map/ppermute | solution.py:21
  260.3 1.7 collective-permute-start.38
  262.2 1.8 unpack_sums.1
  264.0 1.1 fusion.4
  265.1 1.6 collective-permute-done.38
  267.8 1.3 fusion.8
  271.5 1.1 maximum_select_fusion
  (226 shorter events, 44.7 us)
Async XLA Ops:
  0.6 14.3 %collective-permute-start = (bf16[2,64,1536]{2,1,0:T(8,128)(2,1)}, bf16[2,64,1536]{2,1,0:T(8,128)(2,1)S(1)}, u32[]{:S(2)}, u32[]{:S(2)}) collective-permute-start(bf16[2,64,1536]{2,1,0:T(8,128)(2,1)} %tokens_ref.1), channel_id=1, source_target_pairs={{0,2},{1,3},{2,0},{3,1},{4,6},{5,7},{6,4},{7,5},{8,10},{9,11},{10,... | collective-permute-start | bytes 1179656 | tf_op jit(solution)/shard_map/ppermute | solution.py:21
  3.7 17.9 %collective-permute-start.1 = (bf16[2,64,1536]{2,1,0:T(8,128)(2,1)}, bf16[2,64,1536]{2,1,0:T(8,128)(2,1)}, u32[]{:S(2)}, u32[]{:S(2)}) collective-permute-start(bf16[2,64,1536]{2,1,0:T(8,128)(2,1)} %tokens_ref.1), channel_id=1, source_target_pairs={{0,1},{1,0},{2,3},{3,2},{4,5},{5,4},{6,7},{7,6},{8,9},{9,8},{10,11... | collective-permute-start | bytes 1179656 | tf_op jit(solution)/shard_map/ppermute | solution.py:21
  3.7 17.9 %collective-permute-start.3 = (bf16[2,64,1536]{2,1,0:T(8,128)(2,1)}, bf16[2,64,1536]{2,1,0:T(8,128)(2,1)}, u32[]{:S(2)}, u32[]{:S(2)}) collective-permute-start(bf16[2,64,1536]{2,1,0:T(8,128)(2,1)} %cot_ref.1), channel_id=1, source_target_pairs={{0,2},{1,3},{2,0},{3,1},{4,6},{5,7},{6,4},{7,5},{8,10},{9,11},{10,... | collective-permute-start | bytes 1179656 | tf_op jit(solution)/shard_map/ppermute | solution.py:21
  7.8 13.7 %copy-start.9 = (bf16[2,64,1536]{2,1,0:T(8,128)(2,1)S(1)}, bf16[2,64,1536]{2,1,0:T(8,128)(2,1)}, u32[]{:S(2)}) copy-start(bf16[2,64,1536]{2,1,0:T(8,128)(2,1)} %tokens_ref.1) | copy-start | bytes 1179652
  14.9 6.6 %collective-permute-start.2 = (bf16[2,64,1536]{2,1,0:T(8,128)(2,1)S(1)}, bf16[2,64,1536]{2,1,0:T(8,128)(2,1)}, u32[]{:S(2)}, u32[]{:S(2)}) collective-permute-start(bf16[2,64,1536]{2,1,0:T(8,128)(2,1)S(1)} %collective-permute-done.over_ref), channel_id=1, source_target_pairs={{0,1},{1,0},{2,3},{3,2},{4,5},{5,4},{6,7},{7,6},{8,9},{9,8},{10,11... | collective-permute-start | bytes 1179656 | tf_op jit(solution)/shard_map/ppermute | solution.py:21
  16.0 28.5 %collective-permute-start.8 = (bf16[768,1536]{1,0:T(8,128)(2,1)S(1)}, bf16[768,1536]{1,0:T(8,128)(2,1)}, u32[]{:S(2)}, u32[]{:S(2)}) collective-permute-start(bf16[768,1536]{1,0:T(8,128)(2,1)S(1)} %copy-done), channel_id=1, source_target_pairs={{0,1},{1,0},{2,3},{3,2},{4,5},{5,4},{6,7},{7,6},{8,9},{9,8},{10,11... | collective-permute-start | bytes 7077896 | tf_op jit(solution)/shard_map/ppermute | solution.py:21
  17.0 27.6 %copy-start.10 = (f32[2,3,1536]{2,1,0:T(4,128)}, f32[2,3,1536]{2,1,0:T(4,128)S(1)}, u32[]{:S(2)}) copy-start(f32[2,3,1536]{2,1,0:T(4,128)S(1)} %reshape.248.mod_ref) | copy-start | bytes 110596
  30.3 4.6 %collective-permute-start.4 = (bf16[512,1536]{1,0:T(8,128)(2,1)S(1)}, bf16[512,1536]{1,0:T(8,128)(2,1)S(1)}, u32[]{:S(2)}, u32[]{:S(2)}) collective-permute-start(bf16[512,1536]{1,0:T(8,128)(2,1)S(1)} %get-tuple-element.114.own_ref), channel_id=1, source_target_pairs={{0,1},{1,0},{2,3},{3,2},{4,5},{5,4},{6,7},{7,6},{8,9},{9,8},{10,11... | collective-permute-start | bytes 4718600 | tf_op jit(solution)/shard_map/ppermute | solution.py:21
  30.3 14.2 %collective-permute-start.6 = (bf16[2,64,1536]{2,1,0:T(8,128)(2,1)}, bf16[2,64,1536]{2,1,0:T(8,128)(2,1)}, u32[]{:S(2)}, u32[]{:S(2)}) collective-permute-start(bf16[2,64,1536]{2,1,0:T(8,128)(2,1)} %cot_ref.1), channel_id=1, source_target_pairs={{0,1},{1,0},{2,3},{3,2},{4,5},{5,4},{6,7},{7,6},{8,9},{9,8},{10,11... | collective-permute-start | bytes 1179656 | tf_op jit(solution)/shard_map/ppermute | solution.py:21
  30.9 13.7 %collective-permute-start.7 = (bf16[2,64,1536]{2,1,0:T(8,128)(2,1)}, bf16[2,64,1536]{2,1,0:T(8,128)(2,1)}, u32[]{:S(2)}, u32[]{:S(2)}) collective-permute-start(bf16[2,64,1536]{2,1,0:T(8,128)(2,1)} %collective-permute-done.3.over_ref), channel_id=1, source_target_pairs={{0,1},{1,0},{2,3},{3,2},{4,5},{5,4},{6,7},{7,6},{8,9},{9,8},{10,11... | collective-permute-start | bytes 1179656 | tf_op jit(solution)/shard_map/ppermute | solution.py:21
  40.5 14.6 %collective-permute-start.5 = (f32[512,128]{1,0:T(8,128)}, f32[512,128]{1,0:T(8,128)}, u32[]{:S(2)}, u32[]{:S(2)}) collective-permute-start(f32[512,128]{1,0:T(8,128)} %get-tuple-element.115), channel_id=1, source_target_pairs={{0,2},{1,3},{2,0},{3,1},{4,6},{5,7},{6,4},{7,5},{8,10},{9,11},{10,... | collective-permute-start | bytes 786440 | tf_op jit(solution)/shard_map/ppermute | solution.py:21
  43.0 48.7 %collective-permute-start.9 = (bf16[512,768]{1,0:T(8,128)(2,1)}, bf16[512,768]{1,0:T(8,128)(2,1)S(1)}, u32[]{:S(2)}, u32[]{:S(2)}) collective-permute-start(bf16[512,768]{1,0:T(8,128)(2,1)} %copy-done.25), channel_id=1, source_target_pairs={{0,4},{4,0},{8,12},{12,8},{16,20},{20,16},{24,28},{28,24},{1,5},{5... | collective-permute-start | bytes 2359304 | tf_op jit(solution)/shard_map/ppermute | solution.py:21
  53.5 38.2 %collective-permute-start.10 = (bf16[512,768]{1,0:T(8,128)(2,1)S(1)}, bf16[512,768]{1,0:T(8,128)(2,1)S(1)}, u32[]{:S(2)}, u32[]{:S(2)}) collective-permute-start(bf16[512,768]{1,0:T(8,128)(2,1)S(1)} %get-tuple-element.125), channel_id=1, source_target_pairs={{0,8},{4,12},{8,0},{12,4},{16,24},{20,28},{24,16},{28,20},{1,9},{5... | collective-permute-start | bytes 2359304 | tf_op jit(solution)/shard_map/ppermute | solution.py:21
  93.5 2.5 collective-permute-start.11
  93.5 4.7 %collective-permute-start.12 = (bf16[512,768]{1,0:T(8,128)(2,1)}, bf16[512,768]{1,0:T(8,128)(2,1)S(1)}, u32[]{:S(2)}, u32[]{:S(2)}) collective-permute-start(bf16[512,768]{1,0:T(8,128)(2,1)} %get-tuple-element.128), channel_id=1, source_target_pairs={{0,1},{1,0},{2,3},{3,2},{4,5},{5,4},{6,7},{7,6},{8,9},{9,8},{10,11... | collective-permute-start | bytes 2359304 | tf_op jit(solution)/shard_map/ppermute | solution.py:21
  94.0 84.0 %collective-permute-start.22 = (bf16[1536,768]{1,0:T(8,128)(2,1)}, bf16[1536,768]{1,0:T(8,128)(2,1)}, u32[]{:S(2)}, u32[]{:S(2)}) collective-permute-start(bf16[1536,768]{1,0:T(8,128)(2,1)} %constant_dynamic-slice_fusion), channel_id=1, source_target_pairs={{0,1},{1,0},{2,3},{3,2},{4,5},{5,4},{6,7},{7,6},{8,9},{9,8},{10,11... | collective-permute-start | bytes 7077896 | tf_op jit(solution)/shard_map/ppermute | solution.py:21
  101.2 24.6 %copy-start.5 = (bf16[512,768]{1,0:T(8,128)(2,1)}, bf16[512,768]{1,0:T(8,128)(2,1)S(1)}, u32[]{:S(2)}) copy-start(bf16[512,768]{1,0:T(8,128)(2,1)S(1)} %get-tuple-element.170.values_ref) | copy-start | bytes 2359300
  101.2 23.8 %collective-permute-start.15 = (bf16[512,768]{1,0:T(8,128)(2,1)S(1)}, bf16[512,768]{1,0:T(8,128)(2,1)S(1)}, u32[]{:S(2)}, u32[]{:S(2)}) collective-permute-start(bf16[512,768]{1,0:T(8,128)(2,1)S(1)} %get-tuple-element.170.values_ref), channel_id=1, source_target_pairs={{0,8},{4,12},{8,0},{12,4},{16,24},{20,28},{24,16},{28,20},{1,9},{5... | collective-permute-start | bytes 2359304 | tf_op jit(solution)/shard_map/ppermute | solution.py:21
  101.7 23.2 %collective-permute-start.14 = (bf16[512,768]{1,0:T(8,128)(2,1)S(1)}, bf16[512,768]{1,0:T(8,128)(2,1)S(1)}, u32[]{:S(2)}, u32[]{:S(2)}) collective-permute-start(bf16[512,768]{1,0:T(8,128)(2,1)S(1)} %get-tuple-element.140.z_ref), channel_id=1, source_target_pairs={{0,4},{4,0},{8,12},{12,8},{16,20},{20,16},{24,28},{28,24},{1,5},{5... | collective-permute-start | bytes 2359304 | tf_op jit(solution)/shard_map/ppermute | solution.py:21
  102.3 22.6 %copy-start.42 = (bf16[512,768]{1,0:T(8,128)(2,1)S(1)}, bf16[512,768]{1,0:T(8,128)(2,1)}, u32[]{:S(2)}) copy-start(bf16[512,768]{1,0:T(8,128)(2,1)} %copy-done.41) | copy-start | bytes 2359300
  124.6 5.0 %collective-permute-start.13 = (f32[256,128]{1,0:T(8,128)S(1)}, f32[256,128]{1,0:T(8,128)S(1)}, u32[]{:S(2)}, u32[]{:S(2)}) collective-permute-start(f32[256,128]{1,0:T(8,128)S(1)} %get-tuple-element.138), channel_id=1, source_target_pairs={{0,2},{1,3},{2,0},{3,1},{4,6},{5,7},{6,4},{7,5},{8,10},{9,11},{10,... | collective-permute-start | bytes 393224 | tf_op jit(solution)/shard_map/ppermute | solution.py:21
  129.6 26.5 %collective-permute-start.17 = (bf16[2,192,768]{2,1,0:T(8,128)(2,1)S(1)}, bf16[2,192,768]{2,1,0:T(8,128)(2,1)S(1)}, u32[]{:S(2)}, u32[]{:S(2)}) collective-permute-start(bf16[2,192,768]{2,1,0:T(8,128)(2,1)S(1)} %get-tuple-element.151), channel_id=1, source_target_pairs={{0,4},{4,0},{8,12},{12,8},{16,20},{20,16},{24,28},{28,24},{1,5},{5... | collective-permute-start | bytes 1769480 | tf_op jit(solution)/shard_map/ppermute | solution.py:21
  131.2 25.0 %collective-permute-start.16 = (bf16[2,192,768]{2,1,0:T(8,128)(2,1)S(1)}, bf16[2,192,768]{2,1,0:T(8,128)(2,1)S(1)}, u32[]{:S(2)}, u32[]{:S(2)}) collective-permute-start(bf16[2,192,768]{2,1,0:T(8,128)(2,1)S(1)} %get-tuple-element.146), channel_id=1, source_target_pairs={{0,8},{4,12},{8,0},{12,4},{16,24},{20,28},{24,16},{28,20},{1,9},{5... | collective-permute-start | bytes 1769480 | tf_op jit(solution)/shard_map/ppermute | solution.py:21
  155.0 11.4 %collective-permute-start.19 = (f32[256,128]{1,0:T(8,128)S(1)}, f32[256,128]{1,0:T(8,128)S(1)}, u32[]{:S(2)}, u32[]{:S(2)}) collective-permute-start(f32[256,128]{1,0:T(8,128)S(1)} %get-tuple-element.149), channel_id=1, source_target_pairs={{0,2},{1,3},{2,0},{3,1},{4,6},{5,7},{6,4},{7,5},{8,10},{9,11},{10,... | collective-permute-start | bytes 393224 | tf_op jit(solution)/shard_map/ppermute | solution.py:21
  156.3 16.4 %collective-permute-start.18 = (bf16[192,768]{1,0:T(8,128)(2,1)S(1)}, bf16[192,768]{1,0:T(8,128)(2,1)S(1)}, u32[]{:S(2)}, u32[]{:S(2)}) collective-permute-start(bf16[192,768]{1,0:T(8,128)(2,1)S(1)} %fusion.5), channel_id=1, source_target_pairs={{0,16},{4,20},{8,24},{12,28},{16,0},{20,4},{24,8},{28,12},{1,17},{... | collective-permute-start | bytes 884744 | tf_op jit(solution)/shard_map/ppermute | solution.py:21
  173.6 1.7 collective-permute-start.21
  173.6 2.3 collective-permute-start.20
  174.1 16.4 %collective-permute-start.24 = (bf16[192,768]{1,0:T(8,128)(2,1)}, bf16[192,768]{1,0:T(8,128)(2,1)}, u32[]{:S(2)}, u32[]{:S(2)}) collective-permute-start(bf16[192,768]{1,0:T(8,128)(2,1)} %fusion.6), channel_id=1, source_target_pairs={{0,16},{4,20},{8,24},{12,28},{16,0},{20,4},{24,8},{28,12},{1,17},{... | collective-permute-start | bytes 884744 | tf_op jit(solution)/shard_map/ppermute | solution.py:21
  177.0 17.7 %collective-permute-start.23 = (bf16[128,1536]{1,0:T(8,128)(2,1)}, bf16[128,1536]{1,0:T(8,128)(2,1)}, u32[]{:S(2)}, u32[]{:S(2)}) collective-permute-start(bf16[128,1536]{1,0:T(8,128)(2,1)} %get-tuple-element.167), channel_id=1, source_target_pairs={{0,8},{4,12},{8,0},{12,4},{16,24},{20,28},{24,16},{28,20},{1,9},{5... | collective-permute-start | bytes 1179656 | tf_op jit(solution)/shard_map/ppermute | solution.py:21
  177.5 19.3 %collective-permute-start.25 = (bf16[512,768]{1,0:T(8,128)(2,1)S(1)}, bf16[512,768]{1,0:T(8,128)(2,1)S(1)}, u32[]{:S(2)}, u32[]{:S(2)}) collective-permute-start(bf16[512,768]{1,0:T(8,128)(2,1)S(1)} %join_sums.1.x_ref), channel_id=1, source_target_pairs={{0,4},{4,0},{8,12},{12,8},{16,20},{20,16},{24,28},{28,24},{1,5},{5... | collective-permute-start | bytes 2359304 | tf_op jit(solution)/shard_map/ppermute | solution.py:21
  200.1 3.7 %collective-permute-start.27 = (bf16[256,1536]{1,0:T(8,128)(2,1)}, bf16[256,1536]{1,0:T(8,128)(2,1)}, u32[]{:S(2)}, u32[]{:S(2)}) collective-permute-start(bf16[256,1536]{1,0:T(8,128)(2,1)} %get-tuple-element.180), channel_id=1, source_target_pairs={{0,1},{1,0},{2,3},{3,2},{4,5},{5,4},{6,7},{7,6},{8,9},{9,8},{10,11... | collective-permute-start | bytes 2359304 | tf_op jit(solution)/shard_map/ppermute | solution.py:21
  200.1 9.0 %collective-permute-start.26 = (bf16[256,1536]{1,0:T(8,128)(2,1)}, bf16[256,1536]{1,0:T(8,128)(2,1)S(1)}, u32[]{:S(2)}, u32[]{:S(2)}) collective-permute-start(bf16[256,1536]{1,0:T(8,128)(2,1)} %get-tuple-element.178), channel_id=1, source_target_pairs={{0,1},{1,0},{2,3},{3,2},{4,5},{5,4},{6,7},{7,6},{8,9},{9,8},{10,11... | collective-permute-start | bytes 2359304 | tf_op jit(solution)/shard_map/ppermute | solution.py:21
  200.6 11.4 %collective-permute-start.29 = (bf16[64,1536]{1,0:T(8,128)(2,1)}, bf16[64,1536]{1,0:T(8,128)(2,1)S(1)}, u32[]{:S(2)}, u32[]{:S(2)}) collective-permute-start(bf16[64,1536]{1,0:T(8,128)(2,1)} %dynamic-slice_convert_fusion.3), channel_id=1, source_target_pairs={{0,4},{4,0},{8,12},{12,8},{16,20},{20,16},{24,28},{28,24},{1,5},{5... | collective-permute-start | bytes 589832 | tf_op jit(solution)/shard_map/ppermute | solution.py:21
  201.1 32.8 %collective-permute-start.32 = (bf16[2,192,768]{2,1,0:T(8,128)(2,1)}, bf16[2,192,768]{2,1,0:T(8,128)(2,1)}, u32[]{:S(2)}, u32[]{:S(2)}) collective-permute-start(bf16[2,192,768]{2,1,0:T(8,128)(2,1)} %fusion.2), channel_id=1, source_target_pairs={{0,8},{4,12},{8,0},{12,4},{16,24},{20,28},{24,16},{28,20},{1,9},{5... | collective-permute-start | bytes 1769480 | tf_op jit(solution)/shard_map/ppermute | solution.py:21
  205.2 22.8 %copy-start.11 = (f32[2,3,1536]{2,1,0:T(4,128)S(1)}, f32[2,3,1536]{2,1,0:T(4,128)}, u32[]{:S(2)}) copy-start(f32[2,3,1536]{2,1,0:T(4,128)} %copy-done.10) | copy-start | bytes 110596
  208.2 12.2 %collective-permute-start.30 = (bf16[2,64,1536]{2,1,0:T(8,128)(2,1)}, bf16[2,64,1536]{2,1,0:T(8,128)(2,1)S(1)}, u32[]{:S(2)}, u32[]{:S(2)}) collective-permute-start(bf16[2,64,1536]{2,1,0:T(8,128)(2,1)} %get-tuple-element.181), channel_id=1, source_target_pairs={{0,2},{1,3},{2,0},{3,1},{4,6},{5,7},{6,4},{7,5},{8,10},{9,11},{10,... | collective-permute-start | bytes 1179656 | tf_op jit(solution)/shard_map/ppermute | solution.py:21
  210.8 17.2 %collective-permute-start.28 = (bf16[2,64,1536]{2,1,0:T(8,128)(2,1)}, bf16[2,64,1536]{2,1,0:T(8,128)(2,1)S(1)}, u32[]{:S(2)}, u32[]{:S(2)}) collective-permute-start(bf16[2,64,1536]{2,1,0:T(8,128)(2,1)} %get-tuple-element.184), channel_id=1, source_target_pairs={{0,2},{1,3},{2,0},{3,1},{4,6},{5,7},{6,4},{7,5},{8,10},{9,11},{10,... | collective-permute-start | bytes 1179656 | tf_op jit(solution)/shard_map/ppermute | solution.py:21
  212.0 21.3 %collective-permute-start.33 = (bf16[64,1536]{1,0:T(8,128)(2,1)S(1)}, bf16[64,1536]{1,0:T(8,128)(2,1)S(1)}, u32[]{:S(2)}, u32[]{:S(2)}) collective-permute-start(bf16[64,1536]{1,0:T(8,128)(2,1)S(1)} %add_convert_fusion.1), channel_id=1, source_target_pairs={{0,16},{4,20},{8,24},{12,28},{16,0},{20,4},{24,8},{28,12},{1,17},{... | collective-permute-start | bytes 589832 | tf_op jit(solution)/shard_map/ppermute | solution.py:21
  233.3 1.9 collective-permute-start.31
  233.3 7.4 %collective-permute-start.35 = (bf16[64,1536]{1,0:T(8,128)(2,1)S(1)}, bf16[64,1536]{1,0:T(8,128)(2,1)S(1)}, u32[]{:S(2)}, u32[]{:S(2)}) collective-permute-start(bf16[64,1536]{1,0:T(8,128)(2,1)S(1)} %add_convert_fusion), channel_id=1, source_target_pairs={{0,4},{4,0},{8,12},{12,8},{16,20},{20,16},{24,28},{28,24},{1,5},{5... | collective-permute-start | bytes 589832 | tf_op jit(solution)/shard_map/ppermute | solution.py:21
  235.2 5.6 %collective-permute-start.34 = (f32[2,3,1536]{2,1,0:T(4,128)S(1)}, f32[2,3,1536]{2,1,0:T(4,128)S(1)}, u32[]{:S(2)}, u32[]{:S(2)}) collective-permute-start(f32[2,3,1536]{2,1,0:T(4,128)S(1)} %add.142), channel_id=1, source_target_pairs={{0,2},{1,3},{2,0},{3,1},{4,6},{5,7},{6,4},{7,5},{8,10},{9,11},{10,... | collective-permute-start | bytes 110600 | tf_op jit(solution)/shard_map/ppermute | solution.py:21
  240.9 11.8 %collective-permute-start.36 = (bf16[2,6144]{1,0:T(2,128)(2,1)S(1)}, bf16[2,6144]{1,0:T(2,128)(2,1)S(1)}, u32[]{:S(2)}, u32[]{:S(2)}) collective-permute-start(bf16[2,6144]{1,0:T(2,128)(2,1)S(1)} %constant_dynamic-update-slice_fusion), channel_id=1, source_target_pairs={{0,4},{4,0},{8,12},{12,8},{16,20},{20,16},{24,28},{28,24},{1,5},{5... | collective-permute-start | bytes 73736 | tf_op jit(solution)/shard_map/ppermute | solution.py:21
  241.5 22.5 %copy-start.40 = (f32[192,768]{1,0:T(8,128)S(1)}, f32[192,768]{1,0:T(8,128)}, u32[]{:S(2)}) copy-start(f32[192,768]{1,0:T(8,128)} %bitcast_add_fusion.5) | copy-start | bytes 1769476
  241.5 22.5 %collective-permute-start.39 = (bf16[192,768]{1,0:T(8,128)(2,1)S(1)}, bf16[192,768]{1,0:T(8,128)(2,1)S(1)}, u32[]{:S(2)}, u32[]{:S(2)}) collective-permute-start(bf16[192,768]{1,0:T(8,128)(2,1)S(1)} %fusion.7), channel_id=1, source_target_pairs={{0,16},{4,20},{8,24},{12,28},{16,0},{20,4},{24,8},{28,12},{1,17},{... | collective-permute-start | bytes 884744 | tf_op jit(solution)/shard_map/ppermute | solution.py:21
  242.6 19.6 %collective-permute-start.40 = (bf16[128,1536]{1,0:T(8,128)(2,1)S(1)}, bf16[128,1536]{1,0:T(8,128)(2,1)S(1)}, u32[]{:S(2)}, u32[]{:S(2)}) collective-permute-start(bf16[128,1536]{1,0:T(8,128)(2,1)S(1)} %maximum_select_fusion.1.keep_ref), channel_id=1, source_target_pairs={{0,8},{4,12},{8,0},{12,4},{16,24},{20,28},{24,16},{28,20},{1,9},{5... | collective-permute-start | bytes 1179656 | tf_op jit(solution)/shard_map/ppermute | solution.py:21
  252.7 7.4 %collective-permute-start.37 = (bf16[2,2,6144]{2,1,0:T(2,128)(2,1)S(1)}, bf16[2,2,6144]{2,1,0:T(2,128)(2,1)S(1)}, u32[]{:S(2)}, u32[]{:S(2)}) collective-permute-start(bf16[2,2,6144]{2,1,0:T(2,128)(2,1)S(1)} %broadcast_select_fusion.3), channel_id=1, source_target_pairs={{0,8},{4,12},{8,0},{12,4},{16,24},{20,28},{24,16},{28,20},{1,9},{5... | collective-permute-start | bytes 147464 | tf_op jit(solution)/shard_map/ppermute | solution.py:21
  260.3 6.4 %collective-permute-start.38 = (bf16[2,2,2,6144]{3,2,1,0:T(2,128)(2,1)S(1)}, bf16[2,2,2,6144]{3,2,1,0:T(2,128)(2,1)S(1)}, u32[]{:S(2)}, u32[]{:S(2)}) collective-permute-start(bf16[2,2,2,6144]{3,2,1,0:T(2,128)(2,1)S(1)} %broadcast_select_fusion.1), channel_id=1, source_target_pairs={{0,16},{4,20},{8,24},{12,28},{16,0},{20,4},{24,8},{28,12},{1,17},{... | collective-permute-start | bytes 294920 | tf_op jit(solution)/shard_map/ppermute | solution.py:21
  265.1 6.3 %collective-permute-start.41 = (f32[192,768]{1,0:T(8,128)}, f32[192,768]{1,0:T(8,128)S(1)}, u32[]{:S(2)}, u32[]{:S(2)}) collective-permute-start(f32[192,768]{1,0:T(8,128)} %get-tuple-element.238), channel_id=1, source_target_pairs={{0,1},{1,0},{2,3},{3,2},{4,5},{5,4},{6,7},{7,6},{8,9},{9,8},{10,11... | collective-permute-start | bytes 1769480 | tf_op jit(solution)/shard_map/ppermute | solution.py:21
  (49 other events, 277.8 us)
where the time goes:
time: 273 us
  Pallas kernels  142 us (52%)
  waiting for transfers between devices  48.6 us (18%)
  starting transfers between devices  32.5 us (12%)
  local copies, waits for them, and re-layouts  22.8 us (8%)
  matrix products  13.3 us (5%)
  other arithmetic  11.7 us (4%)
    ppermute x42, waiting for transfers between devices, swap(): lax.ppermute(block, axis, [(at, at ^ 1 << bit) for at in range(count)])  48.6 us
    pallas_call x2, Pallas kernels, backward_call(): pl.pallas_call(functools.partial(bwd_kernel, states), grid=(channels // w...  44.5 us
    pallas_call x1, Pallas kernels, forward_call(): pl.pallas_call(functools.partial(fwd_kernel, states), grid=(slots, channe...  34.8 us
    ppermute x42, starting transfers between devices, swap(): lax.ppermute(block, axis, [(at, at ^ 1 << bit) for at in range(count)])  32.5 us
    unnamed x114, local copies, waits for them, and re-layouts  15.6 us
    pallas_call x2, Pallas kernels, conv_back_call(): pl.pallas_call(conv_back_kernel, grid=(2,), in_specs=[scalars(), item, it...  12.7 us
    pallas_call x1, Pallas kernels, cond_call(): pl.pallas_call(cond_kernel, grid=(model // width,), in_specs=[whole(slots...  8.84 us
    pallas_call x1, Pallas kernels, gate_call(): pl.pallas_call(functools.partial(gate_kernel, chunk), grid_spec=pltpu.Pre...  8.02 us
  transfers between devices with their start and end apart: 42, of which 16 were waited for; matrix products, arithmetic and copies ran while one was open for 11% of the time, Pallas kernels for 52%

commit v1 on v0

--- a/solution.py
+++ b/solution.py
@@ -125,6 +125,18 @@
     )
 
 
+def gather_rest(values, axis, bits, *earlier):
+    codes = [code << bits[0] for code in range(1 << len(bits))]
+    got = [values] + [
+        lax.ppermute(values, axis, [(at, at ^ code) for at in range(lax.axis_size(axis))])
+        for code in codes[1:]
+    ]
+    got = after(got, *earlier)
+    mine = lax.axis_index(axis) >> bits[0]
+    stacked = jnp.stack(got)
+    return jnp.take(stacked, jnp.arange(len(codes)) ^ mine, axis=0)
+
+
 def bit_orders(axis):
     bits = lax.axis_size(axis).bit_length() - 1
     first = list(range(bits))
@@ -132,14 +144,6 @@
     if bits > 1:
         second[0], second[1] = 1, 0
     return first, second
-
-
-def shifted(padded, length, by, flip):
-    return jnp.where(
-        flip == 1,
-        padded[MARGIN + by : MARGIN + by + length, :],
-        padded[MARGIN - by : MARGIN - by + length, :],
-    )
 
 
 def kernel_params(megabytes):
@@ -326,23 +330,18 @@
     )(held(first), held(second), held(third), held(fourth))
 
 
-def join_kernel(*refs):
-    out_ref = refs[-1]
-    rows = refs[0].shape[0]
-    for at in range(len(refs) // 2):
-        total = refs[2 * at][...].astype(f32) + refs[2 * at + 1][...].astype(f32)
-        out_ref[at * rows : (at + 1) * rows, :] = total.astype(bf16)
-
-
-def join_call(pairs):
-    rows, cols = pairs[0][0].shape
+def join_kernel(keep_ref, there_ref, out_ref):
+    out_ref[...] = (keep_ref[...].astype(f32) + there_ref[...].astype(f32)).astype(bf16)
+
+
+def join_call(keep, there):
     return pl.pallas_call(
         join_kernel,
-        out_shape=shaped((len(pairs) * rows, cols), bf16),
-        compiler_params=kernel_params(10),
+        out_shape=shaped(keep.shape, bf16),
+        compiler_params=kernel_params(8),
         cost_estimate=LIGHT,
         name="join_sums",
-    )(*[part for pair in pairs for part in pair])
+    )(keep, there)
 
 
 def pack_kernel(side_ref, conv_ref, scan_ref, keep_ref, send_ref, total):
@@ -371,28 +370,30 @@
     )(side, conv, scan)
 
 
-def unpack_kernel(spots, side_ref, keep_ref, there_ref, xproj_ref, taps_ref, dtproj_ref, rates_ref, vec_ref, total):
+def unpack_kernel(
+    spots, side_ref, keep_ref, there_ref, xproj_ref, taps_ref, dtproj_ref, rates_ref, vec_ref, total
+):
     rows = keep_ref.shape[0]
     cols, tap_count, base, rank, states = spots
     side = side_ref[0]
     total[pl.ds(pl.multiple_of(side * rows, rows), rows), :] = keep_ref[...].astype(f32)
     total[pl.ds(pl.multiple_of((1 - side) * rows, rows), rows), :] = there_ref[...].astype(f32)
     dtproj_ref[...] = total[base : base + rank, :]
+    taps_ref[...] = total[cols : cols + tap_count, :]
+    first = base + rank
+    rates_ref[...] = total[first : first + states, :]
     vec_ref[...] = jnp.zeros_like(vec_ref)
     vec_ref[0:1, :] = total[cols + tap_count : cols + tap_count + 1, :]
-    vec_ref[1:3, :] = total[base + rank + states : base + rank + states + 2, :]
+    vec_ref[1:3, :] = total[first + states : first + states + 2, :]
     for at in range(0, total.shape[1], 128):
         here = slice(at, at + 128)
         xproj_ref[here, :] = jnp.transpose(total[0:cols, here])
-        turned = jnp.transpose(total[cols : cols + 128, here])
-        taps_ref[here, :] = turned[:, 0:tap_count]
-        first = base + rank - cols
-        rates_ref[here, :] = turned[:, first : first + states]
 
 
 def unpack_call(side, keep, there, cols, tap_count, base, rank, states):
     rows, channels = keep.shape
-    shapes = [(channels, cols), (channels, tap_count), (rank, channels), (channels, states), (8, channels)]
+    shapes = [(channels, cols), (tap_count, channels), (rank, channels), (states, channels)]
+    shapes += [(8, channels)]
     return pl.pallas_call(
         functools.partial(unpack_kernel, (cols, tap_count, base, rank, states)),
         grid=(1,),
@@ -406,27 +407,33 @@
     )(side, keep, there)
 
 
-def fold_kernel(slots, rows, me_ref, keep_ref, there_ref, mine_ref, sent_ref):
+def fold_kernel(rows, me_ref, *refs):
+    mine_ref, sent_ref = refs[-2:]
+    count = len(refs) // 2 - 1
+    items = refs[0].shape[0] // rows // 2
     chip = me_ref[0] >> 1
-    for slot in range(slots):
-        for which, out_ref in ((chip, mine_ref), (1 - chip, sent_ref)):
-            here = pl.ds(pl.multiple_of((2 * slot + which) * rows, rows), rows)
-            out_ref[slot] = (keep_ref[here, :] + there_ref[here, :].astype(f32)).astype(out_ref.dtype)
-
-
-def fold_call(me, keep, there, slots):
-    count, model = keep.shape
-    rows = count // slots // 2
-    return pl.pallas_call(
-        functools.partial(fold_kernel, slots, rows),
+    for at in range(count):
+        keep_ref, there_ref = refs[at], refs[count + at]
+        for item in range(items):
+            for which, out_ref in ((chip, mine_ref), (1 - chip, sent_ref)):
+                here = pl.ds(pl.multiple_of((2 * item + which) * rows, rows), rows)
+                total = keep_ref[here, :] + there_ref[here, :].astype(f32)
+                out_ref[at * items + item] = total.astype(out_ref.dtype)
+
+
+def fold_call(me, keeps, theres, rows):
+    count, model = keeps[0].shape
+    slots = len(keeps) * count // rows // 2
+    return pl.pallas_call(
+        functools.partial(fold_kernel, rows),
         grid=(1,),
-        in_specs=[scalars(), whole(count, model), whole(count, model)],
+        in_specs=[scalars()] + [whole(count, model)] * (2 * len(keeps)),
         out_specs=[whole(slots, rows, model)] * 2,
         out_shape=[shaped((slots, rows, model), f32), shaped((slots, rows, model), bf16)],
         compiler_params=kernel_params(14),
         cost_estimate=LIGHT,
         name="fold_rows",
-    )(me, keep, there)
+    )(me, *keeps, *theres)
 
 
 def rows_kernel(
@@ -507,22 +514,21 @@
     )(flip, values, weight)
 
 
-def proj_back_kernel(rows, flip_ref, x_ref, z_ref, weight_ref, there_ref, keep_ref, send_ref, x_s, z_s, mine_s):
+def proj_back_kernel(rows, slots, flip_ref, *refs):
+    x_refs = refs[:slots]
+    z_ref, weight_ref, there_ref, keep_ref, send_ref, x_s, z_s, mine_s = refs[slots:]
     core = flip_ref[0]
     half = there_ref.shape[1]
-
-    @pl.when(core == 0)
-    def _():
-        x_s[...] = x_ref[...]
-        z_s[...] = z_ref[...]
-        mine_s[...] = weight_ref[:, :half]
-
-    @pl.when(core == 1)
-    def _():
-        x_s[...] = z_ref[...]
-        z_s[...] = x_ref[...]
-        mine_s[...] = weight_ref[:, half:]
-
+    length = x_refs[0].shape[0]
+
+    def place(x_to, z_to, mine):
+        for slot in range(slots):
+            x_to[slot * length : (slot + 1) * length, :] = x_refs[slot][...]
+        z_to[...] = z_ref[...]
+        mine_s[...] = mine
+
+    pl.when(core == 0)(lambda: place(x_s, z_s, weight_ref[:, :half]))
+    pl.when(core == 1)(lambda: place(z_s, x_s, weight_ref[:, half:]))
     for parity, out_ref in ((core, keep_ref), (1 - core, send_ref)):
         total = contract_cols(pick_rows(x_s, parity, 2, rows), mine_s[...]) + contract_cols(
             pick_rows(z_s, parity, 2, rows), there_ref[...]
@@ -530,27 +536,27 @@
         out_ref[...] = total.astype(out_ref.dtype)
 
 
-def proj_back_call(flip, x, z, weight, there, rows, width):
-    count, depth = x.shape
+def proj_back_call(flip, xs, z, weight, there, rows, width):
+    length, depth = xs[0].shape
+    count = z.shape[0]
     model = there.shape[0]
-    out = [shaped((count // 2, model), f32), shaped((count // 2, model), bf16)]
-    return pl.pallas_call(
-        functools.partial(proj_back_kernel, rows),
+    return pl.pallas_call(
+        functools.partial(proj_back_kernel, rows, len(xs)),
         grid=(model // width,),
-        in_specs=[
-            scalars(),
-            whole(count, depth),
+        in_specs=[scalars()]
+        + [whole(length, depth)] * len(xs)
+        + [
             whole(count, depth),
             pl.BlockSpec((width, 2 * depth), lambda j: (j, 0)),
             pl.BlockSpec((width, depth), lambda j: (j, 0)),
         ],
         out_specs=[pl.BlockSpec((count // 2, width), lambda j: (0, j))] * 2,
-        out_shape=out,
+        out_shape=[shaped((count // 2, model), f32), shaped((count // 2, model), bf16)],
         scratch_shapes=[pltpu.VMEM((count, depth), bf16)] * 2 + [pltpu.VMEM((width, depth), bf16)],
         compiler_params=kernel_params(18),
         cost_estimate=LIGHT,
         name="proj_back",
-    )(flip, x, z, held(weight), held(there))
+    )(flip, *xs, z, held(weight), held(there))
 
 
 def cond_kernel(mod_ref, weight_ref, cond_ref, out_ref):
@@ -559,53 +565,63 @@
     out_ref[...] = contract_cols(mod_ref[...], weight_ref[...]) * sig * (1.0 + value * (1.0 - sig))
 
 
-def cond_call(mods, weight, cond):
+def cond_call(mods, weight, cond, start, count):
     slots, columns = mods.shape
-    model = weight.shape[0]
-    width = 256 if model % 256 == 0 else 128
+    width = 256 if count % 256 == 0 else 128
+    first = start // width
     return pl.pallas_call(
         cond_kernel,
-        grid=(model // width,),
+        grid=(count // width,),
         in_specs=[
             whole(slots, columns),
-            pl.BlockSpec((width, columns), lambda j: (j, 0)),
-            pl.BlockSpec((slots, width), lambda j: (0, j)),
+            pl.BlockSpec((width, columns), lambda j: (first + j, 0)),
+            pl.BlockSpec((slots, width), lambda j: (0, first + j)),
         ],
         out_specs=pl.BlockSpec((slots, width), lambda j: (0, j)),
-        out_shape=shaped((slots, model), f32),
+        out_shape=shaped((slots, count), f32),
         compiler_params=kernel_params(14),
         cost_estimate=LIGHT,
         name="cond_rows",
     )(mods, held(weight), cond)
 
 
+def tap_sum(pad, taps_ref, here, sign, length):
+    taps = taps_ref.shape[0] - 1
+    total = pad[MARGIN : MARGIN + length, :] * taps_ref[taps - 1 : taps, here]
+    for by in range(1, taps):
+        start = MARGIN - sign * by
+        total = total + pad[start : start + length, :] * taps_ref[taps - 1 - by : taps - by, here]
+    return total
+
+
 def conv_kernel(
-    flip_ref, own_ref, other_ref, mask_ref, taps_ref, xproj_ref, x_ref, z_ref, u_ref, dbl_ref, pad
+    flip_ref, own_ref, other_ref, mask_ref, taps_ref, xproj_ref, x_ref, z_ref, u_ref, slope_ref,
+    dbl_ref, pads
 ):
     step = pl.program_id(1)
     length, width = own_ref.shape
+    taps = taps_ref.shape[0] - 1
     flip = flip_ref[0]
 
-    @pl.when(flip == 0)
-    def _():
-        x_ref[...] = own_ref[...]
-        z_ref[...] = other_ref[...]
-
-    @pl.when(flip == 1)
-    def _():
-        x_ref[...] = other_ref[...]
-        z_ref[...] = own_ref[...]
-
-    pad[0:MARGIN, :] = jnp.zeros((MARGIN, width), f32)
-    pad[MARGIN + length :, :] = jnp.zeros((MARGIN, width), f32)
-    pad[MARGIN : MARGIN + length, :] = x_ref[...].astype(f32)
-    taps = taps_ref.shape[0] - 1
-    conv = taps_ref[taps : taps + 1, :] + pad[MARGIN : MARGIN + length, :] * taps_ref[taps - 1 : taps, :]
-    for by in range(1, taps):
-        conv = conv + shifted(pad, length, by, flip) * taps_ref[taps - 1 - by : taps - by, :]
-    u = (mask_ref[...] * (conv * jax.nn.sigmoid(conv))).astype(bf16)
-    u_ref[...] = u
-    part = matmul(u, xproj_ref[...])
+    def run(flipped):
+        x_from, z_from = (other_ref, own_ref) if flipped else (own_ref, other_ref)
+        x_ref[...] = x_from[...]
+        z_ref[...] = z_from[...]
+        mask = jnp.broadcast_to(mask_ref[...], (length, 128))
+        for tile in range(width // 128):
+            here = slice(tile * 128, (tile + 1) * 128)
+            pad = pads.at[tile]
+            pad[0:MARGIN, :] = jnp.zeros((MARGIN, 128), f32)
+            pad[MARGIN + length :, :] = jnp.zeros((MARGIN, 128), f32)
+            pad[MARGIN : MARGIN + length, :] = x_from[:, here].astype(f32)
+            conv = taps_ref[taps : taps + 1, here] + tap_sum(pad, taps_ref, here, -1 if flipped else 1, length)
+            sig = 0.5 + 0.5 * jnp.tanh(0.5 * conv)
+            u_ref[:, here] = (mask * (conv * sig)).astype(bf16)
+            slope_ref[:, here] = mask * (sig * (1.0 + conv * (1.0 - sig)))
+
+    pl.when(flip == 0)(lambda: run(False))
+    pl.when(flip == 1)(lambda: run(True))
+    part = matmul(u_ref[...], xproj_ref[...])
 
     @pl.when(step == 0)
     def _():
@@ -617,45 +633,50 @@
 
 
 def conv_back_kernel(
-    flip_ref, x_ref, u_ref, mask_ref, taps_ref, xproj_ref, us_ref, dg_ref, prev_ref, keep_ref, send_ref,
-    packed_ref, pad
+    flip_ref, x_ref, u_ref, slope_ref, taps_ref, xproj_ref, us_ref, dg_ref, prev_ref, keep_ref,
+    send_ref, packed_ref, grad_s, pads, grad_pads
 ):
     length, width = x_ref.shape
     flip = flip_ref[0]
-    pad[0:MARGIN, :] = jnp.zeros((MARGIN, width), f32)
-    pad[MARGIN + length :, :] = jnp.zeros((MARGIN, width), f32)
-    pad[MARGIN : MARGIN + length, :] = x_ref[...].astype(f32)
     taps = taps_ref.shape[0] - 1
-    conv = taps_ref[taps : taps + 1, :] + pad[MARGIN : MARGIN + length, :] * taps_ref[taps - 1 : taps, :]
-    for by in range(1, taps):
-        conv = conv + shifted(pad, length, by, flip) * taps_ref[taps - 1 - by : taps - by, :]
-    sig = jax.nn.sigmoid(conv)
     dg = dg_ref[...]
-    u_grad = us_ref[...] + contract_cols(dg, xproj_ref[...])
-    conv_grad = u_grad * mask_ref[...] * (sig * (1.0 + conv * (1.0 - sig)))
     cols = dg.shape[1]
-    packed_ref[0:cols, :] = prev_ref[0:cols, :] + matmul(jnp.transpose(dg.astype(f32)).astype(bf16), u_ref[...])
-    for by in range(taps):
-        moved = pad[MARGIN : MARGIN + length, :] if by == 0 else shifted(pad, length, by, flip)
-        row = cols + taps - 1 - by
-        packed_ref[row : row + 1, :] = prev_ref[row : row + 1, :] + jnp.sum(conv_grad * moved, axis=0, keepdims=True)
-    row = cols + taps
-    packed_ref[row : row + 1, :] = prev_ref[row : row + 1, :] + jnp.sum(conv_grad, axis=0, keepdims=True)
+    grad_s[...] = (us_ref[...] + contract_cols(dg, xproj_ref[...])) * slope_ref[...]
+    packed_ref[0:cols, :] = prev_ref[0:cols, :] + matmul(
+        jnp.transpose(dg.astype(f32)).astype(bf16), u_ref[...]
+    )
     rest = packed_ref.shape[0] - cols - taps - 1
     packed_ref[cols + taps + 1 :, :] = jnp.zeros((rest, width), f32)
-    pad[MARGIN : MARGIN + length, :] = conv_grad
-    grad = conv_grad * taps_ref[taps - 1 : taps, :]
-    for by in range(1, taps):
-        grad = grad + shifted(pad, length, by, 1 - flip) * taps_ref[taps - 1 - by : taps - by, :]
-    grad = grad.astype(bf16)
-
-    @pl.when(pl.program_id(0) == flip)
-    def _():
-        keep_ref[...] = grad
-
-    @pl.when(pl.program_id(0) != flip)
-    def _():
-        send_ref[...] = grad
+
+    def run(flipped, out_ref):
+        sign = -1 if flipped else 1
+        for tile in range(width // 128):
+            here = slice(tile * 128, (tile + 1) * 128)
+            pad, grad_pad = pads.at[tile], grad_pads.at[tile]
+            for ref in (pad, grad_pad):
+                ref[0:MARGIN, :] = jnp.zeros((MARGIN, 128), f32)
+                ref[MARGIN + length :, :] = jnp.zeros((MARGIN, 128), f32)
+            conv_grad = grad_s[:, here]
+            pad[MARGIN : MARGIN + length, :] = x_ref[:, here].astype(f32)
+            grad_pad[MARGIN : MARGIN + length, :] = conv_grad
+            for by in range(taps):
+                start = MARGIN - sign * by
+                row = cols + taps - 1 - by
+                packed_ref[row : row + 1, here] = prev_ref[row : row + 1, here] + jnp.sum(
+                    conv_grad * pad[start : start + length, :], axis=0, keepdims=True
+                )
+            row = cols + taps
+            packed_ref[row : row + 1, here] = prev_ref[row : row + 1, here] + jnp.sum(
+                conv_grad, axis=0, keepdims=True
+            )
+            out_ref[:, here] = tap_sum(grad_pad, taps_ref, here, -sign, length).astype(bf16)
+
+    for flipped in (False, True):
+        for block in range(2):
+            out_ref = keep_ref if block == int(flipped) else send_ref
+            pl.when((flip == int(flipped)) & (pl.program_id(0) == block))(
+                functools.partial(run, flipped, out_ref)
+            )
 
 
 def conv_call(flip, own, other, mask, taps, xproj, width):
@@ -674,23 +695,23 @@
             pl.BlockSpec((taps.shape[0], width), lambda i, j: (0, j)),
             pl.BlockSpec((width, cols), lambda i, j: (j, 0)),
         ],
-        out_specs=[block, block, block, pl.BlockSpec((length, cols), lambda i, j: (i, 0))],
+        out_specs=[block] * 4 + [pl.BlockSpec((length, cols), lambda i, j: (i, 0))],
         out_shape=[outer((slots * length, channels), bf16)] * 3
-        + [shaped((slots * length, cols), f32)],
-        scratch_shapes=[pltpu.VMEM((length + 2 * MARGIN, width), f32)],
-        compiler_params=kernel_params(12),
+        + [outer((slots * length, channels), f32), shaped((slots * length, cols), f32)],
+        scratch_shapes=[pltpu.VMEM((width // 128, length + 2 * MARGIN, 128), f32)],
+        compiler_params=kernel_params(16),
         cost_estimate=LIGHT,
         name="conv_forward",
     )(flip, own, other, mask, taps, xproj)
 
 
-def conv_back_call(flip, slot, x, u, mask, taps, xproj, us, dg, prev):
-    length = mask.shape[1]
+def conv_back_call(flip, slot, length, x, u, slope, taps, xproj, us, dg, prev):
     channels = x.shape[1]
     cols = xproj.shape[1]
     width = channels // 2
     rows = prev.shape[0]
     item = pl.BlockSpec((length, width), lambda j: (slot, j))
+    pads = pltpu.VMEM((width // 128, length + 2 * MARGIN, 128), f32)
     return pl.pallas_call(
         conv_back_kernel,
         grid=(2,),
@@ -698,7 +719,7 @@
             scalars(),
             item,
             item,
-            pl.BlockSpec((None, length, 1), lambda j: (slot, 0, 0)),
+            item,
             pl.BlockSpec((taps.shape[0], width), lambda j: (0, j)),
             pl.BlockSpec((width, cols), lambda j: (j, 0)),
             pl.BlockSpec((length, width), lambda j: (0, j)),
@@ -715,11 +736,11 @@
             shaped((length, width), bf16),
             shaped((rows, channels), f32),
         ],
-        scratch_shapes=[pltpu.VMEM((length + 2 * MARGIN, width), f32)],
-        compiler_params=kernel_params(16),
+        scratch_shapes=[pltpu.VMEM((length, width), f32), pads, pads],
+        compiler_params=kernel_params(18),
         cost_estimate=LIGHT,
         name="conv_backward",
-    )(flip, held(x), held(u), mask, taps, xproj, held(us), dg, prev)
+    )(flip, held(x), held(u), held(slope), taps, xproj, held(us), dg, prev)
 
 
 def spread(dbl_ref, first, b_wide, c_wide, rows_s, states):
@@ -1044,13 +1065,10 @@
         over = after(swap(block, "dir", 1), *earlier)
         return block, over, swap(block, "dir", 0), swap(over, "dir", 0)
 
-    in_send = lax.dynamic_slice_in_dim(in_weight, (1 - core) * half, half, 1)
-    in_there = swap(in_send, "dir", 0)
     cond_act = jax.nn.silu(cond.astype(f32)).astype(bf16)
-    modulation = matmul(after(cond_act, in_send), ada_weight) + ada_bias.astype(f32)[None, :]
+    modulation = matmul(cond_act, ada_weight) + ada_bias.astype(f32)[None, :]
     mods = modulation.reshape(slot_count, 3, model)
     token_blocks = gather_rows(tokens, modulation)
-    cot_blocks = gather_rows(cotangent, token_blocks[1])
     out_there = swap(out_weight, "dir", 0)
 
     taps = jnp.concatenate(
@@ -1064,14 +1082,17 @@
         z_side,
         token_blocks,
         mask_cols,
-        after(mods, cot_blocks[1]),
+        mods,
         in_weight,
         width,
         model // dps << z_bit,
     )
-    other = swap(own, "dir", 0)
-    x, z, u, part = conv_call(flip, own, other, mask_cols, taps, xproj_weight, half)
+    in_send = lax.dynamic_slice_in_dim(after(in_weight, left_mine), (1 - core) * half, half, 1)
+    in_there = swap(in_send, "dir", 0)
+    other = after(swap(own, "dir", 0), in_send)
+    x, z, u, slope, part = conv_call(flip, own, other, mask_cols, taps, xproj_weight, half)
     part_there = swap(part, "dir", 1)
+    cot_blocks = gather_rows(cotangent, part)
     branch_mine, branch_give, gg = gate_call(
         me_ref,
         out_side,
@@ -1095,17 +1116,28 @@
     gate_there = swap(gate_all, "dp", out_bit)
     z_there = swap(z_all, "dp", z_bit)
 
+    rows_keep, rows_give = branch_call(flip, gate_all, out_weight, shard_rows, width)
+    rows_there = swap(rows_give, "dir", 0)
+
     rest = lambda out: [bit for bit in first if bit != out]
     scan_rows = -(-(rank + states + 2) // 8) * 8
     packed = jnp.zeros((scan_rows, dt_bias.shape[0]), f32)
-    backs, dgs = [], []
-    u_tied = after(u, z_all, gate_all)
+    conv_rows = -(-(cols + tap_count + 1) // 8) * 8
+    conv_packed = jnp.zeros((conv_rows, dt_bias.shape[0]), f32)
+    length = mask_cols.shape[1]
+
+    def back_conv(slot, us, dg, conv_packed):
+        return conv_back_call(
+            flip, slot, length, x, u, slope, taps, xproj_weight, us, dg, conv_packed
+        )
+
+    x_sums, x_theres = [], []
+    u_tied = after(u, z_all, rows_give)
     for slot in slots:
         us, part_back, packed = backward_call(
             flip, slot, slot_count, dbl, dtproj_weight, vec, rates2, u_tied, *saved, packed, width
         )
         there = swap(part_back, "dir", 1)
-        backs.append((us, part_back, there))
         if slot == 0:
             z_part = Scatter(
                 contract_rows(left_mine, after(z_all, part_back))
@@ -1119,49 +1151,44 @@
                 "dp",
                 rest(out_bit),
             )
-            dgs.append((part_back + after(there, z_part.send, out_part.send)).astype(bf16))
-            u_tied, z_part.send, out_part.send = after((u, z_part.send, out_part.send), dgs[0])
-    end = backs[-1][1]
-    z_part.step(end)
-    out_part.step(end)
-
-    conv_rows = -(-(cols + tap_count + 1) // 8) * 8
-    conv_packed = jnp.zeros((conv_rows, dt_bias.shape[0]), f32)
-    pairs = []
-    for slot in slots:
-        us, part_back, there = backs[slot]
-        if slot == 0:
-            dg = after(dgs[0], z_part.send, out_part.send)
-        else:
-            dg = (part_back + after(there, pairs[-1][0])).astype(bf16)
-        keep, send, conv_packed = conv_back_call(
-            flip, slot, x, u, mask_cols, taps, xproj_weight, us, dg, conv_packed
-        )
-        pairs.append((keep, send))
-    z_part.step(pairs[-1][1])
-    pairs = [(keep, swap(after(send, z_part.values), "dir", 0)) for keep, send in pairs]
-    x_all = join_call(pairs)
-    x_there = swap(x_all, "dp", z_bit)
-    shared = SharedSum(pack_call(out_side, after(conv_packed, x_all), packed), "dp", second)
+        if slot + 1 < slot_count:
+            dg = (part_back + after(there, z_part.send, out_part.send)).astype(bf16)
+            keep, send, conv_packed = back_conv(slot, us, dg, conv_packed)
+            send_there = swap(send, "dir", 0)
+            if slot == 0:
+                rows_mine, branch_sent = fold_call(
+                    me_ref, [rows_keep], [after(rows_there, send)], shard_rows
+                )
+                branch_far = swap(branch_sent, "dir", 1)
+            x_sums.append(join_call(keep, after(send_there, branch_sent)))
+            x_theres.append(swap(x_sums[-1], "dp", z_bit))
+            u_tied, z_part.send, out_part.send = after((u, z_part.send, out_part.send), x_sums[-1])
+
+    z_part.step(part_back, branch_far, *x_theres)
+    out_part.step(part_back)
+    dg = (part_back + after(there, z_part.send, out_part.send)).astype(bf16)
+    keep, send, conv_packed = back_conv(slot_count - 1, us, dg, conv_packed)
+    shared = SharedSum(pack_call(out_side, conv_packed, packed), "dp", second)
+    send_there = swap(after(send, shared.send), "dir", 0)
+    x_sums.append(join_call(keep, send_there))
+    x_there = swap(x_sums[-1], "dp", z_bit)
     norm_keep, norm_give = proj_back_call(
-        flip, after(x_all, shared.send), z_all, in_weight, in_there, shard_rows, width
-    )
-    rows_keep, rows_give = branch_call(
-        flip, after(gate_all, norm_give), out_weight, shard_rows, width
-    )
-    out_part.step(rows_give)
-    shared.step(out_part.values)
-    x_part = contract_rows(left_mine, after(x_all, shared.send)) + contract_rows(
-        left_there, after(x_there, shared.send)
+        flip, x_sums, z_all, in_weight, in_there, shard_rows, width
+    )
+    z_part.step(norm_give)
+    out_part.step(norm_give)
+    shared.step(z_part.values, out_part.values)
+    x_theres.append(after(x_there, shared.send))
+    norm_there = swap(norm_give, "dir", 0)
+    norm_mine, norm_sent = fold_call(
+        me_ref, [norm_keep], [after(norm_there, x_theres[-1])], shard_rows
+    )
+    norm_far = swap(norm_sent, "dir", 1)
+    x_part = contract_rows(left_mine, jnp.concatenate(after(x_sums, norm_sent), 0)) + contract_rows(
+        left_there, jnp.concatenate(after(x_theres, norm_sent), 0)
     )
     x_part = Scatter(x_part, "dp", rest(z_bit))
-    norm_there = swap(after(norm_give, x_part.send), "dir", 0)
-    rows_there = swap(after(rows_give, x_part.send), "dir", 0)
-    norm_mine, norm_sent = fold_call(me_ref, norm_keep, norm_there, slot_count)
-    norm_far = swap(norm_sent, "dir", 1)
-    rows_mine, branch_sent = fold_call(me_ref, rows_keep, after(rows_there, norm_sent), slot_count)
-    branch_far = swap(branch_sent, "dir", 1)
-    shared.step(branch_sent)
+    shared.step(x_part.send)
 
     mixed, token_grads, mod_part = rows_call(
         tokens,
@@ -1169,7 +1196,7 @@
         local_mask,
         mods,
         rows_mine,
-        after(branch_far, shared.send),
+        branch_far,
         norm_mine,
         after(norm_far, shared.send),
     )
@@ -1181,16 +1208,17 @@
     shared.step(mod_pair)
     mod_total = mod_pair + after(mod_far, shared.send)
     mod_low = mod_total.astype(bf16).reshape(slot_count, 3 * model)
-    cond_grad = cond_call(mod_low, ada_weight, cond)
+    half_model = model // 2
+    cond_low = cond_call(mod_low, ada_weight, cond, 0, half_model)
     have = []
-    sides = jnp.concatenate([mod_low, after(cond_act, end)], 1)
-    sides = gather_bit(sides, "dp", first[0], have, cond_grad)
+    sides = jnp.concatenate([mod_low, cond_act], 1)
+    sides = gather_bit(sides, "dp", first[0], have, cond_low)
     while len(shared.plan) > 1:
         shared.step(sides)
     keep, there = shared.last(sides)
-    for bit in first[1:-1]:
-        sides = gather_bit(sides, "dp", bit, have)
-    sides = gather_bit(sides, "dp", first[-1], have)
+    cond_high = cond_call(after(mod_low, sides), ada_weight, cond, half_model, half_model)
+    cond_grad = jnp.concatenate([cond_low, cond_high], 1)
+    sides = gather_rest(sides, "dp", first[1:], cond_high)
     sides = sides.reshape(dps * slot_count, -1)
     total_columns = ada_weight.shape[1]
     columns = total_columns // dirs
@@ -1225,12 +1253,12 @@
         ada_sum,
         bias_sum,
         in_sum,
-        kernel_sum,
+        jnp.transpose(kernel_sum),
         vec_sum[0],
         xproj_sum,
         dtproj_sum,
         vec_sum[1],
-        rate_sum,
+        jnp.transpose(rate_sum),
         vec_sum[2],
         out_sum,
     )

time: 273 us -> 249 us (0.912)
  waiting for transfers between devices: 48.6 us -> 31.7 us
  starting transfers between devices: 32.5 us -> 39.8 us
  Pallas kernels: 142 us -> 135 us
  local copies, waits for them, and re-layouts: 22.8 us -> 15.8 us
    ppermute x42 -> x41, waiting for transfers between devices: 48.6 us -> 31.7 us  [swap(): lax.ppermute(block, axis, [(at, at ^ 1 << bit) for at in range(count)])]
    unnamed x114 -> x57, local copies, waits for them, and re-layouts: 15.6 us -> 8.24 us
    pallas_call x2, Pallas kernels: 12.7 us -> 8.03 us  [conv_back_call(): pl.pallas_call(conv_back_kernel, grid=(2,), in_specs=[scalars(), item, it...]
    ppermute x0 -> x3, starting transfers between devices: none -> 4.44 us  [gather_rest(): lax.ppermute(values, axis, [(at, at ^ code) for at in range(lax.axis_size...]
    pallas_call x5 -> x7, Pallas kernels: 18.6 us -> 15.6 us  [the longest x2 9.5 us: cond_call(): pl.pallas_call(cond_kernel, grid=(count // width,), in_specs=[whole(slots...]
    ppermute x42 -> x41, starting transfers between devices: 32.5 us -> 35.4 us  [swap(): lax.ppermute(block, axis, [(at, at ^ 1 << bit) for at in range(count)])]
  transfers between devices with their start and end apart: 42 -> 44, of which waited for: 16 -> 13; matrix products, arithmetic and copies ran while one was open for 11% -> 12% of each run, Pallas kernels for 52% -> 53%
where the time goes in v1:
time: 249 us
  Pallas kernels  135 us (54%)
  starting transfers between devices  39.8 us (16%)
  waiting for transfers between devices  31.7 us (13%)
  local copies, waits for them, and re-layouts  15.8 us (6%)
  matrix products  13.3 us (5%)
  other arithmetic  10.9 us (4%)
    pallas_call x2, Pallas kernels, backward_call(): pl.pallas_call(functools.partial(bwd_kernel, states), grid=(channels // w...  44.7 us
    ppermute x41, starting transfers between devices, swap(): lax.ppermute(block, axis, [(at, at ^ 1 << bit) for at in range(count)])  35.4 us
    pallas_call x1, Pallas kernels, forward_call(): pl.pallas_call(functools.partial(fwd_kernel, states), grid=(slots, channe...  34.8 us
    ppermute x41, waiting for transfers between devices, swap(): lax.ppermute(block, axis, [(at, at ^ 1 << bit) for at in range(count)])  31.7 us
    pallas_call x2, Pallas kernels, cond_call(): pl.pallas_call(cond_kernel, grid=(count // width,), in_specs=[whole(slots...  9.5 us
    unnamed x57, local copies, waits for them, and re-layouts  8.24 us
    pallas_call x1, Pallas kernels, gate_call(): pl.pallas_call(functools.partial(gate_kernel, chunk), grid_spec=pltpu.Pre...  8.05 us
    pallas_call x2, Pallas kernels, conv_back_call(): pl.pallas_call(conv_back_kernel, grid=(2,), in_specs=[scalars(), item, it...  8.03 us
  transfers between devices with their start and end apart: 44, of which 13 were waited for; matrix products, arithmetic and copies ran while one was open for 12% of the time, Pallas kernels for 53%

profile of v1, /device:TPU:0, one launch (start us, length us, event | category | flops | bytes accessed | tf_op | source)
XLA Modules:
  0.0 248.7 jit_solution(6557690181015929759)
XLA Ops:
  0.6 3.0 %collective-permute-start = (bf16[2,64,1536]{2,1,0:T(8,128)(2,1)}, bf16[2,64,1536]{2,1,0:T(8,128)(2,1)S(1)}, u32[]{:S(2)}, u32[]{:S(2)}) collective-permute-start(bf16[2,64,1536]{2,1,0:T(8,128)(2,1)} %tokens_ref.1), channel_id=1, source_target_pairs={{0,2},{1,3},{2,0},{3,1},{4,6},{5,7},{6,4},{7,5},{8,10},{9,11},{10,... | collective-permute-start | bytes 1179656 | tf_op jit(solution)/shard_map/ppermute | solution.py:21
  4.4 7.1 %convolution_add_fusion = f32[2,4608]{1,0:T(2,128)S(1)} fusion(bf16[1536,4608]{1,0:T(8,128)(2,1)} %weight_ref.7, f32[4608]{0:T(1024)S(1)} %convert_element_type.112, bf16[2,1536]{1,0:T(2,128)(2,1)} %cond_ref.3), kind=kOutput, calls=%fused_computation.1 | convolution fusion | flops 28339200 | bytes 14217216 | tf_op jit(solution)/shard_map/dot_general | solution.py:37
  11.5 1.5 collective-permute-done.over_ref
  14.9 7.7 %norm_project.1 = (bf16[512,768]{1,0:T(8,128)(2,1)S(1)}, bf16[512,768]{1,0:T(8,128)(2,1)S(1)}, bf16[512,1536]{1,0:T(8,128)(2,1)}) custom-call(s32[1]{0:T(128)} %bitcast.2.me_ref, s32[1]{0:T(128)} %bitcast.4.side_ref, bf16[2,64,1536]{2,1,0:T(8,128)(2,1)S(1)} %copy-done.5, bf16[2,64,1536]{2,1,0:T(8,128)(2,1)S(1)} %collective-permute-done.over_ref, ...), custom_call_target="tpu_custom_call" | custom-call | flops 1000 | bytes 1000 | tf_op jit(solution)/shard_map/norm_project/pallas_call | solution.py:220
  24.5 1.8 collective-permute-start.5
  26.4 3.3 %constant_dynamic-slice_fusion = bf16[1536,768]{1,0:T(8,128)(2,1)} fusion(bf16[1536,1536]{1,0:T(8,128)(2,1)} %refs_3_.1, s32[]{:T(128)S(6)} %select_n.105), kind=kLoop, calls=%fused_computation.63 | loop fusion | bytes 4718596 | tf_op jit(solution)/shard_map/dynamic_slice | solution.py:1090
  29.7 7.4 %conv_forward.1 = (bf16[512,1536]{1,0:T(8,128)(2,1)}, bf16[512,1536]{1,0:T(8,128)(2,1)}, bf16[512,1536]{1,0:T(8,128)(2,1)}, f32[512,1536]{1,0:T(8,128)}, f32[512,128]{1,0:T(8,128)}) custom-call(s32[1]{0:T(128)} %bitcast.3.flip_ref, bf16[512,1536]{1,0:T(8,128)(2,1)} %get-tuple-element.113.own_ref, bf16[512,1536]{1,0:T(8,128)(2,1)} %collective-permute-done.3.other_ref, ...), custom_call_target="tpu_custom_call" | custom-call | flops 1000 | bytes 1000 | tf_op jit(solution)/shard_map/conv_forward/pallas_call | solution.py:687
  38.4 1.7 collective-permute-start.9
  40.1 8.1 %gate_project.1 = (bf16[512,768]{1,0:T(8,128)(2,1)S(1)}, bf16[512,768]{1,0:T(8,128)(2,1)S(1)}, bf16[512,1536]{1,0:T(8,128)(2,1)}) custom-call(s32[1]{0:T(128)} %bitcast.2.me_ref, s32[1]{0:T(128)} %bitcast.7.side_ref, bf16[2,64,1536]{2,1,0:T(8,128)(2,1)} %cot_ref.1, bf16[2,64,1536]{2,1,0:T(8,128)(2,1)} %collective-permute-done.5.over_ref, ...), custom_call_target="tpu_custom_call" | custom-call | flops 1000 | bytes 1000 | tf_op jit(solution)/shard_map/gate_project/pallas_call | solution.py:283
  48.2 1.1 add.135.dbl_ref
  49.2 1.6 collective-permute-start.10
  50.9 34.8 %scan_forward.1 = (bf16[512,768]{1,0:T(8,128)(2,1)}, bf16[512,768]{1,0:T(8,128)(2,1)}, bf16[512,768]{1,0:T(8,128)(2,1)}, bf16[512,768]{1,0:T(8,128)(2,1)}, f32[5...) custom-call(s32[1]{0:T(128)} %bitcast.3.flip_ref, ...), custom_call_target="tpu_custom_call" | custom-call | flops 32000000000 | bytes 40000000 | tf_op jit(solution)/shard_map/scan_forward/pallas_call | solution.py:956
  88.0 3.1 %collective-permute-done.11.second_ref = bf16[512,768]{1,0:T(8,128)(2,1)S(1)} collective-permute-done((bf16[512,768]{1,0:T(8,128)(2,1)}, bf16[512,768]{1,0:T(8,128)(2,1)S(1)}, u32[]{:S(2)}, u32[]{:S(2)}) %collective-permute-start.11) | collective-permute-done | bytes 786464 | tf_op jit(solution)/shard_map/ppermute | solution.py:21
  92.0 2.2 pair_sums.1
  94.6 2.0 branch_rows.1
  97.2 1.1 collective-permute-start.15
  98.3 22.5 %scan_backward.2 = (f32[256,1536]{1,0:T(8,128)}, f32[256,128]{1,0:T(8,128)S(1)}, f32[120,1536]{1,0:T(8,128)S(1)}) custom-call(s32[1]{0:T(128)} %bitcast.3.flip_ref, f32[512,128]{1,0:T(8,128)S(1)} %add.135.dbl_ref, bf16[96,1536]{1,0:T(8,128)(2,1)S(1)} %copy-done.11, f32[2,1536]{1,0:T(2,128)S(1)} %pad_maximum_fusion.2.vec_ref, f32[16,1536]{1,0:T(8,128)S(1)} %copy-done.7, ...), custom_call_target="tpu_custom_call" | custom-call | flops 22000001024 | bytes 20000000 | tf_op jit(solution)/shard_map/scan_backward/pallas_call | solution.py:989
  120.8 1.5 collective-permute-start.14
  126.2 4.0 %conv_backward.2 = (bf16[256,768]{1,0:T(8,128)(2,1)S(1)}, bf16[256,768]{1,0:T(8,128)(2,1)S(1)}, f32[136,1536]{1,0:T(8,128)S(1)}) custom-call(s32[1]{0:T(128)} %bitcast.3.flip_ref, bf16[512,1536]{1,0:T(8,128)(2,1)} %get-tuple-element.135.x_ref, bf16[512,1536]{1,0:T(8,128)(2,1)} %get-tuple-element.157.u_ref, f32[512,1536]{1,0:T(8,128)} %get-tuple-element.136.slope_ref, ...), custom_call_target="tpu_custom_call" | custom-call | flops 1000 | bytes 1000 | tf_op jit(solution)/shard_map/conv_backward/pallas_call | solution.py:715
  131.0 1.3 collective-permute-start.17
  133.4 1.1 collective-permute-start.22
  134.5 1.6 collective-permute-start.20
  136.1 22.3 %scan_backward.3 = (f32[256,1536]{1,0:T(8,128)}, f32[256,128]{1,0:T(8,128)S(1)}, f32[120,1536]{1,0:T(8,128)S(1)}) custom-call(s32[1]{0:T(128)} %bitcast.3.flip_ref, f32[512,128]{1,0:T(8,128)S(1)} %add.135.dbl_ref, bf16[96,1536]{1,0:T(8,128)(2,1)S(1)} %copy-done.11, f32[2,1536]{1,0:T(2,128)S(1)} %pad_maximum_fusion.2.vec_ref, f32[16,1536]{1,0:T(8,128)S(1)} %copy-done.8, ...), custom_call_target="tpu_custom_call" | custom-call | flops 22000001024 | bytes 20000000 | tf_op jit(solution)/shard_map/scan_backward/pallas_call | solution.py:989
  159.4 2.6 %collective-permute-start.29 = (bf16[192,768]{1,0:T(8,128)(2,1)S(1)}, bf16[192,768]{1,0:T(8,128)(2,1)S(1)}, u32[]{:S(2)}, u32[]{:S(2)}) collective-permute-start(bf16[192,768]{1,0:T(8,128)(2,1)S(1)} %fusion.13), channel_id=1, source_target_pairs={{0,16},{4,20},{8,24},{12,28},{16,0},{20,4},{24,8},{28,12},{1,17},{... | collective-permute-start | bytes 884744 | tf_op jit(solution)/shard_map/ppermute | solution.py:21
  163.3 4.1 %conv_backward.3 = (bf16[256,768]{1,0:T(8,128)(2,1)S(1)}, bf16[256,768]{1,0:T(8,128)(2,1)S(1)}, f32[136,1536]{1,0:T(8,128)S(1)}) custom-call(s32[1]{0:T(128)} %bitcast.3.flip_ref, bf16[512,1536]{1,0:T(8,128)(2,1)} %get-tuple-element.135.x_ref, bf16[512,1536]{1,0:T(8,128)(2,1)} %get-tuple-element.157.u_ref, f32[512,1536]{1,0:T(8,128)} %get-tuple-element.136.slope_ref, ...), custom_call_target="tpu_custom_call" | custom-call | flops 1000 | bytes 1000 | tf_op jit(solution)/shard_map/conv_backward/pallas_call | solution.py:715
  170.5 1.4 copy-done.18
  171.9 5.6 %proj_back.1 = (f32[256,1536]{1,0:T(8,128)S(1)}, bf16[256,1536]{1,0:T(8,128)(2,1)S(1)}) custom-call(s32[1]{0:T(128)} %bitcast.3.flip_ref, bf16[256,768]{1,0:T(8,128)(2,1)S(1)} %join_sums.2.refs_0_, bf16[256,768]{1,0:T(8,128)(2,1)S(1)} %join_sums.3.refs_1_, bf16[512,768]{1,0:T(8,128)(2,1)S(1)} %get-tuple-element.145.refs_2_, bf16[1536,1536]{1,0:T(8,128)(2,1)} %refs_3_.1, ...), custom_call_target="tpu_custom_call" | custom-call | flops 1000 | bytes 1000 | tf_op jit(solution)/shard_map/proj_back/pallas_call | solution.py:543
  177.6 3.4 %collective-permute-done.29 = bf16[192,768]{1,0:T(8,128)(2,1)S(1)} collective-permute-done((bf16[192,768]{1,0:T(8,128)(2,1)S(1)}, bf16[192,768]{1,0:T(8,128)(2,1)S(1)}, u32[]{:S(2)}, u32[]{:S(2)}) %collective-permute-start.29) | collective-permute-done | bytes 294944 | tf_op jit(solution)/shard_map/ppermute | solution.py:21
  181.0 6.2 %collective-permute-done.28 = bf16[192,768]{1,0:T(8,128)(2,1)S(1)} collective-permute-done((bf16[192,768]{1,0:T(8,128)(2,1)S(1)}, bf16[192,768]{1,0:T(8,128)(2,1)S(1)}, u32[]{:S(2)}, u32[]{:S(2)}) %collective-permute-start.28) | collective-permute-done | bytes 294944 | tf_op jit(solution)/shard_map/ppermute | solution.py:21
  189.0 2.9 %collective-permute-done.27 = bf16[128,1536]{1,0:T(8,128)(2,1)S(1)} collective-permute-done((bf16[128,1536]{1,0:T(8,128)(2,1)S(1)}, bf16[128,1536]{1,0:T(8,128)(2,1)S(1)}, u32[]{:S(2)}, u32[]{:S(2)}) %collective-permute-start.27) | collective-permute-done | bytes 393248 | tf_op jit(solution)/shard_map/ppermute | solution.py:21
  195.7 1.4 copy-done.14
  198.8 1.9 collective-permute-start.34
  201.0 2.2 collective-permute-done.30.norm_far_ref
  203.2 3.0 %owned_rows.1 = (f32[2,64,1536]{2,1,0:T(8,128)}, f32[2,64,1536]{2,1,0:T(8,128)}, f32[2,3,1536]{2,1,0:T(4,128)S(1)}) custom-call(bf16[2,64,1536]{2,1,0:T(8,128)(2,1)S(1)} %copy-done.5, bf16[2,64,1536]{2,1,0:T(8,128)(2,1)} %cot_ref.1, f32[2,64,1]{2,1,0:T(8,128)S(1)} %copy.40.mask_ref, f32[2,3,1536]{2,1,0:T(4,128)S(1)} %reshape.91.mod_ref, ...), custom_call_target="tpu_custom_call" | custom-call | flops 1000 | bytes 1000 | tf_op jit(solution)/shard_map/owned_rows/pallas_call | solution.py:467
  206.2 8.0 %collective-permute-done.34 = bf16[64,1536]{1,0:T(8,128)(2,1)} collective-permute-done((bf16[64,1536]{1,0:T(8,128)(2,1)}, bf16[64,1536]{1,0:T(8,128)(2,1)}, u32[]{:S(2)}, u32[]{:S(2)}) %collective-permute-start.34) | collective-permute-done | bytes 196640 | tf_op jit(solution)/shard_map/ppermute | solution.py:21
  214.2 1.1 add_convert_fusion
  215.3 1.1 collective-permute-start.36
  216.4 1.2 bitcast_add_fusion
  218.4 3.4 %collective-permute-start.41 = (bf16[192,768]{1,0:T(8,128)(2,1)}, bf16[192,768]{1,0:T(8,128)(2,1)S(1)}, u32[]{:S(2)}, u32[]{:S(2)}) collective-permute-start(bf16[192,768]{1,0:T(8,128)(2,1)} %fusion.14), channel_id=1, source_target_pairs={{0,16},{4,20},{8,24},{12,28},{16,0},{20,4},{24,8},{28,12},{1,17},{... | collective-permute-start | bytes 884744 | tf_op jit(solution)/shard_map/ppermute | solution.py:21
  221.8 1.2 collective-permute-start.35
  223.7 2.3 collective-permute-done.35
  227.0 4.8 %cond_rows.2 = f32[2,768]{1,0:T(2,128)S(1)} custom-call(bf16[2,4608]{1,0:T(2,128)(2,1)S(1)} %bitcast.84, bf16[1536,4608]{1,0:T(8,128)(2,1)} %weight_ref.7, bf16[2,1536]{1,0:T(2,128)(2,1)S(1)} %copy-done.6), custom_call_target="tpu_custom_call" | custom-call | flops 1000 | bytes 1000 | tf_op jit(solution)/shard_map/cond_rows/pallas_call | solution.py:572
  232.0 2.0 collective-permute-start.39
  234.0 2.3 collective-permute-start.40
  236.4 4.7 %cond_rows.3 = f32[2,768]{1,0:T(2,128)S(1)} custom-call(bf16[2,4608]{1,0:T(2,128)(2,1)S(1)} %bitcast.85, bf16[1536,4608]{1,0:T(8,128)(2,1)} %weight_ref.7, bf16[2,1536]{1,0:T(2,128)(2,1)S(1)} %copy-done.6), custom_call_target="tpu_custom_call" | custom-call | flops 1000 | bytes 1000 | tf_op jit(solution)/shard_map/cond_rows/pallas_call | solution.py:572
  243.2 1.4 unpack_sums.1
  245.6 1.3 fusion.15
  247.5 1.1 maximum_select_fusion
  (180 shorter events, 34.5 us)
Async XLA Ops:
  0.6 12.4 %collective-permute-start = (bf16[2,64,1536]{2,1,0:T(8,128)(2,1)}, bf16[2,64,1536]{2,1,0:T(8,128)(2,1)S(1)}, u32[]{:S(2)}, u32[]{:S(2)}) collective-permute-start(bf16[2,64,1536]{2,1,0:T(8,128)(2,1)} %tokens_ref.1), channel_id=1, source_target_pairs={{0,2},{1,3},{2,0},{3,1},{4,6},{5,7},{6,4},{7,5},{8,10},{9,11},{10,... | collective-permute-start | bytes 1179656 | tf_op jit(solution)/shard_map/ppermute | solution.py:21
  3.7 10.8 %collective-permute-start.1 = (bf16[2,64,1536]{2,1,0:T(8,128)(2,1)}, bf16[2,64,1536]{2,1,0:T(8,128)(2,1)}, u32[]{:S(2)}, u32[]{:S(2)}) collective-permute-start(bf16[2,64,1536]{2,1,0:T(8,128)(2,1)} %tokens_ref.1), channel_id=1, source_target_pairs={{0,1},{1,0},{2,3},{3,2},{4,5},{5,4},{6,7},{7,6},{8,9},{9,8},{10,11... | collective-permute-start | bytes 1179656 | tf_op jit(solution)/shard_map/ppermute | solution.py:21
  13.0 1.9 collective-permute-start.2
  13.0 27.1 %collective-permute-start.8 = (bf16[768,1536]{1,0:T(8,128)(2,1)S(1)}, bf16[768,1536]{1,0:T(8,128)(2,1)}, u32[]{:S(2)}, u32[]{:S(2)}) collective-permute-start(bf16[768,1536]{1,0:T(8,128)(2,1)S(1)} %copy-done), channel_id=1, source_target_pairs={{0,1},{1,0},{2,3},{3,2},{4,5},{5,4},{6,7},{7,6},{8,9},{9,8},{10,11... | collective-permute-start | bytes 7077896 | tf_op jit(solution)/shard_map/ppermute | solution.py:21
  14.9 11.4 %copy-start.27 = (bf16[1536]{0:T(1024)(128)(2,1)S(1)}, bf16[1536]{0:T(1024)(128)(2,1)}, u32[]{:S(2)}) copy-start(bf16[1536]{0:T(1024)(128)(2,1)} %param.24) | copy-start | bytes 9220
  14.9 11.4 %copy-start.23 = (bf16[1536,4]{0,1:T(4,128)(2,1)S(1)}, bf16[1536,4]{0,1:T(4,128)(2,1)}, u32[]{:S(2)}) copy-start(bf16[1536,4]{0,1:T(4,128)(2,1)} %param.23) | copy-start | bytes 36868
  24.3 5.4 %collective-permute-start.3 = (bf16[512,1536]{1,0:T(8,128)(2,1)}, bf16[512,1536]{1,0:T(8,128)(2,1)}, u32[]{:S(2)}, u32[]{:S(2)}) collective-permute-start(bf16[512,1536]{1,0:T(8,128)(2,1)} %get-tuple-element.113.own_ref), channel_id=1, source_target_pairs={{0,1},{1,0},{2,3},{3,2},{4,5},{5,4},{6,7},{7,6},{8,9},{9,8},{10,11... | collective-permute-start | bytes 4718600 | tf_op jit(solution)/shard_map/ppermute | solution.py:21
  24.5 13.0 %collective-permute-start.5 = (bf16[2,64,1536]{2,1,0:T(8,128)(2,1)}, bf16[2,64,1536]{2,1,0:T(8,128)(2,1)}, u32[]{:S(2)}, u32[]{:S(2)}) collective-permute-start(bf16[2,64,1536]{2,1,0:T(8,128)(2,1)} %cot_ref.1), channel_id=1, source_target_pairs={{0,2},{1,3},{2,0},{3,1},{4,6},{5,7},{6,4},{7,5},{8,10},{9,11},{10,... | collective-permute-start | bytes 1179656 | tf_op jit(solution)/shard_map/ppermute | solution.py:21
  26.2 13.9 %collective-permute-start.6 = (bf16[2,64,1536]{2,1,0:T(8,128)(2,1)}, bf16[2,64,1536]{2,1,0:T(8,128)(2,1)}, u32[]{:S(2)}, u32[]{:S(2)}) collective-permute-start(bf16[2,64,1536]{2,1,0:T(8,128)(2,1)} %cot_ref.1), channel_id=1, source_target_pairs={{0,1},{1,0},{2,3},{3,2},{4,5},{5,4},{6,7},{7,6},{8,9},{9,8},{10,11... | collective-permute-start | bytes 1179656 | tf_op jit(solution)/shard_map/ppermute | solution.py:21
  37.1 11.1 %collective-permute-start.4 = (f32[512,128]{1,0:T(8,128)}, f32[512,128]{1,0:T(8,128)}, u32[]{:S(2)}, u32[]{:S(2)}) collective-permute-start(f32[512,128]{1,0:T(8,128)} %get-tuple-element.117), channel_id=1, source_target_pairs={{0,2},{1,3},{2,0},{3,1},{4,6},{5,7},{6,4},{7,5},{8,10},{9,11},{10,... | collective-permute-start | bytes 786440 | tf_op jit(solution)/shard_map/ppermute | solution.py:21
  37.4 2.7 %collective-permute-start.7 = (bf16[2,64,1536]{2,1,0:T(8,128)(2,1)}, bf16[2,64,1536]{2,1,0:T(8,128)(2,1)}, u32[]{:S(2)}, u32[]{:S(2)}) collective-permute-start(bf16[2,64,1536]{2,1,0:T(8,128)(2,1)} %collective-permute-done.5.over_ref), channel_id=1, source_target_pairs={{0,1},{1,0},{2,3},{3,2},{4,5},{5,4},{6,7},{7,6},{8,9},{9,8},{10,11... | collective-permute-start | bytes 1179656 | tf_op jit(solution)/shard_map/ppermute | solution.py:21
  38.4 47.3 %collective-permute-start.9 = (bf16[512,768]{1,0:T(8,128)(2,1)}, bf16[512,768]{1,0:T(8,128)(2,1)S(1)}, u32[]{:S(2)}, u32[]{:S(2)}) collective-permute-start(bf16[512,768]{1,0:T(8,128)(2,1)} %copy-done.9), channel_id=1, source_target_pairs={{0,4},{4,0},{8,12},{12,8},{16,20},{20,16},{24,28},{28,24},{1,5},{5... | collective-permute-start | bytes 2359304 | tf_op jit(solution)/shard_map/ppermute | solution.py:21
  49.2 36.5 %collective-permute-start.10 = (bf16[512,768]{1,0:T(8,128)(2,1)S(1)}, bf16[512,768]{1,0:T(8,128)(2,1)S(1)}, u32[]{:S(2)}, u32[]{:S(2)}) collective-permute-start(bf16[512,768]{1,0:T(8,128)(2,1)S(1)} %get-tuple-element.128), channel_id=1, source_target_pairs={{0,8},{4,12},{8,0},{12,4},{16,24},{20,28},{24,16},{28,20},{1,9},{5... | collective-permute-start | bytes 2359304 | tf_op jit(solution)/shard_map/ppermute | solution.py:21
  87.5 3.6 %collective-permute-start.11 = (bf16[512,768]{1,0:T(8,128)(2,1)}, bf16[512,768]{1,0:T(8,128)(2,1)S(1)}, u32[]{:S(2)}, u32[]{:S(2)}) collective-permute-start(bf16[512,768]{1,0:T(8,128)(2,1)} %get-tuple-element.129), channel_id=1, source_target_pairs={{0,1},{1,0},{2,3},{3,2},{4,5},{5,4},{6,7},{7,6},{8,9},{9,8},{10,11... | collective-permute-start | bytes 2359304 | tf_op jit(solution)/shard_map/ppermute | solution.py:21
  87.5 3.7 %collective-permute-start.12 = (bf16[512,768]{1,0:T(8,128)(2,1)}, bf16[512,768]{1,0:T(8,128)(2,1)}, u32[]{:S(2)}, u32[]{:S(2)}) collective-permute-start(bf16[512,768]{1,0:T(8,128)(2,1)} %get-tuple-element.131), channel_id=1, source_target_pairs={{0,1},{1,0},{2,3},{3,2},{4,5},{5,4},{6,7},{7,6},{8,9},{9,8},{10,11... | collective-permute-start | bytes 2359304 | tf_op jit(solution)/shard_map/ppermute | solution.py:21
  96.6 25.7 %collective-permute-start.16 = (bf16[512,768]{1,0:T(8,128)(2,1)S(1)}, bf16[512,768]{1,0:T(8,128)(2,1)S(1)}, u32[]{:S(2)}, u32[]{:S(2)}) collective-permute-start(bf16[512,768]{1,0:T(8,128)(2,1)S(1)} %get-tuple-element.148.values_ref), channel_id=1, source_target_pairs={{0,8},{4,12},{8,0},{12,4},{16,24},{20,28},{24,16},{28,20},{1,9},{5... | collective-permute-start | bytes 2359304 | tf_op jit(solution)/shard_map/ppermute | solution.py:21
  97.2 25.1 %collective-permute-start.15 = (bf16[512,768]{1,0:T(8,128)(2,1)S(1)}, bf16[512,768]{1,0:T(8,128)(2,1)S(1)}, u32[]{:S(2)}, u32[]{:S(2)}) collective-permute-start(bf16[512,768]{1,0:T(8,128)(2,1)S(1)} %get-tuple-element.145.refs_2_), channel_id=1, source_target_pairs={{0,4},{4,0},{8,12},{12,8},{16,20},{20,16},{24,28},{28,24},{1,5},{5... | collective-permute-start | bytes 2359304 | tf_op jit(solution)/shard_map/ppermute | solution.py:21
  98.3 24.0 %copy-start.13 = (bf16[512,768]{1,0:T(8,128)(2,1)S(1)}, bf16[512,768]{1,0:T(8,128)(2,1)}, u32[]{:S(2)}) copy-start(bf16[512,768]{1,0:T(8,128)(2,1)} %copy-done.12) | copy-start | bytes 2359300
  120.8 5.3 %collective-permute-start.14 = (f32[256,128]{1,0:T(8,128)S(1)}, f32[256,128]{1,0:T(8,128)S(1)}, u32[]{:S(2)}, u32[]{:S(2)}) collective-permute-start(f32[256,128]{1,0:T(8,128)S(1)} %get-tuple-element.144), channel_id=1, source_target_pairs={{0,2},{1,3},{2,0},{3,1},{4,6},{5,7},{6,4},{7,5},{8,10},{9,11},{10,... | collective-permute-start | bytes 393224 | tf_op jit(solution)/shard_map/ppermute | solution.py:21
  122.3 8.6 %collective-permute-start.13 = (bf16[256,1536]{1,0:T(8,128)(2,1)S(1)}, bf16[256,1536]{1,0:T(8,128)(2,1)S(1)}, u32[]{:S(2)}, u32[]{:S(2)}) collective-permute-start(bf16[256,1536]{1,0:T(8,128)(2,1)S(1)} %get-tuple-element.134), channel_id=1, source_target_pairs={{0,1},{1,0},{2,3},{3,2},{4,5},{5,4},{6,7},{7,6},{8,9},{9,8},{10,11... | collective-permute-start | bytes 2359304 | tf_op jit(solution)/shard_map/ppermute | solution.py:21
  130.2 2.1 collective-permute-start.18
  130.8 39.7 %collective-permute-start.24 = (bf16[1536,768]{1,0:T(8,128)(2,1)S(1)}, bf16[1536,768]{1,0:T(8,128)(2,1)S(1)}, u32[]{:S(2)}, u32[]{:S(2)}) collective-permute-start(bf16[1536,768]{1,0:T(8,128)(2,1)S(1)} %copy-done.16), channel_id=1, source_target_pairs={{0,1},{1,0},{2,3},{3,2},{4,5},{5,4},{6,7},{7,6},{8,9},{9,8},{10,11... | collective-permute-start | bytes 7077896 | tf_op jit(solution)/shard_map/ppermute | solution.py:21
  131.0 28.2 %collective-permute-start.17 = (bf16[2,64,1536]{2,1,0:T(8,128)(2,1)S(1)}, bf16[2,64,1536]{2,1,0:T(8,128)(2,1)S(1)}, u32[]{:S(2)}, u32[]{:S(2)}) collective-permute-start(bf16[2,64,1536]{2,1,0:T(8,128)(2,1)S(1)} %get-tuple-element.154), channel_id=1, source_target_pairs={{0,2},{1,3},{2,0},{3,1},{4,6},{5,7},{6,4},{7,5},{8,10},{9,11},{10,... | collective-permute-start | bytes 1179656 | tf_op jit(solution)/shard_map/ppermute | solution.py:21
  132.4 26.8 %collective-permute-start.21 = (bf16[256,768]{1,0:T(8,128)(2,1)S(1)}, bf16[256,768]{1,0:T(8,128)(2,1)S(1)}, u32[]{:S(2)}, u32[]{:S(2)}) collective-permute-start(bf16[256,768]{1,0:T(8,128)(2,1)S(1)} %join_sums.2.refs_0_), channel_id=1, source_target_pairs={{0,4},{4,0},{8,12},{12,8},{16,20},{20,16},{24,28},{28,24},{1,5},{5... | collective-permute-start | bytes 1179656 | tf_op jit(solution)/shard_map/ppermute | solution.py:21
  133.4 24.9 %collective-permute-start.22 = (bf16[2,192,768]{2,1,0:T(8,128)(2,1)S(1)}, bf16[2,192,768]{2,1,0:T(8,128)(2,1)S(1)}, u32[]{:S(2)}, u32[]{:S(2)}) collective-permute-start(bf16[2,192,768]{2,1,0:T(8,128)(2,1)S(1)} %get-tuple-element.163), channel_id=1, source_target_pairs={{0,4},{4,0},{8,12},{12,8},{16,20},{20,16},{24,28},{28,24},{1,5},{5... | collective-permute-start | bytes 1769480 | tf_op jit(solution)/shard_map/ppermute | solution.py:21
  134.5 24.7 %collective-permute-start.20 = (bf16[2,192,768]{2,1,0:T(8,128)(2,1)S(1)}, bf16[2,192,768]{2,1,0:T(8,128)(2,1)S(1)}, u32[]{:S(2)}, u32[]{:S(2)}) collective-permute-start(bf16[2,192,768]{2,1,0:T(8,128)(2,1)S(1)} %get-tuple-element.161), channel_id=1, source_target_pairs={{0,8},{4,12},{8,0},{12,4},{16,24},{20,28},{24,16},{28,20},{1,9},{5... | collective-permute-start | bytes 1769480 | tf_op jit(solution)/shard_map/ppermute | solution.py:21
  158.3 5.0 %collective-permute-start.19 = (f32[256,128]{1,0:T(8,128)S(1)}, f32[256,128]{1,0:T(8,128)S(1)}, u32[]{:S(2)}, u32[]{:S(2)}) collective-permute-start(f32[256,128]{1,0:T(8,128)S(1)} %get-tuple-element.160), channel_id=1, source_target_pairs={{0,2},{1,3},{2,0},{3,1},{4,6},{5,7},{6,4},{7,5},{8,10},{9,11},{10,... | collective-permute-start | bytes 393224 | tf_op jit(solution)/shard_map/ppermute | solution.py:21
  159.4 21.6 %collective-permute-start.29 = (bf16[192,768]{1,0:T(8,128)(2,1)S(1)}, bf16[192,768]{1,0:T(8,128)(2,1)S(1)}, u32[]{:S(2)}, u32[]{:S(2)}) collective-permute-start(bf16[192,768]{1,0:T(8,128)(2,1)S(1)} %fusion.13), channel_id=1, source_target_pairs={{0,16},{4,20},{8,24},{12,28},{16,0},{20,4},{24,8},{28,12},{1,17},{... | collective-permute-start | bytes 884744 | tf_op jit(solution)/shard_map/ppermute | solution.py:21
  162.2 25.1 %collective-permute-start.28 = (bf16[192,768]{1,0:T(8,128)(2,1)S(1)}, bf16[192,768]{1,0:T(8,128)(2,1)S(1)}, u32[]{:S(2)}, u32[]{:S(2)}) collective-permute-start(bf16[192,768]{1,0:T(8,128)(2,1)S(1)} %fusion.12), channel_id=1, source_target_pairs={{0,16},{4,20},{8,24},{12,28},{16,0},{20,4},{24,8},{28,12},{1,17},{... | collective-permute-start | bytes 884744 | tf_op jit(solution)/shard_map/ppermute | solution.py:21
  167.6 1.8 collective-permute-start.23
  168.1 23.7 %collective-permute-start.27 = (bf16[128,1536]{1,0:T(8,128)(2,1)S(1)}, bf16[128,1536]{1,0:T(8,128)(2,1)S(1)}, u32[]{:S(2)}, u32[]{:S(2)}) collective-permute-start(bf16[128,1536]{1,0:T(8,128)(2,1)S(1)} %get-tuple-element.171), channel_id=1, source_target_pairs={{0,8},{4,12},{8,0},{12,4},{16,24},{20,28},{24,16},{28,20},{1,9},{5... | collective-permute-start | bytes 1179656 | tf_op jit(solution)/shard_map/ppermute | solution.py:21
  169.5 23.5 %collective-permute-start.26 = (bf16[256,768]{1,0:T(8,128)(2,1)S(1)}, bf16[256,768]{1,0:T(8,128)(2,1)S(1)}, u32[]{:S(2)}, u32[]{:S(2)}) collective-permute-start(bf16[256,768]{1,0:T(8,128)(2,1)S(1)} %join_sums.3.refs_1_), channel_id=1, source_target_pairs={{0,4},{4,0},{8,12},{12,8},{16,20},{20,16},{24,28},{28,24},{1,5},{5... | collective-permute-start | bytes 1179656 | tf_op jit(solution)/shard_map/ppermute | solution.py:21
  177.5 15.5 %collective-permute-start.25 = (bf16[256,1536]{1,0:T(8,128)(2,1)S(1)}, bf16[256,1536]{1,0:T(8,128)(2,1)S(1)}, u32[]{:S(2)}, u32[]{:S(2)}) collective-permute-start(bf16[256,1536]{1,0:T(8,128)(2,1)S(1)} %get-tuple-element.174), channel_id=1, source_target_pairs={{0,1},{1,0},{2,3},{3,2},{4,5},{5,4},{6,7},{7,6},{8,9},{9,8},{10,11... | collective-permute-start | bytes 2359304 | tf_op jit(solution)/shard_map/ppermute | solution.py:21
  192.0 6.1 %collective-permute-start.31 = (bf16[64,1536]{1,0:T(8,128)(2,1)S(1)}, bf16[64,1536]{1,0:T(8,128)(2,1)S(1)}, u32[]{:S(2)}, u32[]{:S(2)}) collective-permute-start(bf16[64,1536]{1,0:T(8,128)(2,1)S(1)} %dynamic-slice_convert_fusion.3), channel_id=1, source_target_pairs={{0,4},{4,0},{8,12},{12,8},{16,20},{20,16},{24,28},{28,24},{1,5},{5... | collective-permute-start | bytes 589832 | tf_op jit(solution)/shard_map/ppermute | solution.py:21
  193.1 10.1 %collective-permute-start.30 = (bf16[2,64,1536]{2,1,0:T(8,128)(2,1)S(1)}, bf16[2,64,1536]{2,1,0:T(8,128)(2,1)S(1)}, u32[]{:S(2)}, u32[]{:S(2)}) collective-permute-start(bf16[2,64,1536]{2,1,0:T(8,128)(2,1)S(1)} %get-tuple-element.182), channel_id=1, source_target_pairs={{0,2},{1,3},{2,0},{3,1},{4,6},{5,7},{6,4},{7,5},{8,10},{9,11},{10,... | collective-permute-start | bytes 1179656 | tf_op jit(solution)/shard_map/ppermute | solution.py:21
  197.9 18.5 %collective-permute-start.33 = (bf16[2,192,768]{2,1,0:T(8,128)(2,1)}, bf16[2,192,768]{2,1,0:T(8,128)(2,1)}, u32[]{:S(2)}, u32[]{:S(2)}) collective-permute-start(bf16[2,192,768]{2,1,0:T(8,128)(2,1)} %fusion.9), channel_id=1, source_target_pairs={{0,8},{4,12},{8,0},{12,4},{16,24},{20,28},{24,16},{28,20},{1,9},{5... | collective-permute-start | bytes 1769480 | tf_op jit(solution)/shard_map/ppermute | solution.py:21
  198.8 15.4 %collective-permute-start.34 = (bf16[64,1536]{1,0:T(8,128)(2,1)}, bf16[64,1536]{1,0:T(8,128)(2,1)}, u32[]{:S(2)}, u32[]{:S(2)}) collective-permute-start(bf16[64,1536]{1,0:T(8,128)(2,1)} %add_convert_fusion.1), channel_id=1, source_target_pairs={{0,16},{4,20},{8,24},{12,28},{16,0},{20,4},{24,8},{28,12},{1,17},{... | collective-permute-start | bytes 589832 | tf_op jit(solution)/shard_map/ppermute | solution.py:21
  203.2 13.2 %copy-start.15 = (f32[768,768]{1,0:T(8,128)S(1)}, f32[768,768]{1,0:T(8,128)}, u32[]{:S(2)}) copy-start(f32[768,768]{1,0:T(8,128)} %copy-done.14) | copy-start | bytes 7077892
  206.2 15.5 %collective-permute-start.32 = (f32[2,3,1536]{2,1,0:T(4,128)S(1)}, f32[2,3,1536]{2,1,0:T(4,128)S(1)}, u32[]{:S(2)}, u32[]{:S(2)}) collective-permute-start(f32[2,3,1536]{2,1,0:T(4,128)S(1)} %get-tuple-element.191), channel_id=1, source_target_pairs={{0,1},{1,0},{2,3},{3,2},{4,5},{5,4},{6,7},{7,6},{8,9},{9,8},{10,11... | collective-permute-start | bytes 110600 | tf_op jit(solution)/shard_map/ppermute | solution.py:21
  215.3 7.7 %collective-permute-start.36 = (bf16[64,1536]{1,0:T(8,128)(2,1)S(1)}, bf16[64,1536]{1,0:T(8,128)(2,1)S(1)}, u32[]{:S(2)}, u32[]{:S(2)}) collective-permute-start(bf16[64,1536]{1,0:T(8,128)(2,1)S(1)} %add_convert_fusion), channel_id=1, source_target_pairs={{0,4},{4,0},{8,12},{12,8},{16,20},{20,16},{24,28},{28,24},{1,5},{5... | collective-permute-start | bytes 589832 | tf_op jit(solution)/shard_map/ppermute | solution.py:21
  218.4 26.3 %collective-permute-start.41 = (bf16[192,768]{1,0:T(8,128)(2,1)}, bf16[192,768]{1,0:T(8,128)(2,1)S(1)}, u32[]{:S(2)}, u32[]{:S(2)}) collective-permute-start(bf16[192,768]{1,0:T(8,128)(2,1)} %fusion.14), channel_id=1, source_target_pairs={{0,16},{4,20},{8,24},{12,28},{16,0},{20,4},{24,8},{28,12},{1,17},{... | collective-permute-start | bytes 884744 | tf_op jit(solution)/shard_map/ppermute | solution.py:21
  221.8 4.2 %collective-permute-start.35 = (f32[2,3,1536]{2,1,0:T(4,128)S(1)}, f32[2,3,1536]{2,1,0:T(4,128)S(1)}, u32[]{:S(2)}, u32[]{:S(2)}) collective-permute-start(f32[2,3,1536]{2,1,0:T(4,128)S(1)} %add.157), channel_id=1, source_target_pairs={{0,2},{1,3},{2,0},{3,1},{4,6},{5,7},{6,4},{7,5},{8,10},{9,11},{10,... | collective-permute-start | bytes 110600 | tf_op jit(solution)/shard_map/ppermute | solution.py:21
  223.1 20.1 %collective-permute-start.42 = (bf16[128,1536]{1,0:T(8,128)(2,1)S(1)}, bf16[128,1536]{1,0:T(8,128)(2,1)S(1)}, u32[]{:S(2)}, u32[]{:S(2)}) collective-permute-start(bf16[128,1536]{1,0:T(8,128)(2,1)S(1)} %maximum_select_fusion.1.keep_ref), channel_id=1, source_target_pairs={{0,8},{4,12},{8,0},{12,4},{16,24},{20,28},{24,16},{28,20},{1,9},{5... | collective-permute-start | bytes 1179656 | tf_op jit(solution)/shard_map/ppermute | solution.py:21
  226.0 5.8 %collective-permute-start.37 = (bf16[2,6144]{1,0:T(2,128)(2,1)S(1)}, bf16[2,6144]{1,0:T(2,128)(2,1)S(1)}, u32[]{:S(2)}, u32[]{:S(2)}) collective-permute-start(bf16[2,6144]{1,0:T(2,128)(2,1)S(1)} %pad_maximum_fusion.1), channel_id=1, source_target_pairs={{0,4},{4,0},{8,12},{12,8},{16,20},{20,16},{24,28},{28,24},{1,5},{5... | collective-permute-start | bytes 73736 | tf_op jit(solution)/shard_map/ppermute | solution.py:21
  231.9 9.8 %collective-permute-start.38 = (bf16[2,2,6144]{2,1,0:T(2,128)(2,1)S(1)}, bf16[2,2,6144]{2,1,0:T(2,128)(2,1)S(1)}, u32[]{:S(2)}, u32[]{:S(2)}) collective-permute-start(bf16[2,2,6144]{2,1,0:T(2,128)(2,1)S(1)} %broadcast_select_fusion.1), channel_id=1, source_target_pairs={{0,8},{4,12},{8,0},{12,4},{16,24},{20,28},{24,16},{28,20},{1,9},{5... | collective-permute-start | bytes 147464 | tf_op jit(solution)/shard_map/ppermute | solution.py:131
  232.0 9.8 %collective-permute-start.39 = (bf16[2,2,6144]{2,1,0:T(2,128)(2,1)S(1)}, bf16[2,2,6144]{2,1,0:T(2,128)(2,1)S(1)}, u32[]{:S(2)}, u32[]{:S(2)}) collective-permute-start(bf16[2,2,6144]{2,1,0:T(2,128)(2,1)S(1)} %broadcast_select_fusion.1), channel_id=1, source_target_pairs={{0,16},{4,20},{8,24},{12,28},{16,0},{20,4},{24,8},{28,12},{1,17},{... | collective-permute-start | bytes 147464 | tf_op jit(solution)/shard_map/ppermute | solution.py:131
  234.0 7.7 %collective-permute-start.40 = (bf16[2,2,6144]{2,1,0:T(2,128)(2,1)S(1)}, bf16[2,2,6144]{2,1,0:T(2,128)(2,1)S(1)}, u32[]{:S(2)}, u32[]{:S(2)}) collective-permute-start(bf16[2,2,6144]{2,1,0:T(2,128)(2,1)S(1)} %broadcast_select_fusion.1), channel_id=1, source_target_pairs={{0,24},{4,28},{8,16},{12,20},{16,8},{20,12},{24,0},{28,4},{1,25},{... | collective-permute-start | bytes 147464 | tf_op jit(solution)/shard_map/ppermute | solution.py:131
  244.7 2.8 %collective-permute-start.43 = (f32[192,768]{1,0:T(8,128)S(1)}, f32[192,768]{1,0:T(8,128)S(1)}, u32[]{:S(2)}, u32[]{:S(2)}) collective-permute-start(f32[192,768]{1,0:T(8,128)S(1)} %get-tuple-element.214), channel_id=1, source_target_pairs={{0,1},{1,0},{2,3},{3,2},{4,5},{5,4},{6,7},{7,6},{8,9},{9,8},{10,11... | collective-permute-start | bytes 1769480 | tf_op jit(solution)/shard_map/ppermute | solution.py:21
  (24 other events, 110.0 us)

commit v2 on v1

--- a/solution.py
+++ b/solution.py
@@ -307,7 +307,7 @@
         compiler_params=kernel_params(20),
         cost_estimate=LIGHT,
         name="gate_project",
-    )(me, side, *blocks, mask, mods, held(mine), held(theirs))
+    )(me, side, *blocks, mask, mods, mine, theirs)
 
 
 def pair_kernel(first_ref, second_ref, third_ref, fourth_ref, left_ref, right_ref):
@@ -697,7 +697,7 @@
         ],
         out_specs=[block] * 4 + [pl.BlockSpec((length, cols), lambda i, j: (i, 0))],
         out_shape=[outer((slots * length, channels), bf16)] * 3
-        + [outer((slots * length, channels), f32), shaped((slots * length, cols), f32)],
+        + [outer((slots * length, channels), f32), outer((slots * length, cols), f32)],
         scratch_shapes=[pltpu.VMEM((width // 128, length + 2 * MARGIN, 128), f32)],
         compiler_params=kernel_params(16),
         cost_estimate=LIGHT,
@@ -810,7 +810,7 @@
 
 def fwd_kernel(states, flip_ref, dbl_ref, dtp_ref, vec_ref, rate2_ref, u_ref, z_ref, gg_ref,
                gate_keep, gate_send, z_keep, z_send, delta_ref, yg_ref, prior_ref, cout_ref,
-               b_wide, c_wide, drive_s, y_s, y_tmp, c_acc, rows_s):
+               b_wide, c_wide, drive_s, sig_s, y_s, y_tmp, c_acc, rows_s):
     step = pl.program_id(1)
     length, width = u_ref.shape
     rank = dtp_ref.shape[0]
@@ -827,7 +827,9 @@
     delta_ref[...] = delta
     drive_s[...] = delta * u_ref[...].astype(f32)
     z = z_ref[...].astype(f32)
-    yg_ref[...] = gg_ref[...].astype(f32) * (z * (0.5 + 0.5*jnp.tanh(0.5*z)))
+    sig = 0.5 + 0.5*jnp.tanh(0.5*z)
+    sig_s[...] = sig
+    yg_ref[...] = gg_ref[...].astype(f32) * (z * sig)
     def run(flipped):
         def ahead(chunk, state):
             place = chunks-1-chunk if flipped else chunk
@@ -854,7 +856,7 @@
     pl.when(flip == 1)(lambda: run(True))
     u = u_ref[...].astype(f32)
     z = z_ref[...].astype(f32)
-    sig = (0.5 + 0.5*jnp.tanh(0.5*z))
+    sig = sig_s[...]
     y = y_s[...] + vec_ref[1:2,:]*u
     gated = (y*(z*sig)).astype(bf16)
     zg = (gg_ref[...].astype(f32)*y*(sig*(1.0+z*(1.0-sig)))).astype(bf16)
@@ -966,6 +968,7 @@
             pltpu.VMEM((length * states, 128), f32),
             pltpu.VMEM((length, width), f32),
             pltpu.VMEM((length, width), f32),
+            pltpu.VMEM((length, width), f32),
             pltpu.VMEM((width // 128, CHUNK * 8, 128), f32),
             pltpu.VMEM((length * states, 128), f32),
             pltpu.VMEM((length, cols), f32),
@@ -1149,7 +1152,7 @@
                 contract_rows(branch_mine, after(gate_all, part_back))
                 + contract_rows(branch_there, after(gate_there, part_back)),
                 "dp",
-                rest(out_bit),
+                rest(out_bit)[::-1],
             )
         if slot + 1 < slot_count:
             dg = (part_back + after(there, z_part.send, out_part.send)).astype(bf16)
@@ -1200,25 +1203,24 @@
         norm_mine,
         after(norm_far, shared.send),
     )
-    mod_there = swap(mod_part, "dir", 0)
+    mod_parts = [
+        lax.ppermute(mod_part, "dir", [(at, at ^ code) for at in range(dirs)])
+        for code in range(1, dirs)
+    ]
     shared.step(mod_part)
     x_part.step(shared.send)
-    mod_pair = mod_part + after(mod_there, x_part.send)
-    mod_far = swap(mod_pair, "dir", 1)
-    shared.step(mod_pair)
-    mod_total = mod_pair + after(mod_far, shared.send)
+    beside, *over = after(mod_parts, x_part.send)
+    mod_total = mod_part + beside
+    if over:
+        mod_total = mod_total + (over[0] + over[1])
     mod_low = mod_total.astype(bf16).reshape(slot_count, 3 * model)
-    half_model = model // 2
-    cond_low = cond_call(mod_low, ada_weight, cond, 0, half_model)
     have = []
     sides = jnp.concatenate([mod_low, cond_act], 1)
-    sides = gather_bit(sides, "dp", first[0], have, cond_low)
+    sides = gather_bit(sides, "dp", first[0], have)
     while len(shared.plan) > 1:
         shared.step(sides)
-    keep, there = shared.last(sides)
-    cond_high = cond_call(after(mod_low, sides), ada_weight, cond, half_model, half_model)
-    cond_grad = jnp.concatenate([cond_low, cond_high], 1)
-    sides = gather_rest(sides, "dp", first[1:], cond_high)
+    cond_grad = cond_call(after(mod_low, sides, shared.send), ada_weight, cond, 0, model)
+    sides = gather_rest(sides, "dp", first[1:], cond_grad)
     sides = sides.reshape(dps * slot_count, -1)
     total_columns = ada_weight.shape[1]
     columns = total_columns // dirs
@@ -1230,6 +1232,7 @@
     bias_part = lax.dynamic_slice_in_dim(sides, dp_index * portion, portion, 1)
     bias_sum = jnp.sum(bias_part.astype(f32), axis=0)
 
+    keep, there = shared.last(cond_grad)
     xproj_sum, kernel_sum, dtproj_sum, rate_sum, vec_sum = unpack_call(
         out_side, keep, there, cols, tap_count, conv_rows, rank, states
     )

time: 249 us -> 245 us (0.984)
  waiting for transfers between devices: 31.7 us -> 28.5 us
    ppermute x41 -> x39, waiting for transfers between devices: 31.7 us -> 27.4 us  [swap(): lax.ppermute(block, axis, [(at, at ^ 1 << bit) for at in range(count)])]
    pallas_call x2 -> x1, Pallas kernels: 9.5 us -> 8.84 us  [cond_call(): pl.pallas_call(cond_kernel, grid=(count // width,), in_specs=[whole(slots...]
    ppermute x41 -> x39, starting transfers between devices: 35.4 us -> 35.3 us  [swap(): lax.ppermute(block, axis, [(at, at ^ 1 << bit) for at in range(count)])]
    unnamed x57 -> x63, local copies, waits for them, and re-layouts: 8.24 us -> 8.15 us
  transfers between devices with their start and end apart: 44 -> 45, of which waited for: 13 -> 14; matrix products, arithmetic and copies ran while one was open for 12% -> 12% of each run, Pallas kernels for 53% -> 53%
where the time goes in v2:
time: 245 us; the launch traced here: 244 us
  Pallas kernels  133 us (54%)
  starting transfers between devices  41.6 us (17%)
  waiting for transfers between devices  28.5 us (12%)
  local copies, waits for them, and re-layouts  15.7 us (6%)
  matrix products  13.3 us (5%)
  other arithmetic  9.41 us (4%)
    pallas_call x2, Pallas kernels, backward_call(): pl.pallas_call(functools.partial(bwd_kernel, states), grid=(channels // w...  44.7 us
    ppermute x39, starting transfers between devices, swap(): lax.ppermute(block, axis, [(at, at ^ 1 << bit) for at in range(count)])  35.3 us
    pallas_call x1, Pallas kernels, forward_call(): pl.pallas_call(functools.partial(fwd_kernel, states), grid=(slots, channe...  34.3 us
    ppermute x39, waiting for transfers between devices, swap(): lax.ppermute(block, axis, [(at, at ^ 1 << bit) for at in range(count)])  27.4 us
    pallas_call x1, Pallas kernels, cond_call(): pl.pallas_call(cond_kernel, grid=(count // width,), in_specs=[whole(slots...  8.84 us
    unnamed x63, local copies, waits for them, and re-layouts  8.15 us
    pallas_call x2, Pallas kernels, conv_back_call(): pl.pallas_call(conv_back_kernel, grid=(2,), in_specs=[scalars(), item, it...  8.04 us
    pallas_call x1, Pallas kernels, norm_call(): pl.pallas_call(functools.partial(norm_kernel, chunk), grid=(channels // w...  7.72 us
  transfers between devices with their start and end apart: 45, of which 14 were waited for; matrix products, arithmetic and copies ran while one was open for 12% of the time, Pallas kernels for 53%

profile of v2, /device:TPU:0, one launch (start us, length us, event | category | flops | bytes accessed | tf_op | source)
XLA Modules:
  0.0 243.9 jit_solution(7464058465499124219)
XLA Ops:
  0.6 3.0 %collective-permute-start = (bf16[2,64,1536]{2,1,0:T(8,128)(2,1)}, bf16[2,64,1536]{2,1,0:T(8,128)(2,1)S(1)}, u32[]{:S(2)}, u32[]{:S(2)}) collective-permute-start(bf16[2,64,1536]{2,1,0:T(8,128)(2,1)} %tokens_ref.1), channel_id=1, source_target_pairs={{0,2},{1,3},{2,0},{3,1},{4,6},{5,7},{6,4},{7,5},{8,10},{9,11},{10,... | collective-permute-start | bytes 1179656 | tf_op jit(solution)/shard_map/ppermute | solution.py:21
  4.4 7.1 %convolution_add_fusion = f32[2,4608]{1,0:T(2,128)S(1)} fusion(bf16[1536,4608]{1,0:T(8,128)(2,1)} %weight_ref.5, f32[4608]{0:T(1024)S(1)} %convert_element_type.112, bf16[2,1536]{1,0:T(2,128)(2,1)} %cond_ref.1), kind=kOutput, calls=%fused_computation.1 | convolution fusion | flops 28339200 | bytes 14217216 | tf_op jit(solution)/shard_map/dot_general | solution.py:37
  11.5 1.5 collective-permute-done.over_ref
  14.9 7.7 %norm_project.1 = (bf16[512,768]{1,0:T(8,128)(2,1)S(1)}, bf16[512,768]{1,0:T(8,128)(2,1)S(1)}, bf16[512,1536]{1,0:T(8,128)(2,1)}) custom-call(s32[1]{0:T(128)} %bitcast.2.me_ref, s32[1]{0:T(128)} %bitcast.4.side_ref, bf16[2,64,1536]{2,1,0:T(8,128)(2,1)S(1)} %copy-done.4, bf16[2,64,1536]{2,1,0:T(8,128)(2,1)S(1)} %collective-permute-done.over_ref, ...), custom_call_target="tpu_custom_call" | custom-call | flops 1000 | bytes 1000 | tf_op jit(solution)/shard_map/norm_project/pallas_call | solution.py:220
  23.6 1.8 collective-permute-start.5
  25.5 3.3 %constant_dynamic-slice_fusion = bf16[1536,768]{1,0:T(8,128)(2,1)} fusion(bf16[1536,1536]{1,0:T(8,128)(2,1)} %refs_3_.1, s32[]{:T(128)S(6)} %select_n.106), kind=kLoop, calls=%fused_computation.62 | loop fusion | bytes 4718596 | tf_op jit(solution)/shard_map/dynamic_slice | solution.py:1093
  28.8 7.4 %conv_forward.1 = (bf16[512,1536]{1,0:T(8,128)(2,1)}, bf16[512,1536]{1,0:T(8,128)(2,1)}, bf16[512,1536]{1,0:T(8,128)(2,1)}, f32[512,1536]{1,0:T(8,128)}, f32[512,128]{1,0:T(8,128)}) custom-call(s32[1]{0:T(128)} %bitcast.3.flip_ref, bf16[512,1536]{1,0:T(8,128)(2,1)} %get-tuple-element.113.own_ref, bf16[512,1536]{1,0:T(8,128)(2,1)} %collective-permute-done.3.other_ref, ...), custom_call_target="tpu_custom_call" | custom-call | flops 1000 | bytes 1000 | tf_op jit(solution)/shard_map/conv_forward/pallas_call | solution.py:687
  37.6 1.6 collective-permute-start.9
  39.3 7.7 %gate_project.1 = (bf16[512,768]{1,0:T(8,128)(2,1)S(1)}, bf16[512,768]{1,0:T(8,128)(2,1)S(1)}, bf16[512,1536]{1,0:T(8,128)(2,1)}) custom-call(s32[1]{0:T(128)} %bitcast.2.me_ref, s32[1]{0:T(128)} %bitcast.7.side_ref, bf16[2,64,1536]{2,1,0:T(8,128)(2,1)} %cot_ref.1, bf16[2,64,1536]{2,1,0:T(8,128)(2,1)} %collective-permute-done.5.over_ref, ...), custom_call_target="tpu_custom_call" | custom-call | flops 1000 | bytes 1000 | tf_op jit(solution)/shard_map/gate_project/pallas_call | solution.py:283
  48.8 1.6 collective-permute-start.10
  50.5 34.3 %scan_forward.1 = (bf16[512,768]{1,0:T(8,128)(2,1)}, bf16[512,768]{1,0:T(8,128)(2,1)}, bf16[512,768]{1,0:T(8,128)(2,1)}, bf16[512,768]{1,0:T(8,128)(2,1)}, f32[5...) custom-call(s32[1]{0:T(128)} %bitcast.3.flip_ref, ...), custom_call_target="tpu_custom_call" | custom-call | flops 32000000000 | bytes 40000000 | tf_op jit(solution)/shard_map/scan_forward/pallas_call | solution.py:958
  87.8 2.1 collective-permute-done.11.second_ref
  89.9 1.1 collective-permute-done.12.fourth_ref
  91.0 2.0 pair_sums.1
  93.1 2.1 branch_rows.1
  95.7 1.2 collective-permute-start.15
  97.0 22.5 %scan_backward.2 = (f32[256,1536]{1,0:T(8,128)}, f32[256,128]{1,0:T(8,128)S(1)}, f32[120,1536]{1,0:T(8,128)S(1)}) custom-call(s32[1]{0:T(128)} %bitcast.3.flip_ref, f32[512,128]{1,0:T(8,128)S(1)} %add.139.dbl_ref, bf16[96,1536]{1,0:T(8,128)(2,1)S(1)} %copy-done.12, f32[2,1536]{1,0:T(2,128)S(1)} %pad_maximum_fusion.2.vec_ref, f32[16,1536]{1,0:T(8,128)S(1)} %copy-done.8, ...), custom_call_target="tpu_custom_call" | custom-call | flops 22000001024 | bytes 20000000 | tf_op jit(solution)/shard_map/scan_backward/pallas_call | solution.py:992
  119.4 1.4 collective-permute-start.14
  125.1 4.0 %conv_backward.2 = (bf16[256,768]{1,0:T(8,128)(2,1)S(1)}, bf16[256,768]{1,0:T(8,128)(2,1)S(1)}, f32[136,1536]{1,0:T(8,128)S(1)}) custom-call(s32[1]{0:T(128)} %bitcast.3.flip_ref, bf16[512,1536]{1,0:T(8,128)(2,1)} %get-tuple-element.135.x_ref, bf16[512,1536]{1,0:T(8,128)(2,1)} %get-tuple-element.157.u_ref, f32[512,1536]{1,0:T(8,128)} %get-tuple-element.136.slope_ref, ...), custom_call_target="tpu_custom_call" | custom-call | flops 1000 | bytes 1000 | tf_op jit(solution)/shard_map/conv_backward/pallas_call | solution.py:715
  132.1 2.6 %collective-permute-start.22 = (bf16[2,192,768]{2,1,0:T(8,128)(2,1)S(1)}, bf16[2,192,768]{2,1,0:T(8,128)(2,1)S(1)}, u32[]{:S(2)}, u32[]{:S(2)}) collective-permute-start(bf16[2,192,768]{2,1,0:T(8,128)(2,1)S(1)} %fusion.7), channel_id=1, source_target_pairs={{0,16},{4,20},{8,24},{12,28},{16,0},{20,4},{24,8},{28,12},{1,17},{... | collective-permute-start | bytes 1769480 | tf_op jit(solution)/shard_map/ppermute | solution.py:21
  134.7 1.6 collective-permute-start.20
  136.2 22.2 %scan_backward.3 = (f32[256,1536]{1,0:T(8,128)}, f32[256,128]{1,0:T(8,128)S(1)}, f32[120,1536]{1,0:T(8,128)S(1)}) custom-call(s32[1]{0:T(128)} %bitcast.3.flip_ref, f32[512,128]{1,0:T(8,128)S(1)} %add.139.dbl_ref, bf16[96,1536]{1,0:T(8,128)(2,1)S(1)} %copy-done.12, f32[2,1536]{1,0:T(2,128)S(1)} %pad_maximum_fusion.2.vec_ref, f32[16,1536]{1,0:T(8,128)S(1)} %copy-done.8, ...), custom_call_target="tpu_custom_call" | custom-call | flops 22000001024 | bytes 20000000 | tf_op jit(solution)/shard_map/scan_backward/pallas_call | solution.py:992
  158.4 2.6 %collective-permute-done.22 = bf16[2,192,768]{2,1,0:T(8,128)(2,1)S(1)} collective-permute-done((bf16[2,192,768]{2,1,0:T(8,128)(2,1)S(1)}, bf16[2,192,768]{2,1,0:T(8,128)(2,1)S(1)}, u32[]{:S(2)}, u32[]{:S(2)}) %collective-permute-start.22) | collective-permute-done | bytes 589856 | tf_op jit(solution)/shard_map/ppermute | solution.py:21
  162.2 1.1 collective-permute-start.29
  164.0 2.0 collective-permute-done.19
  166.0 4.1 %conv_backward.3 = (bf16[256,768]{1,0:T(8,128)(2,1)S(1)}, bf16[256,768]{1,0:T(8,128)(2,1)S(1)}, f32[136,1536]{1,0:T(8,128)S(1)}) custom-call(s32[1]{0:T(128)} %bitcast.3.flip_ref, bf16[512,1536]{1,0:T(8,128)(2,1)} %get-tuple-element.135.x_ref, bf16[512,1536]{1,0:T(8,128)(2,1)} %get-tuple-element.157.u_ref, f32[512,1536]{1,0:T(8,128)} %get-tuple-element.136.slope_ref, ...), custom_call_target="tpu_custom_call" | custom-call | flops 1000 | bytes 1000 | tf_op jit(solution)/shard_map/conv_backward/pallas_call | solution.py:715
  170.8 1.4 collective-permute-start.27
  173.3 1.4 copy-done.21
  174.7 5.6 %proj_back.1 = (f32[256,1536]{1,0:T(8,128)S(1)}, bf16[256,1536]{1,0:T(8,128)(2,1)S(1)}) custom-call(s32[1]{0:T(128)} %bitcast.3.flip_ref, bf16[256,768]{1,0:T(8,128)(2,1)S(1)} %join_sums.2.refs_0_, bf16[256,768]{1,0:T(8,128)(2,1)S(1)} %join_sums.3.refs_1_, bf16[512,768]{1,0:T(8,128)(2,1)S(1)} %get-tuple-element.145.refs_2_, bf16[1536,1536]{1,0:T(8,128)(2,1)} %refs_3_.1, ...), custom_call_target="tpu_custom_call" | custom-call | flops 1000 | bytes 1000 | tf_op jit(solution)/shard_map/proj_back/pallas_call | solution.py:543
  182.2 4.2 %collective-permute-done.27 = bf16[128,1536]{1,0:T(8,128)(2,1)S(1)} collective-permute-done((bf16[128,1536]{1,0:T(8,128)(2,1)S(1)}, bf16[128,1536]{1,0:T(8,128)(2,1)S(1)}, u32[]{:S(2)}, u32[]{:S(2)}) %collective-permute-start.27) | collective-permute-done | bytes 393248 | tf_op jit(solution)/shard_map/ppermute | solution.py:21
  187.7 1.3 collective-permute-start.30
  190.6 1.4 copy-done.17
  193.5 1.6 collective-permute-start.36
  195.4 3.2 %collective-permute-done.30.norm_far_ref = bf16[2,64,1536]{2,1,0:T(8,128)(2,1)S(1)} collective-permute-done((bf16[2,64,1536]{2,1,0:T(8,128)(2,1)S(1)}, bf16[2,64,1536]{2,1,0:T(8,128)(2,1)S(1)}, u32[]{:S(2)}, u32[]{:S(2)}) %collective-permute-start.30) | collective-permute-done | bytes 393248 | tf_op jit(solution)/shard_map/ppermute | solution.py:21
  198.5 3.0 %owned_rows.1 = (f32[2,64,1536]{2,1,0:T(8,128)}, f32[2,64,1536]{2,1,0:T(8,128)}, f32[2,3,1536]{2,1,0:T(4,128)S(1)}) custom-call(bf16[2,64,1536]{2,1,0:T(8,128)(2,1)S(1)} %copy-done.4, bf16[2,64,1536]{2,1,0:T(8,128)(2,1)} %cot_ref.1, f32[2,64,1]{2,1,0:T(8,128)S(1)} %copy.38.mask_ref, f32[2,3,1536]{2,1,0:T(4,128)S(1)} %reshape.91.mod_ref, ...), custom_call_target="tpu_custom_call" | custom-call | flops 1000 | bytes 1000 | tf_op jit(solution)/shard_map/owned_rows/pallas_call | solution.py:467
  201.5 1.2 collective-permute-start.33
  203.4 6.4 %collective-permute-done.36 = bf16[64,1536]{1,0:T(8,128)(2,1)} collective-permute-done((bf16[64,1536]{1,0:T(8,128)(2,1)S(1)}, bf16[64,1536]{1,0:T(8,128)(2,1)}, u32[]{:S(2)}, u32[]{:S(2)}) %collective-permute-start.36) | collective-permute-done | bytes 196640 | tf_op jit(solution)/shard_map/ppermute | solution.py:21
  212.0 1.2 bitcast_add_fusion
  215.0 3.5 %collective-permute-start.42 = (bf16[192,768]{1,0:T(8,128)(2,1)}, bf16[192,768]{1,0:T(8,128)(2,1)S(1)}, u32[]{:S(2)}, u32[]{:S(2)}) collective-permute-start(bf16[192,768]{1,0:T(8,128)(2,1)} %fusion.14), channel_id=1, source_target_pairs={{0,16},{4,20},{8,24},{12,28},{16,0},{20,4},{24,8},{28,12},{1,17},{... | collective-permute-start | bytes 884744 | tf_op jit(solution)/shard_map/ppermute | solution.py:21
  218.6 2.1 collective-permute-start.39
  221.2 1.8 collective-permute-start.41
  223.1 1.1 collective-permute-start.43
  224.2 8.8 %cond_rows.1 = f32[2,1536]{1,0:T(2,128)} custom-call(bf16[2,4608]{1,0:T(2,128)(2,1)S(1)} %bitcast.80, bf16[1536,4608]{1,0:T(8,128)(2,1)} %weight_ref.5, bf16[2,1536]{1,0:T(2,128)(2,1)S(1)} %copy-done.9), custom_call_target="tpu_custom_call" | custom-call | flops 1000 | bytes 1000 | tf_op jit(solution)/shard_map/cond_rows/pallas_call | solution.py:572
  233.1 1.1 collective-permute-done.40
  235.6 2.9 %collective-permute-done.43.there_ref = bf16[128,1536]{1,0:T(8,128)(2,1)S(1)} collective-permute-done((bf16[128,1536]{1,0:T(8,128)(2,1)S(1)}, bf16[128,1536]{1,0:T(8,128)(2,1)S(1)}, u32[]{:S(2)}, u32[]{:S(2)}) %collective-permute-start.43) | collective-permute-done | bytes 393248 | tf_op jit(solution)/shard_map/ppermute | solution.py:21
  238.4 1.4 unpack_sums.1
  240.9 1.3 fusion.15
  242.8 1.1 maximum_select_fusion
  (185 shorter events, 35.4 us)
Async XLA Ops:
  0.6 12.4 %collective-permute-start = (bf16[2,64,1536]{2,1,0:T(8,128)(2,1)}, bf16[2,64,1536]{2,1,0:T(8,128)(2,1)S(1)}, u32[]{:S(2)}, u32[]{:S(2)}) collective-permute-start(bf16[2,64,1536]{2,1,0:T(8,128)(2,1)} %tokens_ref.1), channel_id=1, source_target_pairs={{0,2},{1,3},{2,0},{3,1},{4,6},{5,7},{6,4},{7,5},{8,10},{9,11},{10,... | collective-permute-start | bytes 1179656 | tf_op jit(solution)/shard_map/ppermute | solution.py:21
  3.7 10.8 %collective-permute-start.1 = (bf16[2,64,1536]{2,1,0:T(8,128)(2,1)}, bf16[2,64,1536]{2,1,0:T(8,128)(2,1)}, u32[]{:S(2)}, u32[]{:S(2)}) collective-permute-start(bf16[2,64,1536]{2,1,0:T(8,128)(2,1)} %tokens_ref.1), channel_id=1, source_target_pairs={{0,1},{1,0},{2,3},{3,2},{4,5},{5,4},{6,7},{7,6},{8,9},{9,8},{10,11... | collective-permute-start | bytes 1179656 | tf_op jit(solution)/shard_map/ppermute | solution.py:21
  13.0 1.9 collective-permute-start.2
  13.0 26.2 %collective-permute-start.8 = (bf16[768,1536]{1,0:T(8,128)(2,1)S(1)}, bf16[768,1536]{1,0:T(8,128)(2,1)}, u32[]{:S(2)}, u32[]{:S(2)}) collective-permute-start(bf16[768,1536]{1,0:T(8,128)(2,1)S(1)} %copy-done), channel_id=1, source_target_pairs={{0,1},{1,0},{2,3},{3,2},{4,5},{5,4},{6,7},{7,6},{8,9},{9,8},{10,11... | collective-permute-start | bytes 7077896 | tf_op jit(solution)/shard_map/ppermute | solution.py:21
  23.5 5.4 %collective-permute-start.3 = (bf16[512,1536]{1,0:T(8,128)(2,1)}, bf16[512,1536]{1,0:T(8,128)(2,1)}, u32[]{:S(2)}, u32[]{:S(2)}) collective-permute-start(bf16[512,1536]{1,0:T(8,128)(2,1)} %get-tuple-element.113.own_ref), channel_id=1, source_target_pairs={{0,1},{1,0},{2,3},{3,2},{4,5},{5,4},{6,7},{7,6},{8,9},{9,8},{10,11... | collective-permute-start | bytes 4718600 | tf_op jit(solution)/shard_map/ppermute | solution.py:21
  23.6 13.3 %collective-permute-start.5 = (bf16[2,64,1536]{2,1,0:T(8,128)(2,1)}, bf16[2,64,1536]{2,1,0:T(8,128)(2,1)}, u32[]{:S(2)}, u32[]{:S(2)}) collective-permute-start(bf16[2,64,1536]{2,1,0:T(8,128)(2,1)} %cot_ref.1), channel_id=1, source_target_pairs={{0,2},{1,3},{2,0},{3,1},{4,6},{5,7},{6,4},{7,5},{8,10},{9,11},{10,... | collective-permute-start | bytes 1179656 | tf_op jit(solution)/shard_map/ppermute | solution.py:21
  25.3 13.9 %collective-permute-start.6 = (bf16[2,64,1536]{2,1,0:T(8,128)(2,1)}, bf16[2,64,1536]{2,1,0:T(8,128)(2,1)}, u32[]{:S(2)}, u32[]{:S(2)}) collective-permute-start(bf16[2,64,1536]{2,1,0:T(8,128)(2,1)} %cot_ref.1), channel_id=1, source_target_pairs={{0,1},{1,0},{2,3},{3,2},{4,5},{5,4},{6,7},{7,6},{8,9},{9,8},{10,11... | collective-permute-start | bytes 1179656 | tf_op jit(solution)/shard_map/ppermute | solution.py:21
  36.3 11.5 %collective-permute-start.4 = (f32[512,128]{1,0:T(8,128)}, f32[512,128]{1,0:T(8,128)}, u32[]{:S(2)}, u32[]{:S(2)}) collective-permute-start(f32[512,128]{1,0:T(8,128)} %get-tuple-element.117), channel_id=1, source_target_pairs={{0,2},{1,3},{2,0},{3,1},{4,6},{5,7},{6,4},{7,5},{8,10},{9,11},{10,... | collective-permute-start | bytes 786440 | tf_op jit(solution)/shard_map/ppermute | solution.py:21
  36.9 2.3 collective-permute-start.7
  37.6 47.9 %collective-permute-start.9 = (bf16[512,768]{1,0:T(8,128)(2,1)}, bf16[512,768]{1,0:T(8,128)(2,1)S(1)}, u32[]{:S(2)}, u32[]{:S(2)}) collective-permute-start(bf16[512,768]{1,0:T(8,128)(2,1)} %copy-done.10), channel_id=1, source_target_pairs={{0,4},{4,0},{8,12},{12,8},{16,20},{20,16},{24,28},{28,24},{1,5},{5... | collective-permute-start | bytes 2359304 | tf_op jit(solution)/shard_map/ppermute | solution.py:21
  39.2 11.2 %copy-start.7 = (f32[16,1536]{1,0:T(8,128)S(1)}, f32[16,1536]{1,0:T(8,128)}, u32[]{:S(2)}) copy-start(f32[16,1536]{1,0:T(8,128)} %multiply_bitcast_fusion.rate2_ref) | copy-start | bytes 294916
  48.8 36.7 %collective-permute-start.10 = (bf16[512,768]{1,0:T(8,128)(2,1)S(1)}, bf16[512,768]{1,0:T(8,128)(2,1)S(1)}, u32[]{:S(2)}, u32[]{:S(2)}) collective-permute-start(bf16[512,768]{1,0:T(8,128)(2,1)S(1)} %get-tuple-element.128), channel_id=1, source_target_pairs={{0,8},{4,12},{8,0},{12,4},{16,24},{20,28},{24,16},{28,20},{1,9},{5... | collective-permute-start | bytes 2359304 | tf_op jit(solution)/shard_map/ppermute | solution.py:21
  87.3 2.6 %collective-permute-start.11 = (bf16[512,768]{1,0:T(8,128)(2,1)}, bf16[512,768]{1,0:T(8,128)(2,1)}, u32[]{:S(2)}, u32[]{:S(2)}) collective-permute-start(bf16[512,768]{1,0:T(8,128)(2,1)} %get-tuple-element.129), channel_id=1, source_target_pairs={{0,1},{1,0},{2,3},{3,2},{4,5},{5,4},{6,7},{7,6},{8,9},{9,8},{10,11... | collective-permute-start | bytes 2359304 | tf_op jit(solution)/shard_map/ppermute | solution.py:21
  87.3 3.7 %collective-permute-start.12 = (bf16[512,768]{1,0:T(8,128)(2,1)}, bf16[512,768]{1,0:T(8,128)(2,1)}, u32[]{:S(2)}, u32[]{:S(2)}) collective-permute-start(bf16[512,768]{1,0:T(8,128)(2,1)} %get-tuple-element.131), channel_id=1, source_target_pairs={{0,1},{1,0},{2,3},{3,2},{4,5},{5,4},{6,7},{7,6},{8,9},{9,8},{10,11... | collective-permute-start | bytes 2359304 | tf_op jit(solution)/shard_map/ppermute | solution.py:21
  95.2 25.7 %collective-permute-start.16 = (bf16[512,768]{1,0:T(8,128)(2,1)S(1)}, bf16[512,768]{1,0:T(8,128)(2,1)S(1)}, u32[]{:S(2)}, u32[]{:S(2)}) collective-permute-start(bf16[512,768]{1,0:T(8,128)(2,1)S(1)} %get-tuple-element.148.values_ref), channel_id=1, source_target_pairs={{0,8},{4,12},{8,0},{12,4},{16,24},{20,28},{24,16},{28,20},{1,9},{5... | collective-permute-start | bytes 2359304 | tf_op jit(solution)/shard_map/ppermute | solution.py:21
  95.7 25.2 %collective-permute-start.15 = (bf16[512,768]{1,0:T(8,128)(2,1)S(1)}, bf16[512,768]{1,0:T(8,128)(2,1)S(1)}, u32[]{:S(2)}, u32[]{:S(2)}) collective-permute-start(bf16[512,768]{1,0:T(8,128)(2,1)S(1)} %get-tuple-element.145.refs_2_), channel_id=1, source_target_pairs={{0,4},{4,0},{8,12},{12,8},{16,20},{20,16},{24,28},{28,24},{1,5},{5... | collective-permute-start | bytes 2359304 | tf_op jit(solution)/shard_map/ppermute | solution.py:21
  97.0 23.9 %copy-start.16 = (bf16[512,768]{1,0:T(8,128)(2,1)S(1)}, bf16[512,768]{1,0:T(8,128)(2,1)}, u32[]{:S(2)}) copy-start(bf16[512,768]{1,0:T(8,128)(2,1)} %copy-done.15) | copy-start | bytes 2359300
  119.4 5.5 %collective-permute-start.14 = (f32[256,128]{1,0:T(8,128)S(1)}, f32[256,128]{1,0:T(8,128)S(1)}, u32[]{:S(2)}, u32[]{:S(2)}) collective-permute-start(f32[256,128]{1,0:T(8,128)S(1)} %get-tuple-element.144), channel_id=1, source_target_pairs={{0,2},{1,3},{2,0},{3,1},{4,6},{5,7},{6,4},{7,5},{8,10},{9,11},{10,... | collective-permute-start | bytes 393224 | tf_op jit(solution)/shard_map/ppermute | solution.py:21
  120.8 8.9 %collective-permute-start.13 = (bf16[256,1536]{1,0:T(8,128)(2,1)S(1)}, bf16[256,1536]{1,0:T(8,128)(2,1)S(1)}, u32[]{:S(2)}, u32[]{:S(2)}) collective-permute-start(bf16[256,1536]{1,0:T(8,128)(2,1)S(1)} %get-tuple-element.134), channel_id=1, source_target_pairs={{0,1},{1,0},{2,3},{3,2},{4,5},{5,4},{6,7},{7,6},{8,9},{9,8},{10,11... | collective-permute-start | bytes 2359304 | tf_op jit(solution)/shard_map/ppermute | solution.py:21
  129.0 1.9 collective-permute-start.18
  129.7 43.6 %collective-permute-start.24 = (bf16[1536,768]{1,0:T(8,128)(2,1)S(1)}, bf16[1536,768]{1,0:T(8,128)(2,1)S(1)}, u32[]{:S(2)}, u32[]{:S(2)}) collective-permute-start(bf16[1536,768]{1,0:T(8,128)(2,1)S(1)} %copy-done.19), channel_id=1, source_target_pairs={{0,1},{1,0},{2,3},{3,2},{4,5},{5,4},{6,7},{7,6},{8,9},{9,8},{10,11... | collective-permute-start | bytes 7077896 | tf_op jit(solution)/shard_map/ppermute | solution.py:21
  129.9 32.0 %collective-permute-start.17 = (bf16[2,64,1536]{2,1,0:T(8,128)(2,1)S(1)}, bf16[2,64,1536]{2,1,0:T(8,128)(2,1)S(1)}, u32[]{:S(2)}, u32[]{:S(2)}) collective-permute-start(bf16[2,64,1536]{2,1,0:T(8,128)(2,1)S(1)} %get-tuple-element.154), channel_id=1, source_target_pairs={{0,2},{1,3},{2,0},{3,1},{4,6},{5,7},{6,4},{7,5},{8,10},{9,11},{10,... | collective-permute-start | bytes 1179656 | tf_op jit(solution)/shard_map/ppermute | solution.py:21
  131.0 30.9 %collective-permute-start.21 = (bf16[256,768]{1,0:T(8,128)(2,1)S(1)}, bf16[256,768]{1,0:T(8,128)(2,1)S(1)}, u32[]{:S(2)}, u32[]{:S(2)}) collective-permute-start(bf16[256,768]{1,0:T(8,128)(2,1)S(1)} %join_sums.2.refs_0_), channel_id=1, source_target_pairs={{0,4},{4,0},{8,12},{12,8},{16,20},{20,16},{24,28},{28,24},{1,5},{5... | collective-permute-start | bytes 1179656 | tf_op jit(solution)/shard_map/ppermute | solution.py:21
  132.1 29.0 %collective-permute-start.22 = (bf16[2,192,768]{2,1,0:T(8,128)(2,1)S(1)}, bf16[2,192,768]{2,1,0:T(8,128)(2,1)S(1)}, u32[]{:S(2)}, u32[]{:S(2)}) collective-permute-start(bf16[2,192,768]{2,1,0:T(8,128)(2,1)S(1)} %fusion.7), channel_id=1, source_target_pairs={{0,16},{4,20},{8,24},{12,28},{16,0},{20,4},{24,8},{28,12},{1,17},{... | collective-permute-start | bytes 1769480 | tf_op jit(solution)/shard_map/ppermute | solution.py:21
  134.7 27.3 %collective-permute-start.20 = (bf16[2,192,768]{2,1,0:T(8,128)(2,1)S(1)}, bf16[2,192,768]{2,1,0:T(8,128)(2,1)S(1)}, u32[]{:S(2)}, u32[]{:S(2)}) collective-permute-start(bf16[2,192,768]{2,1,0:T(8,128)(2,1)S(1)} %fusion.8), channel_id=1, source_target_pairs={{0,8},{4,12},{8,0},{12,4},{16,24},{20,28},{24,16},{28,20},{1,9},{5... | collective-permute-start | bytes 1769480 | tf_op jit(solution)/shard_map/ppermute | solution.py:21
  161.0 5.0 %collective-permute-start.19 = (f32[256,128]{1,0:T(8,128)S(1)}, f32[256,128]{1,0:T(8,128)S(1)}, u32[]{:S(2)}, u32[]{:S(2)}) collective-permute-start(f32[256,128]{1,0:T(8,128)S(1)} %get-tuple-element.160), channel_id=1, source_target_pairs={{0,2},{1,3},{2,0},{3,1},{4,6},{5,7},{6,4},{7,5},{8,10},{9,11},{10,... | collective-permute-start | bytes 393224 | tf_op jit(solution)/shard_map/ppermute | solution.py:21
  162.2 18.2 %collective-permute-start.29 = (bf16[192,768]{1,0:T(8,128)(2,1)S(1)}, bf16[192,768]{1,0:T(8,128)(2,1)S(1)}, u32[]{:S(2)}, u32[]{:S(2)}) collective-permute-start(bf16[192,768]{1,0:T(8,128)(2,1)S(1)} %get-tuple-element.216), channel_id=1, source_target_pairs={{0,4},{4,0},{8,12},{12,8},{16,20},{20,16},{24,28},{28,24},{1,5},{5... | collective-permute-start | bytes 884744 | tf_op jit(solution)/shard_map/ppermute | solution.py:21
  163.4 17.1 %collective-permute-start.28 = (bf16[192,768]{1,0:T(8,128)(2,1)S(1)}, bf16[192,768]{1,0:T(8,128)(2,1)S(1)}, u32[]{:S(2)}, u32[]{:S(2)}) collective-permute-start(bf16[192,768]{1,0:T(8,128)(2,1)S(1)} %get-tuple-element.215), channel_id=1, source_target_pairs={{0,16},{4,20},{8,24},{12,28},{16,0},{20,4},{24,8},{28,12},{1,17},{... | collective-permute-start | bytes 884744 | tf_op jit(solution)/shard_map/ppermute | solution.py:21
  170.3 1.9 collective-permute-start.23
  170.8 15.6 %collective-permute-start.27 = (bf16[128,1536]{1,0:T(8,128)(2,1)S(1)}, bf16[128,1536]{1,0:T(8,128)(2,1)S(1)}, u32[]{:S(2)}, u32[]{:S(2)}) collective-permute-start(bf16[128,1536]{1,0:T(8,128)(2,1)S(1)} %get-tuple-element.171), channel_id=1, source_target_pairs={{0,8},{4,12},{8,0},{12,4},{16,24},{20,28},{24,16},{28,20},{1,9},{5... | collective-permute-start | bytes 1179656 | tf_op jit(solution)/shard_map/ppermute | solution.py:21
  172.3 15.2 %collective-permute-start.26 = (bf16[256,768]{1,0:T(8,128)(2,1)S(1)}, bf16[256,768]{1,0:T(8,128)(2,1)S(1)}, u32[]{:S(2)}, u32[]{:S(2)}) collective-permute-start(bf16[256,768]{1,0:T(8,128)(2,1)S(1)} %join_sums.3.refs_1_), channel_id=1, source_target_pairs={{0,4},{4,0},{8,12},{12,8},{16,20},{20,16},{24,28},{28,24},{1,5},{5... | collective-permute-start | bytes 1179656 | tf_op jit(solution)/shard_map/ppermute | solution.py:21
  180.3 7.2 %collective-permute-start.25 = (bf16[256,1536]{1,0:T(8,128)(2,1)S(1)}, bf16[256,1536]{1,0:T(8,128)(2,1)S(1)}, u32[]{:S(2)}, u32[]{:S(2)}) collective-permute-start(bf16[256,1536]{1,0:T(8,128)(2,1)S(1)} %get-tuple-element.174), channel_id=1, source_target_pairs={{0,1},{1,0},{2,3},{3,2},{4,5},{5,4},{6,7},{7,6},{8,9},{9,8},{10,11... | collective-permute-start | bytes 2359304 | tf_op jit(solution)/shard_map/ppermute | solution.py:21
  186.5 6.9 %collective-permute-start.31 = (bf16[64,1536]{1,0:T(8,128)(2,1)S(1)}, bf16[64,1536]{1,0:T(8,128)(2,1)S(1)}, u32[]{:S(2)}, u32[]{:S(2)}) collective-permute-start(bf16[64,1536]{1,0:T(8,128)(2,1)S(1)} %dynamic-slice_convert_fusion.4), channel_id=1, source_target_pairs={{0,4},{4,0},{8,12},{12,8},{16,20},{20,16},{24,28},{28,24},{1,5},{5... | collective-permute-start | bytes 589832 | tf_op jit(solution)/shard_map/ppermute | solution.py:21
  187.7 10.8 %collective-permute-start.30 = (bf16[2,64,1536]{2,1,0:T(8,128)(2,1)S(1)}, bf16[2,64,1536]{2,1,0:T(8,128)(2,1)S(1)}, u32[]{:S(2)}, u32[]{:S(2)}) collective-permute-start(bf16[2,64,1536]{2,1,0:T(8,128)(2,1)S(1)} %get-tuple-element.182), channel_id=1, source_target_pairs={{0,2},{1,3},{2,0},{3,1},{4,6},{5,7},{6,4},{7,5},{8,10},{9,11},{10,... | collective-permute-start | bytes 1179656 | tf_op jit(solution)/shard_map/ppermute | solution.py:21
  192.9 19.2 %collective-permute-start.35 = (bf16[2,192,768]{2,1,0:T(8,128)(2,1)}, bf16[2,192,768]{2,1,0:T(8,128)(2,1)}, u32[]{:S(2)}, u32[]{:S(2)}) collective-permute-start(bf16[2,192,768]{2,1,0:T(8,128)(2,1)} %fusion.9), channel_id=1, source_target_pairs={{0,8},{4,12},{8,0},{12,4},{16,24},{20,28},{24,16},{28,20},{1,9},{5... | collective-permute-start | bytes 1769480 | tf_op jit(solution)/shard_map/ppermute | solution.py:21
  193.5 16.3 %collective-permute-start.36 = (bf16[64,1536]{1,0:T(8,128)(2,1)S(1)}, bf16[64,1536]{1,0:T(8,128)(2,1)}, u32[]{:S(2)}, u32[]{:S(2)}) collective-permute-start(bf16[64,1536]{1,0:T(8,128)(2,1)S(1)} %add_convert_fusion.1), channel_id=1, source_target_pairs={{0,16},{4,20},{8,24},{12,28},{16,0},{20,4},{24,8},{28,12},{1,17},{... | collective-permute-start | bytes 589832 | tf_op jit(solution)/shard_map/ppermute | solution.py:21
  198.5 13.5 %copy-start.18 = (f32[768,768]{1,0:T(8,128)S(1)}, f32[768,768]{1,0:T(8,128)}, u32[]{:S(2)}) copy-start(f32[768,768]{1,0:T(8,128)} %copy-done.17) | copy-start | bytes 7077892
  201.5 12.5 %collective-permute-start.32 = (f32[2,3,1536]{2,1,0:T(4,128)S(1)}, f32[2,3,1536]{2,1,0:T(4,128)S(1)}, u32[]{:S(2)}, u32[]{:S(2)}) collective-permute-start(f32[2,3,1536]{2,1,0:T(4,128)S(1)} %get-tuple-element.191), channel_id=1, source_target_pairs={{0,1},{1,0},{2,3},{3,2},{4,5},{5,4},{6,7},{7,6},{8,9},{9,8},{10,11... | collective-permute-start | bytes 110600 | tf_op jit(solution)/shard_map/ppermute | solution.py:1207
  201.5 12.5 %collective-permute-start.33 = (f32[2,3,1536]{2,1,0:T(4,128)S(1)}, f32[2,3,1536]{2,1,0:T(4,128)S(1)}, u32[]{:S(2)}, u32[]{:S(2)}) collective-permute-start(f32[2,3,1536]{2,1,0:T(4,128)S(1)} %get-tuple-element.191), channel_id=1, source_target_pairs={{0,2},{1,3},{2,0},{3,1},{4,6},{5,7},{6,4},{7,5},{8,10},{9,11},{10,... | collective-permute-start | bytes 110600 | tf_op jit(solution)/shard_map/ppermute | solution.py:1207
  202.7 11.3 %collective-permute-start.34 = (f32[2,3,1536]{2,1,0:T(4,128)S(1)}, f32[2,3,1536]{2,1,0:T(4,128)S(1)}, u32[]{:S(2)}, u32[]{:S(2)}) collective-permute-start(f32[2,3,1536]{2,1,0:T(4,128)S(1)} %get-tuple-element.191), channel_id=1, source_target_pairs={{0,3},{1,2},{2,1},{3,0},{4,7},{5,6},{6,5},{7,4},{8,11},{9,10},{10,... | collective-permute-start | bytes 110600 | tf_op jit(solution)/shard_map/ppermute | solution.py:1207
  210.7 12.4 %collective-permute-start.38 = (bf16[64,1536]{1,0:T(8,128)(2,1)S(1)}, bf16[64,1536]{1,0:T(8,128)(2,1)S(1)}, u32[]{:S(2)}, u32[]{:S(2)}) collective-permute-start(bf16[64,1536]{1,0:T(8,128)(2,1)S(1)} %add_convert_fusion), channel_id=1, source_target_pairs={{0,4},{4,0},{8,12},{12,8},{16,20},{20,16},{24,28},{28,24},{1,5},{5... | collective-permute-start | bytes 589832 | tf_op jit(solution)/shard_map/ppermute | solution.py:21
  214.1 4.4 %collective-permute-start.37 = (bf16[2,6144]{1,0:T(2,128)(2,1)S(1)}, bf16[2,6144]{1,0:T(2,128)(2,1)S(1)}, u32[]{:S(2)}, u32[]{:S(2)}) collective-permute-start(bf16[2,6144]{1,0:T(2,128)(2,1)S(1)} %pad_maximum_fusion.1), channel_id=1, source_target_pairs={{0,4},{4,0},{8,12},{12,8},{16,20},{20,16},{24,28},{28,24},{1,5},{5... | collective-permute-start | bytes 73736 | tf_op jit(solution)/shard_map/ppermute | solution.py:21
  215.0 24.9 %collective-permute-start.42 = (bf16[192,768]{1,0:T(8,128)(2,1)}, bf16[192,768]{1,0:T(8,128)(2,1)S(1)}, u32[]{:S(2)}, u32[]{:S(2)}) collective-permute-start(bf16[192,768]{1,0:T(8,128)(2,1)} %fusion.14), channel_id=1, source_target_pairs={{0,16},{4,20},{8,24},{12,28},{16,0},{20,4},{24,8},{28,12},{1,17},{... | collective-permute-start | bytes 884744 | tf_op jit(solution)/shard_map/ppermute | solution.py:21
  218.6 14.5 %collective-permute-start.39 = (bf16[2,2,6144]{2,1,0:T(2,128)(2,1)S(1)}, bf16[2,2,6144]{2,1,0:T(2,128)(2,1)S(1)}, u32[]{:S(2)}, u32[]{:S(2)}) collective-permute-start(bf16[2,2,6144]{2,1,0:T(2,128)(2,1)S(1)} %broadcast_select_fusion.1), channel_id=1, source_target_pairs={{0,8},{4,12},{8,0},{12,4},{16,24},{20,28},{24,16},{28,20},{1,9},{5... | collective-permute-start | bytes 147464 | tf_op jit(solution)/shard_map/ppermute | solution.py:131
  220.6 13.6 %collective-permute-start.40 = (bf16[2,2,6144]{2,1,0:T(2,128)(2,1)S(1)}, bf16[2,2,6144]{2,1,0:T(2,128)(2,1)S(1)}, u32[]{:S(2)}, u32[]{:S(2)}) collective-permute-start(bf16[2,2,6144]{2,1,0:T(2,128)(2,1)S(1)} %broadcast_select_fusion.1), channel_id=1, source_target_pairs={{0,16},{4,20},{8,24},{12,28},{16,0},{20,4},{24,8},{28,12},{1,17},{... | collective-permute-start | bytes 147464 | tf_op jit(solution)/shard_map/ppermute | solution.py:131
  221.2 13.0 %collective-permute-start.41 = (bf16[2,2,6144]{2,1,0:T(2,128)(2,1)S(1)}, bf16[2,2,6144]{2,1,0:T(2,128)(2,1)S(1)}, u32[]{:S(2)}, u32[]{:S(2)}) collective-permute-start(bf16[2,2,6144]{2,1,0:T(2,128)(2,1)S(1)} %broadcast_select_fusion.1), channel_id=1, source_target_pairs={{0,24},{4,28},{8,16},{12,20},{16,8},{20,12},{24,0},{28,4},{1,25},{... | collective-permute-start | bytes 147464 | tf_op jit(solution)/shard_map/ppermute | solution.py:131
  223.1 15.3 %collective-permute-start.43 = (bf16[128,1536]{1,0:T(8,128)(2,1)S(1)}, bf16[128,1536]{1,0:T(8,128)(2,1)S(1)}, u32[]{:S(2)}, u32[]{:S(2)}) collective-permute-start(bf16[128,1536]{1,0:T(8,128)(2,1)S(1)} %maximum_select_fusion.1.keep_ref), channel_id=1, source_target_pairs={{0,8},{4,12},{8,0},{12,4},{16,24},{20,28},{24,16},{28,20},{1,9},{5... | collective-permute-start | bytes 1179656 | tf_op jit(solution)/shard_map/ppermute | solution.py:21
  240.0 2.8 %collective-permute-start.44 = (f32[192,768]{1,0:T(8,128)S(1)}, f32[192,768]{1,0:T(8,128)S(1)}, u32[]{:S(2)}, u32[]{:S(2)}) collective-permute-start(f32[192,768]{1,0:T(8,128)S(1)} %get-tuple-element.214), channel_id=1, source_target_pairs={{0,1},{1,0},{2,3},{3,2},{4,5},{5,4},{6,7},{7,6},{8,9},{9,8},{10,11... | collective-permute-start | bytes 1769480 | tf_op jit(solution)/shard_map/ppermute | solution.py:21
  (28 other events, 136.0 us)

commit v3 on v2

--- a/solution.py
+++ b/solution.py
@@ -56,6 +56,7 @@
     def __init__(self, values, axis, order):
         self.axis, self.order = axis, list(order)
         bits = len(order)
+        values = values.astype(bf16)
         self.values = values.reshape((2,) * bits + (values.shape[0] >> bits,) + values.shape[1:])
         self.left = sorted(order, reverse=True)
         self.split()
@@ -1232,7 +1233,7 @@
     bias_part = lax.dynamic_slice_in_dim(sides, dp_index * portion, portion, 1)
     bias_sum = jnp.sum(bias_part.astype(f32), axis=0)
 
-    keep, there = shared.last(cond_grad)
+    keep, there = shared.last(ada_sum, bias_sum)
     xproj_sum, kernel_sum, dtproj_sum, rate_sum, vec_sum = unpack_call(
         out_side, keep, there, cols, tap_count, conv_rows, rank, states
     )

time: 245 us -> 243 us (level)
  transfers between devices with their start and end apart: 45 -> 45, of which waited for: 14 -> 15; matrix products, arithmetic and copies ran while one was open for 12% -> 12% of each run, Pallas kernels for 53% -> 53%
where the time goes in v3:
time: 243 us
  Pallas kernels  133 us (55%)
  starting transfers between devices  41.4 us (17%)
  waiting for transfers between devices  27.9 us (11%)
  local copies, waits for them, and re-layouts  15.3 us (6%)
  matrix products  13.3 us (5%)
  other arithmetic  9.49 us (4%)
    pallas_call x2, Pallas kernels, backward_call(): pl.pallas_call(functools.partial(bwd_kernel, states), grid=(channels // w...  44.7 us
    ppermute x39, starting transfers between devices, swap(): lax.ppermute(block, axis, [(at, at ^ 1 << bit) for at in range(count)])  34.9 us
    pallas_call x1, Pallas kernels, forward_call(): pl.pallas_call(functools.partial(fwd_kernel, states), grid=(slots, channe...  34.3 us
    ppermute x39, waiting for transfers between devices, swap(): lax.ppermute(block, axis, [(at, at ^ 1 << bit) for at in range(count)])  26.9 us
    pallas_call x1, Pallas kernels, cond_call(): pl.pallas_call(cond_kernel, grid=(count // width,), in_specs=[whole(slots...  8.84 us
    pallas_call x2, Pallas kernels, conv_back_call(): pl.pallas_call(conv_back_kernel, grid=(2,), in_specs=[scalars(), item, it...  8.03 us
    unnamed x63, local copies, waits for them, and re-layouts  7.78 us
    pallas_call x1, Pallas kernels, norm_call(): pl.pallas_call(functools.partial(norm_kernel, chunk), grid=(channels // w...  7.72 us
  transfers between devices with their start and end apart: 45, of which 15 were waited for; matrix products, arithmetic and copies ran while one was open for 12% of the time, Pallas kernels for 53%

profile of v3, /device:TPU:0, one launch (start us, length us, event | category | flops | bytes accessed | tf_op | source)
XLA Modules:
  0.0 242.7 jit_solution(4402766902047931510)
XLA Ops:
  0.6 3.0 %collective-permute-start = (bf16[2,64,1536]{2,1,0:T(8,128)(2,1)}, bf16[2,64,1536]{2,1,0:T(8,128)(2,1)S(1)}, u32[]{:S(2)}, u32[]{:S(2)}) collective-permute-start(bf16[2,64,1536]{2,1,0:T(8,128)(2,1)} %tokens_ref.1), channel_id=1, source_target_pairs={{0,2},{1,3},{2,0},{3,1},{4,6},{5,7},{6,4},{7,5},{8,10},{9,11},{10,... | collective-permute-start | bytes 1179656 | tf_op jit(solution)/shard_map/ppermute | solution.py:21
  4.4 7.1 %convolution_add_fusion = f32[2,4608]{1,0:T(2,128)S(1)} fusion(bf16[1536,4608]{1,0:T(8,128)(2,1)} %weight_ref.5, f32[4608]{0:T(1024)S(1)} %convert_element_type.121, bf16[2,1536]{1,0:T(2,128)(2,1)} %cond_ref.1), kind=kOutput, calls=%fused_computation.1 | convolution fusion | flops 28339200 | bytes 14217216 | tf_op jit(solution)/shard_map/dot_general | solution.py:37
  11.5 1.5 collective-permute-done.over_ref
  14.9 7.7 %norm_project.1 = (bf16[512,768]{1,0:T(8,128)(2,1)S(1)}, bf16[512,768]{1,0:T(8,128)(2,1)S(1)}, bf16[512,1536]{1,0:T(8,128)(2,1)}) custom-call(s32[1]{0:T(128)} %bitcast.2.me_ref, s32[1]{0:T(128)} %bitcast.4.side_ref, bf16[2,64,1536]{2,1,0:T(8,128)(2,1)S(1)} %copy-done.4, bf16[2,64,1536]{2,1,0:T(8,128)(2,1)S(1)} %collective-permute-done.over_ref, ...), custom_call_target="tpu_custom_call" | custom-call | flops 1000 | bytes 1000 | tf_op jit(solution)/shard_map/norm_project/pallas_call | solution.py:221
  23.6 1.8 collective-permute-start.5
  25.5 3.3 %constant_dynamic-slice_fusion = bf16[1536,768]{1,0:T(8,128)(2,1)} fusion(bf16[1536,1536]{1,0:T(8,128)(2,1)} %refs_3_.1, s32[]{:T(128)S(6)} %select_n.106), kind=kLoop, calls=%fused_computation.59 | loop fusion | bytes 4718596 | tf_op jit(solution)/shard_map/dynamic_slice | solution.py:1094
  28.8 7.4 %conv_forward.1 = (bf16[512,1536]{1,0:T(8,128)(2,1)}, bf16[512,1536]{1,0:T(8,128)(2,1)}, bf16[512,1536]{1,0:T(8,128)(2,1)}, f32[512,1536]{1,0:T(8,128)}, f32[512,128]{1,0:T(8,128)}) custom-call(s32[1]{0:T(128)} %bitcast.3.flip_ref, bf16[512,1536]{1,0:T(8,128)(2,1)} %get-tuple-element.113.own_ref, bf16[512,1536]{1,0:T(8,128)(2,1)} %collective-permute-done.3.other_ref, ...), custom_call_target="tpu_custom_call" | custom-call | flops 1000 | bytes 1000 | tf_op jit(solution)/shard_map/conv_forward/pallas_call | solution.py:688
  37.6 1.6 collective-permute-start.9
  39.3 7.7 %gate_project.1 = (bf16[512,768]{1,0:T(8,128)(2,1)S(1)}, bf16[512,768]{1,0:T(8,128)(2,1)S(1)}, bf16[512,1536]{1,0:T(8,128)(2,1)}) custom-call(s32[1]{0:T(128)} %bitcast.2.me_ref, s32[1]{0:T(128)} %bitcast.7.side_ref, bf16[2,64,1536]{2,1,0:T(8,128)(2,1)} %cot_ref.1, bf16[2,64,1536]{2,1,0:T(8,128)(2,1)} %collective-permute-done.5.over_ref, ...), custom_call_target="tpu_custom_call" | custom-call | flops 1000 | bytes 1000 | tf_op jit(solution)/shard_map/gate_project/pallas_call | solution.py:284
  48.8 1.6 collective-permute-start.10
  50.5 34.3 %scan_forward.1 = (bf16[512,768]{1,0:T(8,128)(2,1)}, bf16[512,768]{1,0:T(8,128)(2,1)}, bf16[512,768]{1,0:T(8,128)(2,1)}, bf16[512,768]{1,0:T(8,128)(2,1)}, f32[5...) custom-call(s32[1]{0:T(128)} %bitcast.3.flip_ref, ...), custom_call_target="tpu_custom_call" | custom-call | flops 32000000000 | bytes 40000000 | tf_op jit(solution)/shard_map/scan_forward/pallas_call | solution.py:959
  87.8 2.1 collective-permute-done.11.second_ref
  89.9 1.1 collective-permute-done.12.fourth_ref
  91.0 2.0 pair_sums.1
  93.1 2.1 branch_rows.1
  95.7 1.2 collective-permute-start.15
  97.0 22.5 %scan_backward.2 = (f32[256,1536]{1,0:T(8,128)}, f32[256,128]{1,0:T(8,128)S(1)}, f32[120,1536]{1,0:T(8,128)S(1)}) custom-call(s32[1]{0:T(128)} %bitcast.3.flip_ref, f32[512,128]{1,0:T(8,128)S(1)} %add.139.dbl_ref, bf16[96,1536]{1,0:T(8,128)(2,1)S(1)} %copy-done.12, f32[2,1536]{1,0:T(2,128)S(1)} %pad_maximum_fusion.2.vec_ref, f32[16,1536]{1,0:T(8,128)S(1)} %copy-done.8, ...), custom_call_target="tpu_custom_call" | custom-call | flops 22000001024 | bytes 20000000 | tf_op jit(solution)/shard_map/scan_backward/pallas_call | solution.py:993
  119.4 1.4 collective-permute-start.14
  125.0 4.0 %conv_backward.2 = (bf16[256,768]{1,0:T(8,128)(2,1)S(1)}, bf16[256,768]{1,0:T(8,128)(2,1)S(1)}, f32[136,1536]{1,0:T(8,128)S(1)}) custom-call(s32[1]{0:T(128)} %bitcast.3.flip_ref, bf16[512,1536]{1,0:T(8,128)(2,1)} %get-tuple-element.135.x_ref, bf16[512,1536]{1,0:T(8,128)(2,1)} %get-tuple-element.157.u_ref, f32[512,1536]{1,0:T(8,128)} %get-tuple-element.136.slope_ref, ...), custom_call_target="tpu_custom_call" | custom-call | flops 1000 | bytes 1000 | tf_op jit(solution)/shard_map/conv_backward/pallas_call | solution.py:716
  131.0 1.0 collective-permute-start.21
  132.0 2.6 %collective-permute-start.22 = (bf16[2,192,768]{2,1,0:T(8,128)(2,1)S(1)}, bf16[2,192,768]{2,1,0:T(8,128)(2,1)S(1)}, u32[]{:S(2)}, u32[]{:S(2)}) collective-permute-start(bf16[2,192,768]{2,1,0:T(8,128)(2,1)S(1)} %dynamic-slice_bitcast_fusion.1), channel_id=1, source_target_pairs={{0,16},{4,20},{8,24},{12,28},{16,0},{20,4},{24,8},{28,12},{1,17},{... | collective-permute-start | bytes 1769480 | tf_op jit(solution)/shard_map/ppermute | solution.py:21
  134.6 1.6 collective-permute-start.20
  136.2 22.2 %scan_backward.3 = (f32[256,1536]{1,0:T(8,128)}, f32[256,128]{1,0:T(8,128)S(1)}, f32[120,1536]{1,0:T(8,128)S(1)}) custom-call(s32[1]{0:T(128)} %bitcast.3.flip_ref, f32[512,128]{1,0:T(8,128)S(1)} %add.139.dbl_ref, bf16[96,1536]{1,0:T(8,128)(2,1)S(1)} %copy-done.12, f32[2,1536]{1,0:T(2,128)S(1)} %pad_maximum_fusion.2.vec_ref, f32[16,1536]{1,0:T(8,128)S(1)} %copy-done.8, ...), custom_call_target="tpu_custom_call" | custom-call | flops 22000001024 | bytes 20000000 | tf_op jit(solution)/shard_map/scan_backward/pallas_call | solution.py:993
  158.4 2.6 %collective-permute-done.22 = bf16[2,192,768]{2,1,0:T(8,128)(2,1)S(1)} collective-permute-done((bf16[2,192,768]{2,1,0:T(8,128)(2,1)S(1)}, bf16[2,192,768]{2,1,0:T(8,128)(2,1)S(1)}, u32[]{:S(2)}, u32[]{:S(2)}) %collective-permute-start.22) | collective-permute-done | bytes 589856 | tf_op jit(solution)/shard_map/ppermute | solution.py:21
  162.3 1.1 collective-permute-start.29
  164.0 2.0 collective-permute-done.19
  166.0 4.1 %conv_backward.3 = (bf16[256,768]{1,0:T(8,128)(2,1)S(1)}, bf16[256,768]{1,0:T(8,128)(2,1)S(1)}, f32[136,1536]{1,0:T(8,128)S(1)}) custom-call(s32[1]{0:T(128)} %bitcast.3.flip_ref, bf16[512,1536]{1,0:T(8,128)(2,1)} %get-tuple-element.135.x_ref, bf16[512,1536]{1,0:T(8,128)(2,1)} %get-tuple-element.157.u_ref, f32[512,1536]{1,0:T(8,128)} %get-tuple-element.136.slope_ref, ...), custom_call_target="tpu_custom_call" | custom-call | flops 1000 | bytes 1000 | tf_op jit(solution)/shard_map/conv_backward/pallas_call | solution.py:716
  170.8 1.4 collective-permute-start.27
  173.3 1.4 copy-done.21
  174.7 5.6 %proj_back.1 = (f32[256,1536]{1,0:T(8,128)S(1)}, bf16[256,1536]{1,0:T(8,128)(2,1)S(1)}) custom-call(s32[1]{0:T(128)} %bitcast.3.flip_ref, bf16[256,768]{1,0:T(8,128)(2,1)S(1)} %join_sums.2.refs_0_, bf16[256,768]{1,0:T(8,128)(2,1)S(1)} %join_sums.3.refs_1_, bf16[512,768]{1,0:T(8,128)(2,1)S(1)} %get-tuple-element.145.refs_2_, bf16[1536,1536]{1,0:T(8,128)(2,1)} %refs_3_.1, ...), custom_call_target="tpu_custom_call" | custom-call | flops 1000 | bytes 1000 | tf_op jit(solution)/shard_map/proj_back/pallas_call | solution.py:544
  182.2 4.2 %collective-permute-done.27 = bf16[128,1536]{1,0:T(8,128)(2,1)S(1)} collective-permute-done((bf16[128,1536]{1,0:T(8,128)(2,1)S(1)}, bf16[128,1536]{1,0:T(8,128)(2,1)S(1)}, u32[]{:S(2)}, u32[]{:S(2)}) %collective-permute-start.27) | collective-permute-done | bytes 393248 | tf_op jit(solution)/shard_map/ppermute | solution.py:21
  186.5 1.0 collective-permute-start.31
  187.7 1.3 collective-permute-start.30
  193.5 1.2 collective-permute-start.36
  195.0 3.5 %collective-permute-done.30.norm_far_ref = bf16[2,64,1536]{2,1,0:T(8,128)(2,1)S(1)} collective-permute-done((bf16[2,64,1536]{2,1,0:T(8,128)(2,1)S(1)}, bf16[2,64,1536]{2,1,0:T(8,128)(2,1)S(1)}, u32[]{:S(2)}, u32[]{:S(2)}) %collective-permute-start.30) | collective-permute-done | bytes 393248 | tf_op jit(solution)/shard_map/ppermute | solution.py:21
  198.5 2.9 %owned_rows.1 = (f32[2,64,1536]{2,1,0:T(8,128)}, f32[2,64,1536]{2,1,0:T(8,128)}, f32[2,3,1536]{2,1,0:T(4,128)S(1)}) custom-call(bf16[2,64,1536]{2,1,0:T(8,128)(2,1)S(1)} %copy-done.4, bf16[2,64,1536]{2,1,0:T(8,128)(2,1)} %cot_ref.1, f32[2,64,1]{2,1,0:T(8,128)S(1)} %copy.37.mask_ref, f32[2,3,1536]{2,1,0:T(4,128)S(1)} %reshape.94.mod_ref, ...), custom_call_target="tpu_custom_call" | custom-call | flops 1000 | bytes 1000 | tf_op jit(solution)/shard_map/owned_rows/pallas_call | solution.py:468
  201.5 1.1 collective-permute-start.33
  203.3 5.9 %collective-permute-done.36 = bf16[64,1536]{1,0:T(8,128)(2,1)} collective-permute-done((bf16[64,1536]{1,0:T(8,128)(2,1)S(1)}, bf16[64,1536]{1,0:T(8,128)(2,1)}, u32[]{:S(2)}, u32[]{:S(2)}) %collective-permute-start.36) | collective-permute-done | bytes 196640 | tf_op jit(solution)/shard_map/ppermute | solution.py:21
  211.5 1.2 convert_add_fusion
  214.5 3.5 %collective-permute-start.42 = (bf16[192,768]{1,0:T(8,128)(2,1)}, bf16[192,768]{1,0:T(8,128)(2,1)S(1)}, u32[]{:S(2)}, u32[]{:S(2)}) collective-permute-start(bf16[192,768]{1,0:T(8,128)(2,1)} %fusion.11), channel_id=1, source_target_pairs={{0,16},{4,20},{8,24},{12,28},{16,0},{20,4},{24,8},{28,12},{1,17},{... | collective-permute-start | bytes 884744 | tf_op jit(solution)/shard_map/ppermute | solution.py:21
  218.1 2.2 collective-permute-start.39
  220.7 2.0 collective-permute-start.41
  222.8 1.1 collective-permute-start.43
  223.9 8.8 %cond_rows.1 = f32[2,1536]{1,0:T(2,128)} custom-call(bf16[2,4608]{1,0:T(2,128)(2,1)S(1)} %bitcast.79, bf16[1536,4608]{1,0:T(8,128)(2,1)} %weight_ref.5, bf16[2,1536]{1,0:T(2,128)(2,1)S(1)} %copy-done.9), custom_call_target="tpu_custom_call" | custom-call | flops 1000 | bytes 1000 | tf_op jit(solution)/shard_map/cond_rows/pallas_call | solution.py:573
  235.8 1.3 fusion.12
  237.9 1.4 unpack_sums.1
  240.2 1.3 collective-permute-done.44
  241.5 1.1 maximum_select_fusion
  (185 shorter events, 36.5 us)
Async XLA Ops:
  0.6 12.4 %collective-permute-start = (bf16[2,64,1536]{2,1,0:T(8,128)(2,1)}, bf16[2,64,1536]{2,1,0:T(8,128)(2,1)S(1)}, u32[]{:S(2)}, u32[]{:S(2)}) collective-permute-start(bf16[2,64,1536]{2,1,0:T(8,128)(2,1)} %tokens_ref.1), channel_id=1, source_target_pairs={{0,2},{1,3},{2,0},{3,1},{4,6},{5,7},{6,4},{7,5},{8,10},{9,11},{10,... | collective-permute-start | bytes 1179656 | tf_op jit(solution)/shard_map/ppermute | solution.py:21
  3.7 10.8 %collective-permute-start.1 = (bf16[2,64,1536]{2,1,0:T(8,128)(2,1)}, bf16[2,64,1536]{2,1,0:T(8,128)(2,1)}, u32[]{:S(2)}, u32[]{:S(2)}) collective-permute-start(bf16[2,64,1536]{2,1,0:T(8,128)(2,1)} %tokens_ref.1), channel_id=1, source_target_pairs={{0,1},{1,0},{2,3},{3,2},{4,5},{5,4},{6,7},{7,6},{8,9},{9,8},{10,11... | collective-permute-start | bytes 1179656 | tf_op jit(solution)/shard_map/ppermute | solution.py:21
  13.0 1.9 collective-permute-start.2
  13.0 26.2 %collective-permute-start.8 = (bf16[768,1536]{1,0:T(8,128)(2,1)S(1)}, bf16[768,1536]{1,0:T(8,128)(2,1)}, u32[]{:S(2)}, u32[]{:S(2)}) collective-permute-start(bf16[768,1536]{1,0:T(8,128)(2,1)S(1)} %copy-done), channel_id=1, source_target_pairs={{0,1},{1,0},{2,3},{3,2},{4,5},{5,4},{6,7},{7,6},{8,9},{9,8},{10,11... | collective-permute-start | bytes 7077896 | tf_op jit(solution)/shard_map/ppermute | solution.py:21
  23.5 5.4 %collective-permute-start.3 = (bf16[512,1536]{1,0:T(8,128)(2,1)}, bf16[512,1536]{1,0:T(8,128)(2,1)}, u32[]{:S(2)}, u32[]{:S(2)}) collective-permute-start(bf16[512,1536]{1,0:T(8,128)(2,1)} %get-tuple-element.113.own_ref), channel_id=1, source_target_pairs={{0,1},{1,0},{2,3},{3,2},{4,5},{5,4},{6,7},{7,6},{8,9},{9,8},{10,11... | collective-permute-start | bytes 4718600 | tf_op jit(solution)/shard_map/ppermute | solution.py:21
  23.6 13.3 %collective-permute-start.5 = (bf16[2,64,1536]{2,1,0:T(8,128)(2,1)}, bf16[2,64,1536]{2,1,0:T(8,128)(2,1)}, u32[]{:S(2)}, u32[]{:S(2)}) collective-permute-start(bf16[2,64,1536]{2,1,0:T(8,128)(2,1)} %cot_ref.1), channel_id=1, source_target_pairs={{0,2},{1,3},{2,0},{3,1},{4,6},{5,7},{6,4},{7,5},{8,10},{9,11},{10,... | collective-permute-start | bytes 1179656 | tf_op jit(solution)/shard_map/ppermute | solution.py:21
  25.3 13.9 %collective-permute-start.6 = (bf16[2,64,1536]{2,1,0:T(8,128)(2,1)}, bf16[2,64,1536]{2,1,0:T(8,128)(2,1)}, u32[]{:S(2)}, u32[]{:S(2)}) collective-permute-start(bf16[2,64,1536]{2,1,0:T(8,128)(2,1)} %cot_ref.1), channel_id=1, source_target_pairs={{0,1},{1,0},{2,3},{3,2},{4,5},{5,4},{6,7},{7,6},{8,9},{9,8},{10,11... | collective-permute-start | bytes 1179656 | tf_op jit(solution)/shard_map/ppermute | solution.py:21
  36.3 11.5 %collective-permute-start.4 = (f32[512,128]{1,0:T(8,128)}, f32[512,128]{1,0:T(8,128)}, u32[]{:S(2)}, u32[]{:S(2)}) collective-permute-start(f32[512,128]{1,0:T(8,128)} %get-tuple-element.117), channel_id=1, source_target_pairs={{0,2},{1,3},{2,0},{3,1},{4,6},{5,7},{6,4},{7,5},{8,10},{9,11},{10,... | collective-permute-start | bytes 786440 | tf_op jit(solution)/shard_map/ppermute | solution.py:21
  36.9 2.3 collective-permute-start.7
  37.6 47.9 %collective-permute-start.9 = (bf16[512,768]{1,0:T(8,128)(2,1)}, bf16[512,768]{1,0:T(8,128)(2,1)S(1)}, u32[]{:S(2)}, u32[]{:S(2)}) collective-permute-start(bf16[512,768]{1,0:T(8,128)(2,1)} %copy-done.10), channel_id=1, source_target_pairs={{0,4},{4,0},{8,12},{12,8},{16,20},{20,16},{24,28},{28,24},{1,5},{5... | collective-permute-start | bytes 2359304 | tf_op jit(solution)/shard_map/ppermute | solution.py:21
  39.2 11.2 %copy-start.7 = (f32[16,1536]{1,0:T(8,128)S(1)}, f32[16,1536]{1,0:T(8,128)}, u32[]{:S(2)}) copy-start(f32[16,1536]{1,0:T(8,128)} %multiply_bitcast_fusion.rate2_ref) | copy-start | bytes 294916
  48.8 36.7 %collective-permute-start.10 = (bf16[512,768]{1,0:T(8,128)(2,1)S(1)}, bf16[512,768]{1,0:T(8,128)(2,1)S(1)}, u32[]{:S(2)}, u32[]{:S(2)}) collective-permute-start(bf16[512,768]{1,0:T(8,128)(2,1)S(1)} %get-tuple-element.128), channel_id=1, source_target_pairs={{0,8},{4,12},{8,0},{12,4},{16,24},{20,28},{24,16},{28,20},{1,9},{5... | collective-permute-start | bytes 2359304 | tf_op jit(solution)/shard_map/ppermute | solution.py:21
  87.3 2.6 %collective-permute-start.11 = (bf16[512,768]{1,0:T(8,128)(2,1)}, bf16[512,768]{1,0:T(8,128)(2,1)}, u32[]{:S(2)}, u32[]{:S(2)}) collective-permute-start(bf16[512,768]{1,0:T(8,128)(2,1)} %get-tuple-element.129), channel_id=1, source_target_pairs={{0,1},{1,0},{2,3},{3,2},{4,5},{5,4},{6,7},{7,6},{8,9},{9,8},{10,11... | collective-permute-start | bytes 2359304 | tf_op jit(solution)/shard_map/ppermute | solution.py:21
  87.3 3.7 %collective-permute-start.12 = (bf16[512,768]{1,0:T(8,128)(2,1)}, bf16[512,768]{1,0:T(8,128)(2,1)}, u32[]{:S(2)}, u32[]{:S(2)}) collective-permute-start(bf16[512,768]{1,0:T(8,128)(2,1)} %get-tuple-element.131), channel_id=1, source_target_pairs={{0,1},{1,0},{2,3},{3,2},{4,5},{5,4},{6,7},{7,6},{8,9},{9,8},{10,11... | collective-permute-start | bytes 2359304 | tf_op jit(solution)/shard_map/ppermute | solution.py:21
  95.2 25.7 %collective-permute-start.16 = (bf16[512,768]{1,0:T(8,128)(2,1)S(1)}, bf16[512,768]{1,0:T(8,128)(2,1)S(1)}, u32[]{:S(2)}, u32[]{:S(2)}) collective-permute-start(bf16[512,768]{1,0:T(8,128)(2,1)S(1)} %get-tuple-element.148.values_ref), channel_id=1, source_target_pairs={{0,8},{4,12},{8,0},{12,4},{16,24},{20,28},{24,16},{28,20},{1,9},{5... | collective-permute-start | bytes 2359304 | tf_op jit(solution)/shard_map/ppermute | solution.py:21
  95.7 25.2 %collective-permute-start.15 = (bf16[512,768]{1,0:T(8,128)(2,1)S(1)}, bf16[512,768]{1,0:T(8,128)(2,1)S(1)}, u32[]{:S(2)}, u32[]{:S(2)}) collective-permute-start(bf16[512,768]{1,0:T(8,128)(2,1)S(1)} %get-tuple-element.145.refs_2_), channel_id=1, source_target_pairs={{0,4},{4,0},{8,12},{12,8},{16,20},{20,16},{24,28},{28,24},{1,5},{5... | collective-permute-start | bytes 2359304 | tf_op jit(solution)/shard_map/ppermute | solution.py:21
  97.0 23.9 %copy-start.16 = (bf16[512,768]{1,0:T(8,128)(2,1)S(1)}, bf16[512,768]{1,0:T(8,128)(2,1)}, u32[]{:S(2)}) copy-start(bf16[512,768]{1,0:T(8,128)(2,1)} %copy-done.15) | copy-start | bytes 2359300
  119.4 5.5 %collective-permute-start.14 = (f32[256,128]{1,0:T(8,128)S(1)}, f32[256,128]{1,0:T(8,128)S(1)}, u32[]{:S(2)}, u32[]{:S(2)}) collective-permute-start(f32[256,128]{1,0:T(8,128)S(1)} %get-tuple-element.144), channel_id=1, source_target_pairs={{0,2},{1,3},{2,0},{3,1},{4,6},{5,7},{6,4},{7,5},{8,10},{9,11},{10,... | collective-permute-start | bytes 393224 | tf_op jit(solution)/shard_map/ppermute | solution.py:21
  120.8 8.9 %collective-permute-start.13 = (bf16[256,1536]{1,0:T(8,128)(2,1)S(1)}, bf16[256,1536]{1,0:T(8,128)(2,1)S(1)}, u32[]{:S(2)}, u32[]{:S(2)}) collective-permute-start(bf16[256,1536]{1,0:T(8,128)(2,1)S(1)} %get-tuple-element.134), channel_id=1, source_target_pairs={{0,1},{1,0},{2,3},{3,2},{4,5},{5,4},{6,7},{7,6},{8,9},{9,8},{10,11... | collective-permute-start | bytes 2359304 | tf_op jit(solution)/shard_map/ppermute | solution.py:21
  129.0 1.9 collective-permute-start.18
  129.7 43.6 %collective-permute-start.24 = (bf16[1536,768]{1,0:T(8,128)(2,1)S(1)}, bf16[1536,768]{1,0:T(8,128)(2,1)S(1)}, u32[]{:S(2)}, u32[]{:S(2)}) collective-permute-start(bf16[1536,768]{1,0:T(8,128)(2,1)S(1)} %copy-done.19), channel_id=1, source_target_pairs={{0,1},{1,0},{2,3},{3,2},{4,5},{5,4},{6,7},{7,6},{8,9},{9,8},{10,11... | collective-permute-start | bytes 7077896 | tf_op jit(solution)/shard_map/ppermute | solution.py:21
  129.9 32.0 %collective-permute-start.17 = (bf16[2,64,1536]{2,1,0:T(8,128)(2,1)S(1)}, bf16[2,64,1536]{2,1,0:T(8,128)(2,1)S(1)}, u32[]{:S(2)}, u32[]{:S(2)}) collective-permute-start(bf16[2,64,1536]{2,1,0:T(8,128)(2,1)S(1)} %get-tuple-element.154), channel_id=1, source_target_pairs={{0,2},{1,3},{2,0},{3,1},{4,6},{5,7},{6,4},{7,5},{8,10},{9,11},{10,... | collective-permute-start | bytes 1179656 | tf_op jit(solution)/shard_map/ppermute | solution.py:21
  131.0 30.9 %collective-permute-start.21 = (bf16[256,768]{1,0:T(8,128)(2,1)S(1)}, bf16[256,768]{1,0:T(8,128)(2,1)S(1)}, u32[]{:S(2)}, u32[]{:S(2)}) collective-permute-start(bf16[256,768]{1,0:T(8,128)(2,1)S(1)} %join_sums.2.refs_0_), channel_id=1, source_target_pairs={{0,4},{4,0},{8,12},{12,8},{16,20},{20,16},{24,28},{28,24},{1,5},{5... | collective-permute-start | bytes 1179656 | tf_op jit(solution)/shard_map/ppermute | solution.py:21
  132.0 29.0 %collective-permute-start.22 = (bf16[2,192,768]{2,1,0:T(8,128)(2,1)S(1)}, bf16[2,192,768]{2,1,0:T(8,128)(2,1)S(1)}, u32[]{:S(2)}, u32[]{:S(2)}) collective-permute-start(bf16[2,192,768]{2,1,0:T(8,128)(2,1)S(1)} %dynamic-slice_bitcast_fusion.1), channel_id=1, source_target_pairs={{0,16},{4,20},{8,24},{12,28},{16,0},{20,4},{24,8},{28,12},{1,17},{... | collective-permute-start | bytes 1769480 | tf_op jit(solution)/shard_map/ppermute | solution.py:21
  134.6 27.3 %collective-permute-start.20 = (bf16[2,192,768]{2,1,0:T(8,128)(2,1)S(1)}, bf16[2,192,768]{2,1,0:T(8,128)(2,1)S(1)}, u32[]{:S(2)}, u32[]{:S(2)}) collective-permute-start(bf16[2,192,768]{2,1,0:T(8,128)(2,1)S(1)} %dynamic-slice_bitcast_fusion.2), channel_id=1, source_target_pairs={{0,8},{4,12},{8,0},{12,4},{16,24},{20,28},{24,16},{28,20},{1,9},{5... | collective-permute-start | bytes 1769480 | tf_op jit(solution)/shard_map/ppermute | solution.py:21
  161.0 5.0 %collective-permute-start.19 = (f32[256,128]{1,0:T(8,128)S(1)}, f32[256,128]{1,0:T(8,128)S(1)}, u32[]{:S(2)}, u32[]{:S(2)}) collective-permute-start(f32[256,128]{1,0:T(8,128)S(1)} %get-tuple-element.160), channel_id=1, source_target_pairs={{0,2},{1,3},{2,0},{3,1},{4,6},{5,7},{6,4},{7,5},{8,10},{9,11},{10,... | collective-permute-start | bytes 393224 | tf_op jit(solution)/shard_map/ppermute | solution.py:21
  162.3 18.2 %collective-permute-start.29 = (bf16[192,768]{1,0:T(8,128)(2,1)S(1)}, bf16[192,768]{1,0:T(8,128)(2,1)S(1)}, u32[]{:S(2)}, u32[]{:S(2)}) collective-permute-start(bf16[192,768]{1,0:T(8,128)(2,1)S(1)} %get-tuple-element.216), channel_id=1, source_target_pairs={{0,4},{4,0},{8,12},{12,8},{16,20},{20,16},{24,28},{28,24},{1,5},{5... | collective-permute-start | bytes 884744 | tf_op jit(solution)/shard_map/ppermute | solution.py:21
  163.4 17.1 %collective-permute-start.28 = (bf16[192,768]{1,0:T(8,128)(2,1)S(1)}, bf16[192,768]{1,0:T(8,128)(2,1)S(1)}, u32[]{:S(2)}, u32[]{:S(2)}) collective-permute-start(bf16[192,768]{1,0:T(8,128)(2,1)S(1)} %get-tuple-element.215), channel_id=1, source_target_pairs={{0,16},{4,20},{8,24},{12,28},{16,0},{20,4},{24,8},{28,12},{1,17},{... | collective-permute-start | bytes 884744 | tf_op jit(solution)/shard_map/ppermute | solution.py:21
  170.3 2.0 collective-permute-start.23
  170.8 15.6 %collective-permute-start.27 = (bf16[128,1536]{1,0:T(8,128)(2,1)S(1)}, bf16[128,1536]{1,0:T(8,128)(2,1)S(1)}, u32[]{:S(2)}, u32[]{:S(2)}) collective-permute-start(bf16[128,1536]{1,0:T(8,128)(2,1)S(1)} %get-tuple-element.171), channel_id=1, source_target_pairs={{0,8},{4,12},{8,0},{12,4},{16,24},{20,28},{24,16},{28,20},{1,9},{5... | collective-permute-start | bytes 1179656 | tf_op jit(solution)/shard_map/ppermute | solution.py:21
  172.3 15.2 %collective-permute-start.26 = (bf16[256,768]{1,0:T(8,128)(2,1)S(1)}, bf16[256,768]{1,0:T(8,128)(2,1)S(1)}, u32[]{:S(2)}, u32[]{:S(2)}) collective-permute-start(bf16[256,768]{1,0:T(8,128)(2,1)S(1)} %join_sums.3.refs_1_), channel_id=1, source_target_pairs={{0,4},{4,0},{8,12},{12,8},{16,20},{20,16},{24,28},{28,24},{1,5},{5... | collective-permute-start | bytes 1179656 | tf_op jit(solution)/shard_map/ppermute | solution.py:21
  180.4 7.2 %collective-permute-start.25 = (bf16[256,1536]{1,0:T(8,128)(2,1)S(1)}, bf16[256,1536]{1,0:T(8,128)(2,1)S(1)}, u32[]{:S(2)}, u32[]{:S(2)}) collective-permute-start(bf16[256,1536]{1,0:T(8,128)(2,1)S(1)} %get-tuple-element.174), channel_id=1, source_target_pairs={{0,1},{1,0},{2,3},{3,2},{4,5},{5,4},{6,7},{7,6},{8,9},{9,8},{10,11... | collective-permute-start | bytes 2359304 | tf_op jit(solution)/shard_map/ppermute | solution.py:21
  186.5 6.9 %collective-permute-start.31 = (bf16[64,1536]{1,0:T(8,128)(2,1)S(1)}, bf16[64,1536]{1,0:T(8,128)(2,1)S(1)}, u32[]{:S(2)}, u32[]{:S(2)}) collective-permute-start(bf16[64,1536]{1,0:T(8,128)(2,1)S(1)} %dynamic-slice_convert_fusion.3), channel_id=1, source_target_pairs={{0,4},{4,0},{8,12},{12,8},{16,20},{20,16},{24,28},{28,24},{1,5},{5... | collective-permute-start | bytes 589832 | tf_op jit(solution)/shard_map/ppermute | solution.py:21
  187.7 10.8 %collective-permute-start.30 = (bf16[2,64,1536]{2,1,0:T(8,128)(2,1)S(1)}, bf16[2,64,1536]{2,1,0:T(8,128)(2,1)S(1)}, u32[]{:S(2)}, u32[]{:S(2)}) collective-permute-start(bf16[2,64,1536]{2,1,0:T(8,128)(2,1)S(1)} %get-tuple-element.182), channel_id=1, source_target_pairs={{0,2},{1,3},{2,0},{3,1},{4,6},{5,7},{6,4},{7,5},{8,10},{9,11},{10,... | collective-permute-start | bytes 1179656 | tf_op jit(solution)/shard_map/ppermute | solution.py:21
  192.4 19.1 %collective-permute-start.35 = (bf16[2,192,768]{2,1,0:T(8,128)(2,1)}, bf16[2,192,768]{2,1,0:T(8,128)(2,1)}, u32[]{:S(2)}, u32[]{:S(2)}) collective-permute-start(bf16[2,192,768]{2,1,0:T(8,128)(2,1)} %dynamic-slice_bitcast_fusion), channel_id=1, source_target_pairs={{0,8},{4,12},{8,0},{12,4},{16,24},{20,28},{24,16},{28,20},{1,9},{5... | collective-permute-start | bytes 1769480 | tf_op jit(solution)/shard_map/ppermute | solution.py:21
  193.5 15.8 %collective-permute-start.36 = (bf16[64,1536]{1,0:T(8,128)(2,1)S(1)}, bf16[64,1536]{1,0:T(8,128)(2,1)}, u32[]{:S(2)}, u32[]{:S(2)}) collective-permute-start(bf16[64,1536]{1,0:T(8,128)(2,1)S(1)} %add_convert_fusion.4), channel_id=1, source_target_pairs={{0,16},{4,20},{8,24},{12,28},{16,0},{20,4},{24,8},{28,12},{1,17},{... | collective-permute-start | bytes 589832 | tf_op jit(solution)/shard_map/ppermute | solution.py:21
  198.5 13.0 %copy-start.18 = (bf16[768,768]{1,0:T(8,128)(2,1)S(1)}, bf16[768,768]{1,0:T(8,128)(2,1)}, u32[]{:S(2)}) copy-start(bf16[768,768]{1,0:T(8,128)(2,1)} %copy-done.17) | copy-start | bytes 3538948
  201.5 12.0 %collective-permute-start.32 = (f32[2,3,1536]{2,1,0:T(4,128)S(1)}, f32[2,3,1536]{2,1,0:T(4,128)S(1)}, u32[]{:S(2)}, u32[]{:S(2)}) collective-permute-start(f32[2,3,1536]{2,1,0:T(4,128)S(1)} %get-tuple-element.191), channel_id=1, source_target_pairs={{0,1},{1,0},{2,3},{3,2},{4,5},{5,4},{6,7},{7,6},{8,9},{9,8},{10,11... | collective-permute-start | bytes 110600 | tf_op jit(solution)/shard_map/ppermute | solution.py:1208
  201.5 12.0 %collective-permute-start.33 = (f32[2,3,1536]{2,1,0:T(4,128)S(1)}, f32[2,3,1536]{2,1,0:T(4,128)S(1)}, u32[]{:S(2)}, u32[]{:S(2)}) collective-permute-start(f32[2,3,1536]{2,1,0:T(4,128)S(1)} %get-tuple-element.191), channel_id=1, source_target_pairs={{0,2},{1,3},{2,0},{3,1},{4,6},{5,7},{6,4},{7,5},{8,10},{9,11},{10,... | collective-permute-start | bytes 110600 | tf_op jit(solution)/shard_map/ppermute | solution.py:1208
  202.5 11.0 %collective-permute-start.34 = (f32[2,3,1536]{2,1,0:T(4,128)S(1)}, f32[2,3,1536]{2,1,0:T(4,128)S(1)}, u32[]{:S(2)}, u32[]{:S(2)}) collective-permute-start(f32[2,3,1536]{2,1,0:T(4,128)S(1)} %get-tuple-element.191), channel_id=1, source_target_pairs={{0,3},{1,2},{2,1},{3,0},{4,7},{5,6},{6,5},{7,4},{8,11},{9,10},{10,... | collective-permute-start | bytes 110600 | tf_op jit(solution)/shard_map/ppermute | solution.py:1208
  210.2 12.5 %collective-permute-start.38 = (bf16[64,1536]{1,0:T(8,128)(2,1)S(1)}, bf16[64,1536]{1,0:T(8,128)(2,1)S(1)}, u32[]{:S(2)}, u32[]{:S(2)}) collective-permute-start(bf16[64,1536]{1,0:T(8,128)(2,1)S(1)} %add_convert_fusion.3), channel_id=1, source_target_pairs={{0,4},{4,0},{8,12},{12,8},{16,20},{20,16},{24,28},{28,24},{1,5},{5... | collective-permute-start | bytes 589832 | tf_op jit(solution)/shard_map/ppermute | solution.py:21
  213.6 4.4 %collective-permute-start.37 = (bf16[2,6144]{1,0:T(2,128)(2,1)S(1)}, bf16[2,6144]{1,0:T(2,128)(2,1)S(1)}, u32[]{:S(2)}, u32[]{:S(2)}) collective-permute-start(bf16[2,6144]{1,0:T(2,128)(2,1)S(1)} %pad_maximum_fusion.1), channel_id=1, source_target_pairs={{0,4},{4,0},{8,12},{12,8},{16,20},{20,16},{24,28},{28,24},{1,5},{5... | collective-permute-start | bytes 73736 | tf_op jit(solution)/shard_map/ppermute | solution.py:21
  214.5 24.8 %collective-permute-start.42 = (bf16[192,768]{1,0:T(8,128)(2,1)}, bf16[192,768]{1,0:T(8,128)(2,1)S(1)}, u32[]{:S(2)}, u32[]{:S(2)}) collective-permute-start(bf16[192,768]{1,0:T(8,128)(2,1)} %fusion.11), channel_id=1, source_target_pairs={{0,16},{4,20},{8,24},{12,28},{16,0},{20,4},{24,8},{28,12},{1,17},{... | collective-permute-start | bytes 884744 | tf_op jit(solution)/shard_map/ppermute | solution.py:21
  218.1 14.7 %collective-permute-start.39 = (bf16[2,2,6144]{2,1,0:T(2,128)(2,1)S(1)}, bf16[2,2,6144]{2,1,0:T(2,128)(2,1)S(1)}, u32[]{:S(2)}, u32[]{:S(2)}) collective-permute-start(bf16[2,2,6144]{2,1,0:T(2,128)(2,1)S(1)} %broadcast_select_fusion.1), channel_id=1, source_target_pairs={{0,8},{4,12},{8,0},{12,4},{16,24},{20,28},{24,16},{28,20},{1,9},{5... | collective-permute-start | bytes 147464 | tf_op jit(solution)/shard_map/ppermute | solution.py:132
  220.3 13.4 %collective-permute-start.40 = (bf16[2,2,6144]{2,1,0:T(2,128)(2,1)S(1)}, bf16[2,2,6144]{2,1,0:T(2,128)(2,1)S(1)}, u32[]{:S(2)}, u32[]{:S(2)}) collective-permute-start(bf16[2,2,6144]{2,1,0:T(2,128)(2,1)S(1)} %broadcast_select_fusion.1), channel_id=1, source_target_pairs={{0,16},{4,20},{8,24},{12,28},{16,0},{20,4},{24,8},{28,12},{1,17},{... | collective-permute-start | bytes 147464 | tf_op jit(solution)/shard_map/ppermute | solution.py:132
  220.7 12.9 %collective-permute-start.41 = (bf16[2,2,6144]{2,1,0:T(2,128)(2,1)S(1)}, bf16[2,2,6144]{2,1,0:T(2,128)(2,1)S(1)}, u32[]{:S(2)}, u32[]{:S(2)}) collective-permute-start(bf16[2,2,6144]{2,1,0:T(2,128)(2,1)S(1)} %broadcast_select_fusion.1), channel_id=1, source_target_pairs={{0,24},{4,28},{8,16},{12,20},{16,8},{20,12},{24,0},{28,4},{1,25},{... | collective-permute-start | bytes 147464 | tf_op jit(solution)/shard_map/ppermute | solution.py:132
  222.8 15.1 %collective-permute-start.43 = (bf16[128,1536]{1,0:T(8,128)(2,1)S(1)}, bf16[128,1536]{1,0:T(8,128)(2,1)S(1)}, u32[]{:S(2)}, u32[]{:S(2)}) collective-permute-start(bf16[128,1536]{1,0:T(8,128)(2,1)S(1)} %maximum_select_fusion.1.keep_ref), channel_id=1, source_target_pairs={{0,8},{4,12},{8,0},{12,4},{16,24},{20,28},{24,16},{28,20},{1,9},{5... | collective-permute-start | bytes 1179656 | tf_op jit(solution)/shard_map/ppermute | solution.py:21
  239.5 2.1 collective-permute-start.44
  (28 other events, 134.6 us)
